TPU v7x, 256 devices: a whole 4x4x8 slice. The times are simulated.
256 devices in a mesh: expert: 64 (over z_hi, y, x, core), loop: 4 (over z_lo).
Axes of the slice: x: 4, y: 4, z: 8 (z_hi: 2, z_lo: 4; z = z_hi * 4 + z_lo), core: 2. Of those that a mesh axis runs over, the one named last changes fastest.
Arguments:
- tokens: bfloat16 [65536, 1280], P(('expert', 'loop')), may hold values from -6 to 6
- routes: int32 [65536, 1], P(('expert', 'loop')), may hold values from 0 to 63; in each aligned block of 256 rows (0 to 255, 256 to 511, ...) at most 6 rows name the same one
- gate_prob: float32 [65536], P(('expert', 'loop')), may hold values from 0.2 to 1
- expert_quota: int32 [64], replicated, may hold values from 1 to 6, as said below
- w_in: bfloat16 [64, 1280, 5120], P('expert', None, 'loop'), may hold values from -0.15625 to 0.15625
- w_out: bfloat16 [64, 1280, 5120], P('expert', None, 'loop'), may hold values from -0.078125 to 0.078125
- other_pooled: bfloat16 [32512, 1280], P(('expert', 'loop')), may hold values from -6 to 6
- head: bfloat16 [1280, 1024], replicated, may hold values from -0.15625 to 0.15625
- text_embed: bfloat16 [32768, 1024], P(('expert', 'loop')), may hold values from -6 to 6
- labels: int32 [32768], P(('expert', 'loop')), may hold values from 0 to 3
Outputs:
- layer_out: bfloat16 [65536, 1280], P(('expert', 'loop'))
- loss_rows: float32 [32768], P(('expert', 'loop'))
- image_grad: float32 [32768, 1024], P(('expert', 'loop'))
- text_grad: float32 [32768, 1024], P(('expert', 'loop'))
Inputs may be any that keep to these rules, and one draw needn't show every extreme that they name: `routes`: in the 256 rows of one device no expert is named by more than 6 rows. `expert_quota`: some expert has a quota of exactly 6.
All inputs are finite; a program needn't handle non-finite values.
Results may differ from a plain program's by a relative error of at most 0.0065.
Values may be sent and summed in bfloat16 or wider, within the bound.
No kernel may reach another device: no remote copies, remote signals or barrier semaphores. Data moves between devices by JAX's collectives and lax.ppermute only.
A program may use at most 128 MiB of HBM per device.

v0:
```python
import jax
import jax.numpy as jnp
from jax import lax
from jax.sharding import PartitionSpec as P

PATCHES = 256


scale_logit = 4.0
shift_logit = -1.0


def normalize_rows(values):
    return values / jnp.sqrt(jnp.sum(values * values, axis=1, keepdims=True) + 1e-06)


def shards(
    tokens, routes, gate_prob, expert_quota, w_in, w_out, other_pooled, head, text_embed, labels
):
    experts = lax.axis_size("expert")
    tok_rows = tokens.shape[0]
    width = tokens.shape[1]
    slots = max(2, 3 * tok_rows // (2 * experts))
    expert_ids = routes[:, 0]
    onehot = (expert_ids[:, None] == jnp.arange(experts, dtype=jnp.int32)[None, :]).astype(
        jnp.int32
    )
    slot = jnp.sum((jnp.cumsum(onehot, axis=0) - 1) * onehot, axis=1)
    quota_tok = jnp.sum(onehot * expert_quota[None, :], axis=1)
    position = jnp.where(slot < quota_tok, expert_ids * slots + slot, -1)
    placing = (position[:, None] == jnp.arange(experts * slots, dtype=jnp.int32)[None, :]).astype(
        jnp.bfloat16
    )
    outgoing = lax.dot_general(
        placing, tokens, (((0,), (0,)), ((), ())), preferred_element_type=jnp.float32
    )
    outgoing = outgoing.astype(jnp.bfloat16).reshape(experts, slots, width)
    received = lax.all_to_all(outgoing, "expert", split_axis=0, concat_axis=0, tiled=True).reshape(
        experts * slots, width
    )
    first_local = w_in[0]
    second_local = w_out[0]
    hidden = jax.nn.gelu(
        jnp.dot(
            lax.all_gather(received, "loop", axis=0, tiled=True),
            first_local,
            preferred_element_type=jnp.float32,
        )
    ).astype(jnp.bfloat16)
    term = lax.dot_general(
        hidden, second_local, (((1,), (1,)), ((), ())), preferred_element_type=jnp.float32
    )
    term = lax.optimization_barrier(term.astype(jnp.bfloat16))
    result = lax.psum_scatter(
        term.astype(jnp.float32).astype(jnp.bfloat16), "loop", scatter_dimension=0, tiled=True
    )
    going_back = result.reshape(experts, slots, width)
    returned = lax.all_to_all(
        going_back, "expert", split_axis=0, concat_axis=0, tiled=True
    ).reshape(experts * slots, width)
    contrib = jnp.dot(placing, returned, preferred_element_type=jnp.float32)
    layer = tokens.astype(jnp.float32) + gate_prob[:, None] * contrib
    layer_out = layer.astype(jnp.bfloat16)
    own = jnp.mean(layer.reshape(-1, PATCHES, width), axis=1).astype(jnp.bfloat16)
    pooled = jnp.concatenate([own, other_pooled], axis=0)
    projected = jnp.dot(pooled, head, preferred_element_type=jnp.float32)
    image = normalize_rows(projected).astype(jnp.bfloat16)
    text = normalize_rows(text_embed.astype(jnp.float32)).astype(jnp.bfloat16)
    label_values = labels.astype(jnp.bfloat16)
    their_image = lax.all_gather(image, "loop", axis=0, tiled=True)
    their_text = lax.all_gather(text, "loop", axis=0, tiled=True)
    their_label = lax.all_gather(label_values, "loop", axis=0, tiled=True)
    logit_mine = (
        scale_logit
        * lax.dot_general(
            image, their_text, (((1,), (1,)), ((), ())), preferred_element_type=jnp.float32
        )
        + shift_logit
    )
    sign_mine = jnp.where(label_values[:, None] == their_label[None, :], 1.0, -1.0).astype(
        jnp.float32
    )
    loss_acc = jnp.sum(jax.nn.softplus(-sign_mine * logit_mine), axis=1)
    coef_mine = (-scale_logit * sign_mine * jax.nn.sigmoid(-sign_mine * logit_mine)).astype(
        jnp.bfloat16
    )
    image_acc = jnp.dot(coef_mine, their_text, preferred_element_type=jnp.float32)
    logit_their = (
        scale_logit
        * lax.dot_general(
            their_image, text, (((1,), (1,)), ((), ())), preferred_element_type=jnp.float32
        )
        + shift_logit
    )
    sign_their = jnp.where(their_label[:, None] == label_values[None, :], 1.0, -1.0).astype(
        jnp.float32
    )
    coef_their = (-scale_logit * sign_their * jax.nn.sigmoid(-sign_their * logit_their)).astype(
        jnp.bfloat16
    )
    text_acc = lax.dot_general(
        coef_their, their_image, (((0,), (0,)), ((), ())), preferred_element_type=jnp.float32
    )
    return (layer_out, loss_acc, image_acc, text_acc)


def solution(mesh):
    in_specs = (
        P(("expert", "loop"), None),
        P(("expert", "loop"), None),
        P(("expert", "loop")),
        P(),
        P("expert", None, "loop"),
        P("expert", None, "loop"),
        P(("expert", "loop"), None),
        P(),
        P(("expert", "loop"), None),
        P(("expert", "loop")),
    )
    out_specs = (
        P(("expert", "loop"), None),
        P(("expert", "loop")),
        P(("expert", "loop"), None),
        P(("expert", "loop"), None),
    )
    return jax.shard_map(shards, mesh=mesh, in_specs=in_specs, out_specs=out_specs, check_vma=False)
```

profile of v0, /device:TPU:2, one launch (start us, length us, event | category | flops | bytes accessed | tf_op | source)
XLA Modules:
  0.0 352.0 jit_solution(16635129478390138676)
XLA Ops:
  7.2 0.0 copy-start
  7.2 0.0 all-gather.5.cloned.1.call-start
  7.2 0.8 fusion.54
  8.1 0.6 reduce-window.6
  8.7 0.2 slice_reduce_fusion
  8.9 0.8 select_reduce_fusion
  9.7 0.7 compare_select_fusion.1
  10.4 2.6 convolution_convert_fusion.1
  13.0 2.3 reshape.85
  15.3 41.5 %all_to_all.10 = bf16[64,6,1280]{2,1,0:T(8,128)(2,1)} all-to-all(bf16[64,6,1280]{2,1,0:T(8,128)(2,1)} %reshape.85), channel_id=1, replica_groups=mesh['expert'=64,'loop'=4] {'expert'}, dimensions={0} | all-to-all | bytes 1966080 | tf_op jit(solution)/shard_map/all_to_all | solution.py:38
  56.8 2.2 reshape.86
  59.0 0.0 all-gather.5.cloned.1.call-update
  59.0 0.0 reduce-scatter.2.cloned.1.call-start
  59.1 84.8 %all-gather.5.cloned.1.call-done = bf16[1536,1280]{1,0:T(8,128)(2,1)} async-done(((bf16[384,1280]{1,0:T(8,128)(2,1)}), bf16[1536,1280]{1,0:T(8,128)(2,1)}) %all-gather.5.cloned.1.call-update) | async-done | bytes 3932176 | tf_op jit(solution)/shard_map/all_gather | solution.py:45
  143.9 0.0 copy-done
  143.9 0.0 copy-start.3
  143.9 7.6 %fusion.14 = f32[1536,1280]{1,0:T(8,128)S(1)} fusion(bf16[1536,1280]{1,0:T(8,128)(2,1)} %all-gather.5.cloned.1.call-done, bf16[1,1280,1280]{2,1,0:T(8,128)(2,1)S(1)} %copy-done), kind=kOutput, calls=%fused_computation.15 | convolution fusion | flops 5033164800 | bytes 15073280 | tf_op jit(solution)/shard_map/dot_general | solution.py:44
  151.5 0.0 copy-done.3
  151.5 8.2 %convolution_convert_fusion = bf16[1536,1280]{1,0:T(8,128)(2,1)} fusion(f32[1536,1280]{1,0:T(8,128)S(1)} %fusion.14, bf16[1,1280,1280]{2,1,0:T(8,128)(2,1)S(1)} %copy-done.3), kind=kOutput, calls=%fused_computation.9 | convolution fusion | flops 5052825600 | bytes 15073280 | tf_op jit(solution)/shard_map/dot_general | solution.py:50
  159.8 0.0 copy-start.1
  159.8 0.0 reduce-scatter.2.cloned.1.call-update
  159.8 0.0 copy-start.4
  159.8 78.2 %reduce-scatter.2.cloned.1.call-done = bf16[384,1280]{1,0:T(8,128)(2,1)} async-done(((bf16[1536,1280]{1,0:T(8,128)(2,1)}), bf16[384,1280]{1,0:T(8,128)(2,1)}) %reduce-scatter.2.cloned.1.call-update) | async-done | bytes 983056 | tf_op jit(solution)/shard_map/reduce_scatter | solution.py:54
  237.9 2.3 reshape.87
  240.2 12.1 %all-to-all-start.1 = ((bf16[64,6,1280]{2,1,0:T(8,128)(2,1)}), bf16[64,6,1280]{2,1,0:T(8,128)(2,1)}, u32[]{:S(2)}, u32[]{:S(2)}) async-start(bf16[64,6,1280]{2,1,0:T(8,128)(2,1)} %reshape.87), calls=%async_computation.2 | async-start | bytes 2621440 | tf_op jit(solution)/shard_map/all_to_all | solution.py:58
  252.4 0.0 all-gather.7.cloned.1.call-start
  252.4 0.0 copy-done.1
  252.4 0.1 fusion.28
  252.6 0.8 fusion.29
  253.4 0.0 all-gather.7.cloned.1.call-update
  253.4 0.2 all-gather.9.cloned.1.call-start
  253.7 27.0 %all-to-all-done.1 = bf16[64,6,1280]{2,1,0:T(8,128)(2,1)} async-done(((bf16[64,6,1280]{2,1,0:T(8,128)(2,1)}), bf16[64,6,1280]{2,1,0:T(8,128)(2,1)}, u32[]{:S(2)}, u32[]{:S(2)}) %all-to-all-start.1) | async-done | bytes 983072 | tf_op jit(solution)/shard_map/all_to_all | solution.py:58
  280.6 2.2 reshape.88
  282.9 0.0 copy-done.4
  282.9 0.0 copy-start.5
  282.9 2.8 fusion.67
  285.7 0.0 copy-start.2
  285.7 2.5 multiply_reduce_fusion
  288.2 0.8 divide_convert_fusion
  289.0 0.0 all-gather.9.cloned.1.call-update
  289.1 0.0 copy-done.5
  289.1 31.4 %all-gather = bf16[4,1,128]{2,1,0:T(2,128)(2,1)S(1)} all-gather(bf16[1,1,128]{2,1,0:T(2,128)(2,1)S(1)} %get-tuple-element.9), channel_id=1, replica_groups=mesh['expert'=64,'loop'=4] {'loop'}, dimensions={0}, use_global_device_ids=true | all-gather | bytes 1280 | tf_op jit(solution)/shard_map/all_gather | solution.py:72
  320.5 0.0 all-gather.7.cloned.1.call-done
  320.5 2.6 fusion.36
  323.1 2.4 fusion.39
  325.5 16.7 %all-gather.9.cloned.1.call-done = bf16[512,1024]{1,0:T(8,128)(2,1)} async-done(((bf16[128,1024]{1,0:T(8,128)(2,1)}), bf16[512,1024]{1,0:T(8,128)(2,1)}) %all-gather.9.cloned.1.call-update) | async-done | bytes 1048592 | tf_op jit(solution)/shard_map/all_gather | solution.py:70
  342.2 0.0 copy-done.2
  342.2 3.3 fusion.27
  (8 shorter events, 0.1 us)
Async XLA Ops:
  7.2 136.7 %copy-start = (bf16[1,1280,1280]{2,1,0:T(8,128)(2,1)S(1)}, bf16[1,1280,1280]{2,1,0:T(8,128)(2,1)}, u32[]{:S(2)}) copy-start(bf16[1,1280,1280]{2,1,0:T(8,128)(2,1)} %param.14) | copy-start | bytes 9830404
  7.2 136.7 %all-gather.5.cloned.1.call-start = ((), (), s32[]{:S(2)}) async-start(), calls=%async_computation.3 | async-start | bytes 4915200 | tf_op jit(solution)/shard_map/all_gather | solution.py:45
  59.0 178.9 %reduce-scatter.2.cloned.1.call-start = ((), (), s32[]{:S(2)}) async-start(), calls=%async_computation.4 | async-start | bytes 4915200 | tf_op jit(solution)/shard_map/reduce_scatter | solution.py:54
  143.9 7.6 %copy-start.3 = (bf16[1,1280,1280]{2,1,0:T(8,128)(2,1)S(1)}, bf16[1,1280,1280]{2,1,0:T(8,128)(2,1)}, u32[]{:S(2)}) copy-start(bf16[1,1280,1280]{2,1,0:T(8,128)(2,1)} %param.15) | copy-start | bytes 9830404
  159.8 92.7 %copy-start.1 = (bf16[128,1024]{1,0:T(8,128)(2,1)S(1)}, bf16[128,1024]{1,0:T(8,128)(2,1)}, u32[]{:S(2)}) copy-start(bf16[128,1024]{1,0:T(8,128)(2,1)} %param.18) | copy-start | bytes 786436
  159.8 123.1 %copy-start.4 = (f32[256]{0:T(256)S(1)}, f32[256]{0:T(256)}, u32[]{:S(2)}) copy-start(f32[256]{0:T(256)} %param.12) | copy-start | bytes 3076
  240.2 40.4 %all-to-all-start.1 = ((bf16[64,6,1280]{2,1,0:T(8,128)(2,1)}), bf16[64,6,1280]{2,1,0:T(8,128)(2,1)}, u32[]{:S(2)}, u32[]{:S(2)}) async-start(bf16[64,6,1280]{2,1,0:T(8,128)(2,1)} %reshape.87), calls=%async_computation.2 | async-start | bytes 2621440 | tf_op jit(solution)/shard_map/all_to_all | solution.py:58
  252.4 68.1 %all-gather.7.cloned.1.call-start = ((), (), s32[]{:S(2)}) async-start(), calls=%async_computation.5 | async-start | bytes 1310720 | tf_op jit(solution)/shard_map/all_gather | solution.py:71
  253.4 88.7 %all-gather.9.cloned.1.call-start = ((), (), s32[]{:S(2)}) async-start(), calls=%async_computation.6 | async-start | bytes 1310720 | tf_op jit(solution)/shard_map/all_gather | solution.py:70
  282.9 6.2 %copy-start.5 = (s32[128]{0:T(128)S(1)}, s32[128]{0:T(128)}, u32[]{:S(2)}) copy-start(s32[128]{0:T(128)} %param.19) | copy-start | bytes 1540
  285.7 56.5 %copy-start.2 = (bf16[128,1024]{1,0:T(8,128)(2,1)S(1)}, bf16[128,1024]{1,0:T(8,128)(2,1)}, u32[]{:S(2)}) copy-start(bf16[128,1024]{1,0:T(8,128)(2,1)} %fusion.29) | copy-start | bytes 786436
Sparse Core Ops, SparseCore 0:
  59.1 84.7 all-gather.4
  159.9 78.0 reduce-scatter.1
  255.0 46.5 all-gather.6
  303.8 38.2 all-gather.8
where the time goes:
time: 353 us; the launch traced here: 352 us
  waiting for transfers between devices  207 us (59%)
  blocking collectives  72.9 us (21%)
  matrix products  32 us (9%)
  between operations  13.9 us (4%)
  starting transfers between devices  12.5 us (4%)
  local copies, waits for them, and re-layouts  9.24 us (3%)
  other arithmetic  4.81 us (1%)
    all_gather x1, waiting for transfers between devices, shards(): lax.all_gather(received, 'loop', axis=0, tiled=True)  84.8 us
    reduce_scatter x1, waiting for transfers between devices, shards(): lax.psum_scatter(term.astype(jnp.float32).astype(jnp.bfloat16), 'loop', s...  78.2 us
    all_to_all x1, blocking collectives, shards(): lax.all_to_all(outgoing, 'expert', split_axis=0, concat_axis=0, tiled=True)  41.5 us
    all_gather x1, blocking collectives, shards(): their_label = lax.all_gather(label_values, 'loop', axis=0, tiled=True)  31.4 us
    all_to_all x1, waiting for transfers between devices, shards(): lax.all_to_all(going_back, 'expert', split_axis=0, concat_axis=0, tiled=T...  27 us
    all_gather x1, waiting for transfers between devices, shards(): their_image = lax.all_gather(image, 'loop', axis=0, tiled=True)  16.7 us
    all_to_all x1, starting transfers between devices, shards(): lax.all_to_all(going_back, 'expert', split_axis=0, concat_axis=0, tiled=T...  12.1 us
    dot_general x1, matrix products, shards(): lax.dot_general(hidden, second_local, (((1,), (1,)), ((), ())), preferred...  8.21 us
  transfers between devices with their start and end apart: 5, of which 4 were waited for; matrix products, arithmetic and copies ran while one was open for 4% of the time, Pallas kernels for 0%

commit v1 on v0

v1 whole, which is shorter than its diff:
```python
import jax
import jax.numpy as jnp
from jax import lax
from jax.sharding import PartitionSpec as P

PATCHES = 256
PAIRS = 128
LOOP = 4

scale_logit = 4.0
shift_logit = -1.0


def normalize_rows(values):
    return values / jnp.sqrt(jnp.sum(values * values, axis=1, keepdims=True) + 1e-06)


def coefficients(logit, sign):
    return (-scale_logit * sign * jax.nn.sigmoid(-sign * logit)).astype(jnp.bfloat16)


def signs(rows, columns):
    return jnp.where(rows[:, None] == columns[None, :], 1.0, -1.0).astype(jnp.float32)


def logits(rows, columns):
    return (
        scale_logit
        * lax.dot_general(
            rows, columns, (((1,), (1,)), ((), ())), preferred_element_type=jnp.float32
        )
        + shift_logit
    )


def shards(
    tokens, routes, gate_prob, expert_quota, w_in, w_out, other_pooled, head, text_embed, labels
):
    experts = lax.axis_size("expert")
    tok_rows = tokens.shape[0]
    width = tokens.shape[1]
    embed = head.shape[1]
    slots = max(2, 3 * tok_rows // (2 * experts))

    pooled = jnp.concatenate([jnp.zeros((1, width), jnp.bfloat16), other_pooled], axis=0)
    image = normalize_rows(jnp.dot(pooled, head, preferred_element_type=jnp.float32)).astype(
        jnp.bfloat16
    )
    text = normalize_rows(text_embed.astype(jnp.float32)).astype(jnp.bfloat16)
    label_values = labels.astype(jnp.bfloat16)
    label_rows = jnp.pad(label_values[None, :], ((0, 7), (0, embed - PAIRS)))
    packed = jnp.concatenate([text, image, label_rows], axis=0)
    gathered = lax.all_gather(packed, "loop", axis=0)

    expert_ids = routes[:, 0]
    onehot = (expert_ids[:, None] == jnp.arange(experts, dtype=jnp.int32)[None, :]).astype(
        jnp.int32
    )
    slot = jnp.sum((jnp.cumsum(onehot, axis=0) - 1) * onehot, axis=1)
    quota_tok = jnp.sum(onehot * expert_quota[None, :], axis=1)
    position = jnp.where(slot < quota_tok, expert_ids * slots + slot, -1)
    placing = (position[:, None] == jnp.arange(experts * slots, dtype=jnp.int32)[None, :]).astype(
        jnp.bfloat16
    )
    outgoing = lax.dot_general(
        placing, tokens, (((0,), (0,)), ((), ())), preferred_element_type=jnp.float32
    )
    outgoing = outgoing.astype(jnp.bfloat16).reshape(experts, slots, width)
    received = lax.all_to_all(outgoing, "expert", split_axis=0, concat_axis=0, tiled=True).reshape(
        experts * slots, width
    )
    received, gathered = lax.optimization_barrier((received, gathered))
    first_local = w_in[0]
    second_local = w_out[0]
    hidden = jax.nn.gelu(
        jnp.dot(
            lax.all_gather(received, "loop", axis=0, tiled=True),
            first_local,
            preferred_element_type=jnp.float32,
        )
    ).astype(jnp.bfloat16)
    term = lax.dot_general(
        hidden, second_local, (((1,), (1,)), ((), ())), preferred_element_type=jnp.float32
    )
    term = lax.optimization_barrier(term.astype(jnp.bfloat16))
    result = lax.psum_scatter(
        term.astype(jnp.float32).astype(jnp.bfloat16), "loop", scatter_dimension=0, tiled=True
    )

    their_text = gathered[:, :PAIRS].reshape(LOOP * PAIRS, embed)
    their_image = gathered[:, PAIRS : 2 * PAIRS].reshape(LOOP * PAIRS, embed)
    their_label = gathered[:, 2 * PAIRS, :PAIRS].reshape(LOOP * PAIRS)
    logit_mine = logits(image, their_text)
    sign_mine = signs(label_values, their_label)
    loss_acc = jnp.sum(jax.nn.softplus(-sign_mine * logit_mine), axis=1)
    image_acc = jnp.dot(
        coefficients(logit_mine, sign_mine), their_text, preferred_element_type=jnp.float32
    )
    coef_their = coefficients(logits(their_image, text), signs(their_label, label_values))
    text_acc = lax.dot_general(
        coef_their, their_image, (((0,), (0,)), ((), ())), preferred_element_type=jnp.float32
    )

    going_back = result.reshape(experts, slots, width)
    returned = lax.all_to_all(
        going_back, "expert", split_axis=0, concat_axis=0, tiled=True
    ).reshape(experts * slots, width)
    contrib = jnp.dot(placing, returned, preferred_element_type=jnp.float32)
    layer = tokens.astype(jnp.float32) + gate_prob[:, None] * contrib
    layer_out = layer.astype(jnp.bfloat16)
    own = jnp.mean(layer.reshape(-1, PATCHES, width), axis=1).astype(jnp.bfloat16)

    own_image = normalize_rows(jnp.dot(own, head, preferred_element_type=jnp.float32)).astype(
        jnp.bfloat16
    )
    me = lax.axis_index("loop")
    own_images = [own_image] + [
        lax.ppermute(own_image, "loop", [(i, (i + step) % LOOP) for i in range(LOOP)])
        for step in range(1, LOOP)
    ]
    own_images = jnp.concatenate(own_images, axis=0)
    first_labels = their_label.reshape(LOOP, PAIRS)[:, 0]
    own_labels = jnp.take(first_labels, (me - jnp.arange(LOOP)) % LOOP)
    own_logit = logits(own_image, their_text)
    own_sign = signs(label_values[:1], their_label)
    own_loss = jnp.sum(jax.nn.softplus(-own_sign * own_logit), axis=1)
    own_grad = jnp.dot(
        coefficients(own_logit, own_sign), their_text, preferred_element_type=jnp.float32
    )
    coef_own = coefficients(logits(own_images, text), signs(own_labels, label_values))
    text_acc = text_acc + lax.dot_general(
        coef_own, own_images, (((0,), (0,)), ((), ())), preferred_element_type=jnp.float32
    )
    loss_acc = lax.dynamic_update_slice(loss_acc, own_loss, (0,))
    image_acc = lax.dynamic_update_slice(image_acc, own_grad, (0, 0))
    return (layer_out, loss_acc, image_acc, text_acc)


def solution(mesh):
    rows = P(("expert", "loop"), None)
    flat = P(("expert", "loop"))
    weights = P("expert", None, "loop")
    in_specs = (rows, rows, flat, P(), weights, weights, rows, P(), rows, flat)
    out_specs = (rows, flat, rows, rows)
    return jax.shard_map(shards, mesh=mesh, in_specs=in_specs, out_specs=out_specs, check_vma=False)
```

time: 353 us -> 382 us (1.082); the launches traced: 352 us -> 376 us
  local copies, waits for them, and re-layouts: 9.24 us -> 67.4 us
  waiting for transfers between devices: 207 us -> 173 us
  blocking collectives: 72.9 us -> 57.4 us
  matrix products: 32 us -> 38.5 us
  other arithmetic: 4.81 us -> 9.1 us
  starting transfers between devices: 12.5 us -> 16.6 us
    optimization_barrier x0 -> x1, local copies, waits for them, and re-layouts: none -> 46.6 us  [shards(): received, gathered = lax.optimization_barrier((received, gathered))]
    all_gather x1 -> x0, blocking collectives: 31.4 us -> none  [shards(): their_label = lax.all_gather(label_values, 'loop', axis=0, tiled=True)]
    all_to_all x1, waiting for transfers between devices: 27 us -> 0.01 us  [shards(): lax.all_to_all(going_back, 'expert', split_axis=0, concat_axis=0, tiled=T...]
    all_to_all x1, blocking collectives: 41.5 us -> 57.4 us  [shards(): lax.all_to_all(outgoing, 'expert', split_axis=0, concat_axis=0, tiled=True)]
    dot_general x3 -> x7, matrix products: 7.45 us -> 13.9 us  [the longest x2 3.45 us: logits(): lax.dot_general(rows, columns, (((1,), (1,)), ((), ())), preferred_elemen...]
    all_gather x2 -> x1, waiting for transfers between devices: 16.7 us -> 11.3 us  [shards(): gathered = lax.all_gather(packed, 'loop', axis=0)]
    slice x1 -> x3, local copies, waits for them, and re-layouts: 0.18 us -> 4.58 us  [the longest x1 2.74 us: shards(): their_image = gathered[:, PAIRS:2 * PAIRS].reshape(LOOP * PAIRS, embed)]
    ppermute x0 -> x3, starting transfers between devices: none -> 4.29 us  [shards(): lax.ppermute(own_image, 'loop', [(i, (i + step) % LOOP) for i in range(LO...]
  transfers between devices with their start and end apart: 5 -> 7, of which waited for: 4 -> 3; matrix products, arithmetic and copies ran while one was open for 4% -> 22% of each run, Pallas kernels for 0% -> 0%
where the time goes in v1:
time: 382 us; the launch traced here: 376 us
  waiting for transfers between devices  173 us (45%)
  local copies, waits for them, and re-layouts  67.4 us (18%)
  blocking collectives  57.4 us (15%)
  matrix products  38.5 us (10%)
  starting transfers between devices  16.6 us (4%)
  between operations  14.5 us (4%)
  other arithmetic  9.1 us (2%)
    all_gather x1, waiting for transfers between devices, shards(): lax.all_gather(received, 'loop', axis=0, tiled=True)  83.3 us
    reduce_scatter x1, waiting for transfers between devices, shards(): lax.psum_scatter(term.astype(jnp.float32).astype(jnp.bfloat16), 'loop', s...  78.2 us
    all_to_all x1, blocking collectives, shards(): lax.all_to_all(outgoing, 'expert', split_axis=0, concat_axis=0, tiled=True)  57.4 us
    optimization_barrier x1, local copies, waits for them, and re-layouts, shards(): received, gathered = lax.optimization_barrier((received, gathered))  46.6 us
    all_to_all x1, starting transfers between devices, shards(): lax.all_to_all(going_back, 'expert', split_axis=0, concat_axis=0, tiled=T...  12.2 us
    all_gather x1, waiting for transfers between devices, shards(): gathered = lax.all_gather(packed, 'loop', axis=0)  11.3 us
    dot_general x1, matrix products, shards(): lax.dot_general(hidden, second_local, (((1,), (1,)), ((), ())), preferred...  8.2 us
  transfers between devices with their start and end apart: 7, of which 3 were waited for; matrix products, arithmetic and copies ran while one was open for 22% of the time, Pallas kernels for 0%

profile of v1, /device:TPU:2, one launch (start us, length us, event | category | flops | bytes accessed | tf_op | source)
XLA Modules:
  0.0 376.4 jit_solution(533126834105471515)
XLA Ops:
  7.2 0.0 all-gather.6.cloned.1.call-start
  7.3 2.6 multiply_reduce_fusion
  9.9 0.1 fusion.38
  10.0 0.5 fusion.109
  10.6 0.1 fusion.39
  10.8 0.7 copy-done.4
  11.4 0.8 fusion.37
  12.3 0.0 all-gather.6.cloned.1.call-update
  12.3 0.0 all-gather.4.cloned.1.call-start
  12.4 0.6 fusion.62
  13.0 2.0 reduce-window.6
  15.0 1.0 slice_reduce_fusion
  16.0 1.0 select_reduce_fusion
  17.0 2.6 convolution_convert_fusion.1
  19.6 2.3 reshape.188
  21.9 57.4 %all_to_all.10 = bf16[64,6,1280]{2,1,0:T(8,128)(2,1)} all-to-all(bf16[64,6,1280]{2,1,0:T(8,128)(2,1)} %reshape.188), channel_id=1, replica_groups=mesh['expert'=64,'loop'=4] {'expert'}, dimensions={0} | all-to-all | bytes 1966080 | tf_op jit(solution)/shard_map/all_to_all | solution.py:69
  79.3 2.2 reshape.189
  81.6 11.3 %all-gather.6.cloned.1.call-done = bf16[1056,1024]{1,0:T(8,128)(2,1)} async-done(((bf16[264,1024]{1,0:T(8,128)(2,1)}), bf16[1056,1024]{1,0:T(8,128)(2,1)}) %all-gather.6.cloned.1.call-update) | async-done | bytes 2162704 | tf_op jit(solution)/shard_map/all_gather | solution.py:53
  92.8 0.0 all-gather.4.cloned.1.call-update
  92.9 0.0 reduce-scatter.2.cloned.1.call-start
  92.9 83.3 %all-gather.4.cloned.1.call-done = bf16[1536,1280]{1,0:T(8,128)(2,1)} async-done(((bf16[384,1280]{1,0:T(8,128)(2,1)}), bf16[1536,1280]{1,0:T(8,128)(2,1)}) %all-gather.4.cloned.1.call-update) | async-done | bytes 3932176 | tf_op jit(solution)/shard_map/all_gather | solution.py:77
  176.2 7.6 %fusion.14 = f32[1536,1280]{1,0:T(8,128)S(1)} fusion(bf16[1536,1280]{1,0:T(8,128)(2,1)} %all-gather.4.cloned.1.call-done, bf16[1,1280,1280]{2,1,0:T(8,128)(2,1)S(1)} %copy-done), kind=kOutput, calls=%fused_computation.16 | convolution fusion | flops 5033164800 | bytes 15073280 | tf_op jit(solution)/shard_map/dot_general | solution.py:76
  183.9 8.2 %convolution_convert_fusion = bf16[1536,1280]{1,0:T(8,128)(2,1)} fusion(f32[1536,1280]{1,0:T(8,128)S(1)} %fusion.14, bf16[1,1280,1280]{2,1,0:T(8,128)(2,1)S(1)} %copy-done.10), kind=kOutput, calls=%fused_computation.10 | convolution fusion | flops 5052825600 | bytes 15073280 | tf_op jit(solution)/shard_map/dot_general | solution.py:82
  192.1 78.2 %reduce-scatter.2.cloned.1.call-done = bf16[384,1280]{1,0:T(8,128)(2,1)} async-done(((bf16[1536,1280]{1,0:T(8,128)(2,1)}), bf16[384,1280]{1,0:T(8,128)(2,1)}) %reduce-scatter.2.cloned.1.call-update) | async-done | bytes 983056 | tf_op jit(solution)/shard_map/reduce_scatter | solution.py:86
  270.2 2.3 reshape.190
  272.5 12.2 %all-to-all-start.1 = ((bf16[64,6,1280]{2,1,0:T(8,128)(2,1)}), bf16[64,6,1280]{2,1,0:T(8,128)(2,1)}, u32[]{:S(2)}, u32[]{:S(2)}) async-start(bf16[64,6,1280]{2,1,0:T(8,128)(2,1)} %reshape.190), calls=%async_computation.2 | async-start | bytes 2621440 | tf_op jit(solution)/shard_map/all_to_all | solution.py:105
  284.7 46.6 %copy.16 = bf16[4,264,1024]{0,2,1:T(8,128)(2,1)} copy(bf16[4,264,1024]{2,1,0:T(8,128)(2,1)} %bitcast.70) | data formatting | bytes 4325376 | tf_op jit(solution)/shard_map/optimization_barrier | solution.py:72
  331.3 1.4 slice_bitcast_fusion.1
  332.7 0.8 copy.17
  333.5 0.7 slice_bitcast_fusion
  334.2 1.1 gather_fusion
  335.4 1.2 and_select_fusion.1
  336.6 2.7 fusion.107
  339.4 1.9 fusion.44
  341.2 1.2 fusion.47
  342.4 3.4 fusion.27
  345.8 2.2 reshape.191
  348.1 2.8 fusion.108
  350.9 2.2 fusion.110
  353.1 0.6 multiply_reduce_fusion.1
  354.3 0.7 collective-permute-start
  355.0 3.6 collective-permute-start.1
  358.6 1.6 fusion.111
  360.2 2.0 fusion.79
  362.2 2.1 fusion.112
  364.2 1.4 dynamic_update_slice.7
  365.6 1.8 constant_dynamic-update-slice_fusion
  367.4 2.4 convolution_add_fusion
  (44 shorter events, 0.2 us)
Async XLA Ops:
  7.2 169.0 %copy-start = (bf16[1,1280,1280]{2,1,0:T(8,128)(2,1)S(1)}, bf16[1,1280,1280]{2,1,0:T(8,128)(2,1)}, u32[]{:S(2)}) copy-start(bf16[1,1280,1280]{2,1,0:T(8,128)(2,1)} %param.14) | copy-start | bytes 9830404
  7.2 2.7 copy-start.2
  7.2 5.2 %copy-start.6 = (s32[256,1]{0,1:T(1,128)S(1)}, s32[256,1]{0,1:T(1,128)}, u32[]{:S(2)}) copy-start(s32[256,1]{0,1:T(1,128)} %param.11) | copy-start | bytes 3076
  7.2 8.8 %copy-start.9 = (s32[64]{0:T(128)S(1)}, s32[64]{0:T(128)}, u32[]{:S(2)}) copy-start(s32[64]{0:T(128)} %param.13) | copy-start | bytes 772
  7.2 85.6 %all-gather.6.cloned.1.call-start = ((), (), s32[]{:S(2)}) async-start(), calls=%async_computation.5 | async-start | bytes 2703360 | tf_op jit(solution)/shard_map/all_gather | solution.py:53
  7.3 2.8 copy-start.12
  7.3 3.3 copy-start.3
  10.7 0.7 copy-start.4
  12.3 163.9 %all-gather.4.cloned.1.call-start = ((), (), s32[]{:S(2)}) async-start(), calls=%async_computation.3 | async-start | bytes 4915200 | tf_op jit(solution)/shard_map/all_gather | solution.py:77
  92.9 177.4 %reduce-scatter.2.cloned.1.call-start = ((), (), s32[]{:S(2)}) async-start(), calls=%async_computation.4 | async-start | bytes 4915200 | tf_op jit(solution)/shard_map/reduce_scatter | solution.py:86
  176.2 7.6 %copy-start.10 = (bf16[1,1280,1280]{2,1,0:T(8,128)(2,1)S(1)}, bf16[1,1280,1280]{2,1,0:T(8,128)(2,1)}, u32[]{:S(2)}) copy-start(bf16[1,1280,1280]{2,1,0:T(8,128)(2,1)} %param.15) | copy-start | bytes 9830404
  272.5 73.3 %all-to-all-start.1 = ((bf16[64,6,1280]{2,1,0:T(8,128)(2,1)}), bf16[64,6,1280]{2,1,0:T(8,128)(2,1)}, u32[]{:S(2)}, u32[]{:S(2)}) async-start(bf16[64,6,1280]{2,1,0:T(8,128)(2,1)} %reshape.190), calls=%async_computation.2 | async-start | bytes 2621440 | tf_op jit(solution)/shard_map/all_to_all | solution.py:105
  333.5 8.9 %copy-start.7 = (bf16[4,1,128]{2,0,1:T(4,128)(2,1)}, bf16[4,1,128]{2,0,1:T(4,128)(2,1)S(1)}, u32[]{:S(2)}) copy-start(bf16[4,1,128]{2,0,1:T(4,128)(2,1)S(1)} %copy.17) | copy-start | bytes 3076
  335.4 4.0 %copy-start.5 = (bf16[128,1024]{1,0:T(8,128)(2,1)S(1)}, bf16[128,1024]{1,0:T(8,128)(2,1)}, u32[]{:S(2)}) copy-start(bf16[128,1024]{1,0:T(8,128)(2,1)} %copy-done.4) | copy-start | bytes 786436
  335.4 5.8 %copy-start.8 = (bf16[128]{0:T(256)(128)(2,1)S(1)}, bf16[128]{0:T(256)(128)(2,1)}, u32[]{:S(2)}) copy-start(bf16[128]{0:T(256)(128)(2,1)} %get-tuple-element.18) | copy-start | bytes 772
  339.4 1.9 copy-start.1
  342.4 5.7 %copy-start.11 = (f32[256]{0:T(256)S(1)}, f32[256]{0:T(256)}, u32[]{:S(2)}) copy-start(f32[256]{0:T(256)} %param.12) | copy-start | bytes 3076
  354.3 13.1 %collective-permute-start = (bf16[1,1024]{1,0:T(2,128)(2,1)S(1)}, bf16[1,1024]{1,0:T(2,128)(2,1)S(1)}, u32[]{:S(2)}, u32[]{:S(2)}) collective-permute-start(bf16[1,1024]{1,0:T(2,128)(2,1)S(1)} %convert_element_type.77), channel_id=1, source_target_pairs={{0,1},{1,2},{2,3},{3,0},{4,5},{5,6},{6,7},{7,4},{8,9},{9,10},{10,1... | collective-permute-start | bytes 6152 | tf_op jit(solution)/shard_map/ppermute | solution.py:118
  355.0 12.4 %collective-permute-start.1 = (bf16[1,1024]{1,0:T(2,128)(2,1)S(1)}, bf16[1,1024]{1,0:T(2,128)(2,1)S(1)}, u32[]{:S(2)}, u32[]{:S(2)}) collective-permute-start(bf16[1,1024]{1,0:T(2,128)(2,1)S(1)} %convert_element_type.77), channel_id=1, source_target_pairs={{0,2},{1,3},{2,0},{3,1},{4,6},{5,7},{6,4},{7,5},{8,10},{9,11},{10,... | collective-permute-start | bytes 6152 | tf_op jit(solution)/shard_map/ppermute | solution.py:118
  358.6 8.8 %collective-permute-start.2 = (bf16[1,1024]{1,0:T(2,128)(2,1)S(1)}, bf16[1,1024]{1,0:T(2,128)(2,1)S(1)}, u32[]{:S(2)}, u32[]{:S(2)}) collective-permute-start(bf16[1,1024]{1,0:T(2,128)(2,1)S(1)} %convert_element_type.77), channel_id=1, source_target_pairs={{0,3},{1,0},{2,1},{3,2},{4,7},{5,4},{6,5},{7,6},{8,11},{9,8},{10,9... | collective-permute-start | bytes 6152 | tf_op jit(solution)/shard_map/ppermute | solution.py:118
Sparse Core Ops, SparseCore 0:
  12.4 80.3 all-gather.5
  94.7 81.5 all-gather.3
  192.2 78.0 reduce-scatter.1

commit v2 on v0

v2 whole, which is shorter than its diff:
```python
import functools

import jax
import jax.numpy as jnp
import numpy as np
from jax import lax
from jax.experimental import pallas as pl
from jax.experimental.pallas import tpu as pltpu
from jax.sharding import Mesh
from jax.sharding import PartitionSpec as P

PATCHES = 256
PAIRS = 128
LOOP = 4
RING = 8
PLANE = 32
SLOTS = 6
EXPERTS = 64
GROUPS = 4
PIECE = 48
BLOCK = PLANE * SLOTS
TOK = 256
ROWS = TOK + 16
SHARD = 2 * PAIRS + 16

AXES = ("zh", "y", "x", "c", "zl")
EXPERT = ("zh", "y", "x", "c")
FLAT = ("y", "x", "c")
Z = ("zh", "zl")

scale_logit = 4.0
shift_logit = -1.0

F32 = jnp.float32
BF16 = jnp.bfloat16


def call(kernel, out_shape, scratch=(), aliases=None, flops=0, vmem=24):
    return pl.pallas_call(
        kernel,
        out_shape=out_shape,
        scratch_shapes=list(scratch),
        input_output_aliases=aliases or {},
        cost_estimate=pl.CostEstimate(flops=flops, bytes_accessed=4 << 20, transcendentals=0),
        compiler_params=pltpu.CompilerParams(vmem_limit_bytes=vmem << 20),
    )


def struct(shape, dtype):
    return jax.ShapeDtypeStruct(shape, dtype)


def iota(shape, dim):
    return lax.broadcasted_iota(jnp.int32, shape, dim)


def dot(a, b):
    return jnp.dot(a, b, preferred_element_type=F32)


def dot_t(a, b):
    return lax.dot_general(a, b, (((1,), (1,)), ((), ())), preferred_element_type=F32)


def as_row(column):
    n = column.shape[0]
    return jnp.sum(jnp.where(iota((n, n), 0) == iota((n, n), 1), column, 0.0), 0, keepdims=True)


def as_column(row):
    n = row.shape[1]
    return jnp.sum(jnp.where(iota((n, n), 0) == iota((n, n), 1), row, 0.0), 1, keepdims=True)


def normalize_rows(values):
    return values / jnp.sqrt(jnp.sum(values * values, axis=1, keepdims=True) + 1e-06)


def softplus(x):
    return jnp.maximum(x, 0.0) + jnp.log1p(jnp.exp(-jnp.abs(x)))


def coefficients(logit, sign):
    return (-scale_logit * sign * lax.logistic(-sign * logit)).astype(BF16)


def sign_of(a, b):
    return jnp.where(a == b, 1.0, -1.0)


def swap_matrix():
    order = np.arange(8 * PIECE).reshape(8, 8, SLOTS).transpose(1, 0, 2).reshape(-1)
    return np.eye(8 * PIECE, dtype=np.float32)[order].astype(jnp.bfloat16)


def half_matrix():
    order = np.arange(2 * BLOCK).reshape(PLANE, 2, SLOTS).transpose(1, 0, 2).reshape(-1)
    return np.eye(2 * BLOCK, dtype=np.float32)[order].astype(jnp.bfloat16)


def route_kernel(tokens, routes, quota, packed, outgoing, position):
    half = packed.shape[1]
    ids = routes[...]
    hit = ids == iota((TOK, EXPERTS), 1)
    onehot = jnp.where(hit, 1.0, 0.0)
    before = dot(
        jnp.where(iota((TOK, TOK), 1) < iota((TOK, TOK), 0), 1.0, 0.0).astype(BF16),
        onehot.astype(BF16),
    )
    slot = jnp.sum(onehot * before, axis=1, keepdims=True)
    limit = jnp.sum(onehot * quota[...].astype(F32), axis=1, keepdims=True)
    kept = slot < limit
    far = jnp.where(ids >= PLANE, 1, 0)
    place = (ids - far * PLANE) * (2 * SLOTS) + far * SLOTS
    column = jnp.where(kept, place.astype(F32) + slot, -1.0)
    position[...] = column
    id_row = as_row(ids.astype(F32))
    slot_row = as_row(jnp.where(kept, slot, 64.0))
    line = iota((16, TOK), 0)
    packed[0:TOK, :] = tokens[:, :half]
    packed[TOK:ROWS, :] = jnp.zeros((16, half), BF16)
    packed[TOK:ROWS, 0:TOK] = jnp.where(
        line == 0, id_row, jnp.where(line == 1, slot_row, 0.0)
    ).astype(BF16)
    place = as_row(column).astype(jnp.int32)
    onto = jnp.where(iota((EXPERTS * SLOTS, TOK), 0) == place, 1.0, 0.0).astype(BF16)
    outgoing[...] = dot(onto, tokens[:, half:]).astype(BF16)


def choose_kernel(gathered, side, swap, chosen, target, held):
    first = side[0, 0].astype(F32) * PLANE
    for z in range(RING):
        info = gathered[z * ROWS + TOK : (z + 1) * ROWS, 0:TOK].astype(F32)
        ids = info[0:1] - first
        slot = info[1:2]
        mine = (ids >= 0.0) & (ids < float(PLANE)) & (slot < float(SLOTS))
        row = jnp.where(mine, ids * SLOTS + slot, -1.0)
        target[z : z + 1, :] = row
        onto = jnp.where(iota((BLOCK, TOK), 0) == row.astype(jnp.int32), 1.0, 0.0).astype(BF16)
        held[z * BLOCK : (z + 1) * BLOCK, :] = dot(
            onto, gathered[z * ROWS : z * ROWS + TOK, :]
        ).astype(BF16)
    for g in range(GROUPS):
        rows = jnp.concatenate(
            [held[z * BLOCK + g * PIECE : z * BLOCK + (g + 1) * PIECE, :] for z in range(RING)], 0
        )
        chosen[g * 8 * PIECE : (g + 1) * 8 * PIECE, :] = dot(swap[...], rows).astype(BF16)


def spread_kernel(rows, swap, out):
    for g in range(GROUPS):
        moved = dot(swap[...], rows[g * 8 * PIECE : (g + 1) * 8 * PIECE, :]).astype(BF16)
        for z in range(RING):
            at = z * BLOCK + g * PIECE
            out[at : at + PIECE, :] = moved[z * PIECE : (z + 1) * PIECE, :]


def unspread_kernel(rows, swap, out):
    for g in range(GROUPS):
        starts = [z * BLOCK + g * PIECE for z in range(RING)]
        piece = jnp.concatenate([rows[at : at + PIECE, :] for at in starts], 0)
        out[g * 8 * PIECE : (g + 1) * 8 * PIECE, :] = dot(swap[...], piece).astype(BF16)


def turn_kernel(rows, matrix, out):
    out[...] = dot(matrix[...], rows[...]).astype(BF16)


def expert_kernel(side, rows, partial, first, second, hidden, term):
    x = jnp.concatenate([rows[0, 0], rows[1, 0]], 0)
    value = jax.nn.gelu(partial[...] + dot(x, first[...])).astype(BF16)
    hidden[...] = value
    result = dot_t(value, second[...]).astype(BF16)
    nothing = jnp.zeros((BLOCK, result.shape[1]), BF16)
    for k in range(2):
        mine = result[k * BLOCK : (k + 1) * BLOCK]
        for far in range(2):
            term[k, far] = jnp.where(side[0] == far, mine, nothing)


def expert_right(side, rows, partial, first, second):
    half, inner = first.shape
    spec = pl.BlockSpec
    return pl.pallas_call(
        expert_kernel,
        out_shape=(
            struct((RING * BLOCK, inner), BF16),
            struct((RING, 2, BLOCK, half), BF16),
        ),
        grid_spec=pltpu.PrefetchScalarGridSpec(
            num_scalar_prefetch=1,
            grid=(RING // 2,),
            in_specs=[
                spec((2, 1, BLOCK, half), lambda i, side: (i, side[0], 0, 0)),
                spec((2 * BLOCK, inner), lambda i, side: (i, 0)),
                spec((half, inner), lambda i, side: (0, 0)),
                spec((half, inner), lambda i, side: (0, 0)),
            ],
            out_specs=[
                spec((2 * BLOCK, inner), lambda i, side: (i, 0)),
                spec((2, 2, BLOCK, half), lambda i, side: (i, 0, 0, 0)),
            ],
        ),
        cost_estimate=pl.CostEstimate(
            flops=4 * RING * BLOCK * half * inner, bytes_accessed=20 << 20, transcendentals=0
        ),
        compiler_params=pltpu.CompilerParams(vmem_limit_bytes=32 << 20),
    )(side, rows, partial, first, second)


def scatter_kernel(rows, swap, target, out, held):
    for g in range(GROUPS):
        moved = dot(swap[...], rows[g * 8 * PIECE : (g + 1) * 8 * PIECE, :]).astype(BF16)
        for z in range(RING):
            at = z * BLOCK + g * PIECE
            held[at : at + PIECE, :] = moved[z * PIECE : (z + 1) * PIECE, :]
    for z in range(RING):
        column = as_column(target[z : z + 1, :]).astype(jnp.int32)
        onto = jnp.where(iota((TOK, BLOCK), 1) == column, 1.0, 0.0).astype(BF16)
        out[z * TOK : (z + 1) * TOK, :] = dot(
            onto, held[z * BLOCK : (z + 1) * BLOCK, :]
        ).astype(BF16)


def layer_kernel(tokens, position, gate, returned, given, head, layer_out, own_image):
    half = given.shape[1]
    onto = jnp.where(
        iota((TOK, EXPERTS * SLOTS), 1) == position[...].astype(jnp.int32), 1.0, 0.0
    ).astype(BF16)
    left = tokens[:, :half].astype(F32) + gate[...] * given[...].astype(F32)
    right = tokens[:, half:].astype(F32) + gate[...] * dot(onto, returned[...])
    layer_out[:, :half] = left.astype(BF16)
    layer_out[:, half:] = right.astype(BF16)
    own_left = (jnp.sum(left, axis=0, keepdims=True) / PATCHES).astype(BF16)
    own_right = (jnp.sum(right, axis=0, keepdims=True) / PATCHES).astype(BF16)
    own_left = jnp.broadcast_to(own_left.astype(F32), (16, half)).astype(BF16)
    own_right = jnp.broadcast_to(own_right.astype(F32), (16, half)).astype(BF16)
    image = dot(own_left, head[:half, :]) + dot(own_right, head[half:, :])
    own_image[...] = normalize_rows(image)[0:1].astype(BF16)


def pack_kernel(pooled, head, text_embed, labels, packed):
    packed[0:PAIRS, :] = normalize_rows(text_embed[...].astype(F32)).astype(BF16)
    image = normalize_rows(dot(pooled[...], head[...]))
    packed[PAIRS : 2 * PAIRS, :] = image.astype(BF16)
    packed[2 * PAIRS : SHARD, :] = jnp.zeros((16, packed.shape[1]), BF16)
    packed[2 * PAIRS : SHARD, 0:PAIRS] = jnp.where(
        iota((16, PAIRS), 0) == 0, labels[...].astype(F32), 0.0
    ).astype(BF16)


def label_row(shard):
    return shard[2 * PAIRS : SHARD, 0:PAIRS].astype(F32)[0:1]


def score_kernel(own, s1, s2, s3, loss, image_acc, text_acc):
    text = own[0:PAIRS, :]
    image = own[PAIRS : 2 * PAIRS, :]
    mine = as_column(label_row(own))
    losses = jnp.zeros((PAIRS, 1), F32)
    for k, shard in enumerate((own, s1, s2, s3)):
        their_text = shard[0:PAIRS, :]
        their_image = shard[PAIRS : 2 * PAIRS, :]
        sign = sign_of(mine, label_row(shard))
        logit = scale_logit * dot_t(image, their_text) + shift_logit
        losses = losses + jnp.sum(softplus(-sign * logit), axis=1, keepdims=True)
        grad = dot(coefficients(logit, sign), their_text)
        logit = scale_logit * dot_t(text, their_image) + shift_logit
        text_grad = dot(coefficients(logit, sign), their_image)
        image_acc[...] = grad if k == 0 else image_acc[...] + grad
        text_acc[...] = text_grad if k == 0 else text_acc[...] + text_grad
    loss[...] = as_row(losses)


def own_row_kernel(own_image, own, s1, s2, s3, loss, image_acc, loss_out, image_out):
    row = jnp.broadcast_to(own_image[...].astype(F32), (16, own_image.shape[1])).astype(BF16)
    label = label_row(own)[0:1, 0:1]
    total = jnp.zeros((16, 1), F32)
    grad = jnp.zeros((16, own_image.shape[1]), F32)
    for shard in (own, s1, s2, s3):
        their_text = shard[0:PAIRS, :]
        sign = sign_of(label, label_row(shard))
        logit = scale_logit * dot_t(row, their_text) + shift_logit
        total = total + jnp.sum(softplus(-sign * logit), axis=1, keepdims=True)
        grad = grad + dot(coefficients(logit, sign), their_text)
    loss_out[...] = jnp.where(iota((1, PAIRS), 1) == 0, total[0:1], loss[...])
    image_out[...] = image_acc[...]
    image_out[0:1, :] = grad[0:1]


def own_text_kernel(i0, i1, i2, i3, own, s1, s2, s3, text_acc, out):
    line = iota((16, i0.shape[1]), 0)
    images = jnp.zeros((16, i0.shape[1]), F32)
    for k, row in enumerate((i0, i1, i2, i3)):
        images = jnp.where(line == k, row[...].astype(F32), images)
    images = images.astype(BF16)
    place = iota((1, 16), 1)
    labels = jnp.full((1, 16), -1.0, F32)
    for k, shard in enumerate((own, s1, s2, s3)):
        labels = jnp.where(place == k, label_row(shard)[0:1, 0:1], labels)
    sign = sign_of(as_column(label_row(own)), labels)
    logit = scale_logit * dot_t(own[0:PAIRS, :], images) + shift_logit
    out[...] = text_acc[...] + dot(coefficients(logit, sign), images)


def shards(
    tokens, routes, gate_prob, expert_quota, w_in, w_out, other_pooled, head, text_embed, labels
):
    width = tokens.shape[1]
    half = width // 2
    embed = head.shape[1]
    swap = jnp.asarray(swap_matrix())
    apart = jnp.asarray(half_matrix())
    together = jnp.asarray(half_matrix().T)
    side = lax.axis_index("zh").astype(jnp.int32).reshape(1, 1)

    packed, outgoing, position = call(
        route_kernel,
        (
            struct((ROWS, half), BF16),
            struct((EXPERTS * SLOTS, half), BF16),
            struct((TOK, 1), F32),
        ),
        flops=1 << 28,
    )(tokens, routes, expert_quota.reshape(1, EXPERTS))

    pooled = jnp.concatenate([jnp.zeros((1, width), BF16), other_pooled], axis=0)
    own_pairs = call(pack_kernel, struct((SHARD, embed), BF16), flops=1 << 28)(
        pooled, head, text_embed, labels.reshape(1, PAIRS)
    )
    shift = lambda value, step: lax.ppermute(
        value, "zl", [(i, (i + step) % LOOP) for i in range(LOOP)]
    )

    around = lax.all_gather(packed, Z, axis=0, tiled=True)
    received = lax.all_to_all(
        outgoing.reshape(PLANE, 2 * SLOTS, half), FLAT, split_axis=0, concat_axis=0, tiled=True
    ).reshape(2 * BLOCK, half)
    received = call(turn_kernel, struct((2 * BLOCK, half), BF16), flops=1 << 28)(received, apart)
    received, around, own_pairs = lax.optimization_barrier((received, around, own_pairs))
    right = lax.all_gather(received, Z, axis=0, tiled=True)

    chosen, target = call(
        choose_kernel,
        (struct((RING * BLOCK, half), BF16), struct((RING, TOK), F32)),
        scratch=[pltpu.VMEM((RING * BLOCK, half), BF16)],
        flops=1 << 30,
    )(around, side, swap)
    arrived = lax.all_to_all(
        chosen.reshape(PLANE, PIECE, half), FLAT, split_axis=0, concat_axis=0, tiled=True
    ).reshape(RING * BLOCK, half)
    left = call(spread_kernel, struct((RING * BLOCK, half), BF16), flops=1 << 30)(arrived, swap)

    first = w_in[0]
    second = w_out[0]
    partial = dot(left, first[:half])
    partial, own_pairs = lax.optimization_barrier((partial, own_pairs))
    pairs = [own_pairs] + [shift(own_pairs, step) for step in range(1, LOOP)]
    hidden, term_right = expert_right(
        side.reshape(1), right.reshape(RING, 2, BLOCK, half), partial, first[half:], second[half:]
    )
    hidden, term_right, pairs[1] = lax.optimization_barrier((hidden, term_right, pairs[1]))
    result = lax.psum_scatter(
        term_right.reshape(2 * RING * BLOCK, half), Z, scatter_dimension=0, tiled=True
    )
    term_left = lax.optimization_barrier(dot_t(hidden, second[:half]).astype(BF16))
    leaving = call(unspread_kernel, struct((RING * BLOCK, half), BF16), flops=1 << 30)(
        term_left, swap
    )
    back = lax.all_to_all(
        leaving.reshape(PLANE, PIECE, half), FLAT, split_axis=0, concat_axis=0, tiled=True
    ).reshape(RING * BLOCK, half)
    back, result, *pairs = lax.optimization_barrier((back, result, *pairs))
    by_token = call(
        scatter_kernel,
        struct((RING * TOK, half), BF16),
        scratch=[pltpu.VMEM((RING * BLOCK, half), BF16)],
        flops=1 << 30,
    )(back, swap, target)
    given = lax.psum_scatter(by_token, Z, scatter_dimension=0, tiled=True)
    result = call(turn_kernel, struct((2 * BLOCK, half), BF16), flops=1 << 28)(result, together)
    returned = lax.all_to_all(
        result.reshape(PLANE, 2 * SLOTS, half), FLAT, split_axis=0, concat_axis=0, tiled=True
    ).reshape(2 * BLOCK, half)

    square = struct((PAIRS, embed), F32)
    line = struct((1, PAIRS), F32)
    loss, image_acc, text_acc = call(score_kernel, (line, square, square), flops=1 << 30)(*pairs)
    loss, image_acc, text_acc, returned = lax.optimization_barrier(
        (loss, image_acc, text_acc, returned)
    )

    layer_out, own_image = call(
        layer_kernel, (struct((TOK, width), BF16), struct((1, embed), BF16)), flops=1 << 28
    )(tokens, position, gate_prob.reshape(TOK, 1), returned, given, head)
    own_images = [own_image] + [shift(own_image, step) for step in range(1, LOOP)]
    loss, image_acc = call(own_row_kernel, (line, square), flops=1 << 26)(
        own_image, *pairs, loss, image_acc
    )
    text_acc = call(own_text_kernel, square, flops=1 << 26)(*own_images, *pairs, text_acc)
    return (layer_out, loss.reshape(PAIRS), image_acc, text_acc)


def solution(mesh):
    fine = Mesh(mesh.devices.reshape(2, 4, 4, 2, LOOP), AXES)
    rows = P(AXES, None)
    flat = P(AXES)
    weights = P(EXPERT, None, "zl")
    in_specs = (rows, rows, flat, P(), weights, weights, rows, P(), rows, flat)
    out_specs = (rows, flat, rows, rows)
    return jax.shard_map(shards, mesh=fine, in_specs=in_specs, out_specs=out_specs, check_vma=False)
```

time: 353 us -> 297 us (0.84)
  waiting for transfers between devices: 207 us -> 127 us
  blocking collectives: 72.9 us -> 33.2 us
  local copies, waits for them, and re-layouts: 9.24 us -> 44.6 us
  Pallas kernels: 0 us -> 28.7 us
  starting transfers between devices: 12.5 us -> 37.5 us
  matrix products: 32 us -> 11.2 us
  other arithmetic: 4.81 us -> 0 us
    all_gather x3 -> x2, waiting for transfers between devices: 102 us -> 27.1 us  [the longest x1 20.3 us: shards(): around = lax.all_gather(packed, Z, axis=0, tiled=True)]
    ppermute x0 -> x6, waiting for transfers between devices: none -> 40 us  [shards(): lax.ppermute(value, 'zl', [(i, (i + step) % LOOP) for i in range(LOOP)])]
    unnamed x12 -> x81, local copies, waits for them, and re-layouts: 0.03 us -> 35.7 us
    reduce_scatter x1 -> x2, waiting for transfers between devices: 78.2 us -> 44.6 us  [the longest x1 26.7 us: shards(): lax.psum_scatter(term_right.reshape(2 * RING * BLOCK, half), Z, scatter_d...]
    all_gather x1 -> x0, blocking collectives: 31.4 us -> none  [shards(): their_label = lax.all_gather(label_values, 'loop', axis=0, tiled=True)]
    pallas_call x0 -> x13, Pallas kernels: none -> 28.7 us  [the longest x1 7.77 us: expert_right(): pl.pallas_call(expert_kernel, out_shape=(struct((RING * BLOCK, inner), BF...]
    dot_general x8 -> x2, matrix products: 32 us -> 11.2 us  [the longest x1 5.87 us: dot_t(): lax.dot_general(a, b, (((1,), (1,)), ((), ())), preferred_element_type=F32)]
    all_to_all x1 -> x3, starting transfers between devices: 12.1 us -> 25.6 us  [the longest x1 10.4 us: shards(): lax.all_to_all(leaving.reshape(PLANE, PIECE, half), FLAT, split_axis=0, c...]
  transfers between devices with their start and end apart: 5 -> 13, of which waited for: 4 -> 8; matrix products, arithmetic and copies ran while one was open for 4% -> 7% of each run, Pallas kernels for 0% -> 7%
where the time goes in v2:
time: 297 us; the launch traced here: 296 us
  waiting for transfers between devices  127 us (43%)
  local copies, waits for them, and re-layouts  44.6 us (15%)
  starting transfers between devices  37.5 us (13%)
  blocking collectives  33.2 us (11%)
  Pallas kernels  28.7 us (10%)
  between operations  14.1 us (5%)
  matrix products  11.2 us (4%)
    ppermute x6, waiting for transfers between devices, shards(): lax.ppermute(value, 'zl', [(i, (i + step) % LOOP) for i in range(LOOP)])  40 us
    unnamed x81, local copies, waits for them, and re-layouts  35.7 us
    all_to_all x1, blocking collectives, shards(): lax.all_to_all(chosen.reshape(PLANE, PIECE, half), FLAT, split_axis=0, co...  33.2 us
    reduce_scatter x1, waiting for transfers between devices, shards(): lax.psum_scatter(term_right.reshape(2 * RING * BLOCK, half), Z, scatter_d...  26.7 us
    all_gather x1, waiting for transfers between devices, shards(): around = lax.all_gather(packed, Z, axis=0, tiled=True)  20.3 us
    reduce_scatter x1, waiting for transfers between devices, shards(): given = lax.psum_scatter(by_token, Z, scatter_dimension=0, tiled=True)  17.8 us
    ppermute x6, starting transfers between devices, shards(): lax.ppermute(value, 'zl', [(i, (i + step) % LOOP) for i in range(LOOP)])  11.8 us
    all_to_all x1, starting transfers between devices, shards(): lax.all_to_all(leaving.reshape(PLANE, PIECE, half), FLAT, split_axis=0, c...  10.4 us
  transfers between devices with their start and end apart: 13, of which 8 were waited for; matrix products, arithmetic and copies ran while one was open for 7% of the time, Pallas kernels for 7%

profile of v2, /device:TPU:2, one launch (start us, length us, event | category | flops | bytes accessed | tf_op | source)
XLA Modules:
  0.0 296.3 jit_solution(4420195843833958194)
XLA Ops:
  8.2 1.1 copy-done.17
  9.9 1.4 shard_map.156
  13.0 7.7 %all-to-all-start = ((bf16[32,12,640]{2,1,0:T(8,128)(2,1)}), bf16[32,12,640]{2,1,0:T(8,128)(2,1)}, u32[]{:S(2)}, u32[]{:S(2)}) async-start(bf16[32,12,640]{2,1,0:T(8,128)(2,1)} %reshape.59), calls=%async_computation | async-start | bytes 1310720 | tf_op jit(solution)/shard_map/all_to_all | solution.py:336
  22.5 10.2 %all-to-all-done = bf16[32,12,640]{2,1,0:T(8,128)(2,1)} async-done(((bf16[32,12,640]{2,1,0:T(8,128)(2,1)}), bf16[32,12,640]{2,1,0:T(8,128)(2,1)}, u32[]{:S(2)}, u32[]{:S(2)}) %all-to-all-start) | async-done | bytes 491552 | tf_op jit(solution)/shard_map/all_to_all | solution.py:336
  32.6 2.0 reshape.60.rows
  34.6 1.0 copy-done.13
  37.8 20.3 %all-gather.3.cloned.1.call-done.gathered = bf16[2176,640]{1,0:T(8,128)(2,1)} async-done(((bf16[272,640]{1,0:T(8,128)(2,1)}), bf16[2176,640]{1,0:T(8,128)(2,1)}) %all-gather.3.cloned.1.call-update) | async-done | bytes 2785296 | tf_op jit(solution)/shard_map/all_gather | solution.py:335
  58.2 1.8 copy-done.32
  60.0 2.0 shard_map.159
  61.9 33.2 %all_to_all.20 = bf16[32,48,640]{2,1,0:T(8,128)(2,1)S(1)} all-to-all(bf16[32,48,640]{2,1,0:T(8,128)(2,1)S(1)} %bitcast.27), channel_id=1, replica_groups=mesh['zh'=2,'y'=4,'x'=4,'c'=2,'zl'=4] {'y','x','c'}, dimensions={0} | all-to-all | bytes 3932160 | tf_op jit(solution)/shard_map/all_to_all | solution.py:349
  95.1 1.3 shard_map.160
  97.1 5.3 %fusion.1.partial = f32[1536,1280]{1,0:T(8,128)} fusion(bf16[1536,640]{1,0:T(8,128)(2,1)S(1)} %shard_map.160, bf16[1,1280,1280]{2,1,0:T(8,128)(2,1)S(1)} %copy-done.36), kind=kOutput, calls=%fused_computation.2 | convolution fusion | flops 2516582400 | bytes 11468800 | tf_op jit(solution)/shard_map/dot_general | solution.py:58
  102.4 1.6 collective-permute-start
  104.0 1.9 slice_bitcast_fusion
  106.0 6.8 %all-gather.5.cloned.1.call-done = bf16[3072,640]{1,0:T(8,128)(2,1)} async-done(((bf16[384,640]{1,0:T(8,128)(2,1)}), bf16[3072,640]{1,0:T(8,128)(2,1)}) %all-gather.5.cloned.1.call-update) | async-done | bytes 3932176 | tf_op jit(solution)/shard_map/all_gather | solution.py:341
  112.7 1.4 copy-done.15
  114.2 1.4 copy-done.16
  115.6 2.1 copy-done.31
  117.7 3.2 %copy-done.34 = f32[1536,1280]{1,0:T(8,128)S(1)} copy-done((f32[1536,1280]{1,0:T(8,128)S(1)}, f32[1536,1280]{1,0:T(8,128)}, u32[]{:S(2)}) %copy-start.34) | copy-done | bytes 7864344
  121.0 7.8 %shard_map.161 = (bf16[1536,1280]{1,0:T(8,128)(2,1)S(1)}, bf16[8,2,192,640]{3,2,1,0:T(8,128)(2,1)S(1)}) custom-call(s32[1]{0:T(128)} %bitcast.2.side, bf16[8,2,192,640]{3,2,1,0:T(8,128)(2,1)S(1)} %bitcast.29, f32[1536,1280]{1,0:T(8,128)S(1)} %copy-done.34, bf16[640,1280]{1,0:T(8,128)(2,1)S(1)} %copy-done.16, bf16[640,1280]{1,0:T(8,128)(2,1)S(1)} %copy-done.15), custom_call_target="tpu_custom_call" | custom-call | flops 5033164800 | bytes 20971520 | tf_op jit(solution)/shard_map/pallas_call | solution.py:184
  128.7 1.9 copy-done.3
  130.6 1.9 copy-done.35
  132.6 5.9 %convolution_convert_fusion.rows = bf16[1536,640]{1,0:T(8,128)(2,1)S(1)} fusion(bf16[1536,1280]{1,0:T(8,128)(2,1)} %copy-done.35, bf16[1,1280,1280]{2,1,0:T(8,128)(2,1)} %param.18), kind=kOutput, calls=%fused_computation | convolution fusion | flops 2517565440 | bytes 7536640 | tf_op jit(solution)/shard_map/dot_general | solution.py:62
  138.5 1.3 shard_map.162
  139.8 1.4 copy-done.2
  141.1 10.4 %all-to-all-start.2 = ((bf16[32,48,640]{2,1,0:T(8,128)(2,1)}), bf16[32,48,640]{2,1,0:T(8,128)(2,1)}, u32[]{:S(2)}, u32[]{:S(2)}) async-start(bf16[32,48,640]{2,1,0:T(8,128)(2,1)} %bitcast.24), calls=%async_computation.2 | async-start | bytes 3932160 | tf_op jit(solution)/shard_map/all_to_all | solution.py:370
  151.6 5.1 %collective-permute-start.1 = (bf16[272,1024]{1,0:T(8,128)(2,1)S(1)}, bf16[272,1024]{1,0:T(8,128)(2,1)S(1)}, u32[]{:S(2)}, u32[]{:S(2)}) collective-permute-start(bf16[272,1024]{1,0:T(8,128)(2,1)S(1)} %shard_map.158.own), channel_id=1, source_target_pairs={{0,2},{1,3},{2,0},{3,1},{4,6},{5,7},{6,4},{7,5},{8,10},{9,11},{10,... | collective-permute-start | bytes 1671176 | tf_op jit(solution)/shard_map/ppermute | solution.py:331
  157.0 36.8 %collective-permute-done.1.s2 = bf16[272,1024]{1,0:T(8,128)(2,1)S(1)} collective-permute-done((bf16[272,1024]{1,0:T(8,128)(2,1)S(1)}, bf16[272,1024]{1,0:T(8,128)(2,1)S(1)}, u32[]{:S(2)}, u32[]{:S(2)}) %collective-permute-start.1) | collective-permute-done | bytes 557088 | tf_op jit(solution)/shard_map/ppermute | solution.py:331
  194.7 3.2 %collective-permute-done.2.s3 = bf16[272,1024]{1,0:T(8,128)(2,1)S(1)} collective-permute-done((bf16[272,1024]{1,0:T(8,128)(2,1)S(1)}, bf16[272,1024]{1,0:T(8,128)(2,1)S(1)}, u32[]{:S(2)}, u32[]{:S(2)}) %collective-permute-start.2) | collective-permute-done | bytes 557088 | tf_op jit(solution)/shard_map/ppermute | solution.py:331
  198.7 26.7 %reduce-scatter.3.cloned.1.call-done.rows = bf16[384,640]{1,0:T(8,128)(2,1)} async-done(((bf16[3072,640]{1,0:T(8,128)(2,1)}), bf16[384,640]{1,0:T(8,128)(2,1)}) %reduce-scatter.3.cloned.1.call-update) | async-done | bytes 491536 | tf_op jit(solution)/shard_map/reduce_scatter | solution.py:363
  225.4 3.7 %shard_map.165 = bf16[2048,640]{1,0:T(8,128)(2,1)S(1)} custom-call(bf16[1536,640]{1,0:T(8,128)(2,1)} %bitcast.13.rows, bf16[384,384]{1,0:T(8,128)(2,1)S(1)} %copy-done.4, f32[8,256]{1,0:T(8,128)S(1)} %get-tuple-element.60.target), custom_call_target="tpu_custom_call" | custom-call | flops 1073741824 | bytes 4194304 | tf_op jit(solution)/shard_map/pallas_call | solution.py:374
  229.1 1.5 copy-done.1
  231.6 1.0 copy-done.23
  233.8 2.0 reshape.69
  235.8 7.5 %all-to-all-start.3 = ((bf16[32,12,640]{2,1,0:T(8,128)(2,1)}), bf16[32,12,640]{2,1,0:T(8,128)(2,1)}, u32[]{:S(2)}, u32[]{:S(2)}) async-start(bf16[32,12,640]{2,1,0:T(8,128)(2,1)} %reshape.69), calls=%async_computation.4 | async-start | bytes 1310720 | tf_op jit(solution)/shard_map/all_to_all | solution.py:382
  243.4 1.1 copy-done.6
  244.5 1.1 copy-done.9
  245.5 3.1 %shard_map.163 = (f32[1,128]{1,0:T(1,128)S(1)}, f32[128,1024]{1,0:T(8,128)S(1)}, f32[128,1024]{1,0:T(8,128)S(1)}) custom-call(bf16[272,1024]{1,0:T(8,128)(2,1)S(1)} %shard_map.158.own, bf16[272,1024]{1,0:T(8,128)(2,1)} %collective-permute-done.s1, bf16[272,1024]{1,0:T(8,128)(2,1)S(1)} %copy-done.6, bf16[272,1024]{1,0:T(8,128)(2,1)S(1)} %copy-done.9), custom_call_target="tpu_custom_call" | custom-call | flops 1073741824 | bytes 4194304 | tf_op jit(solution)/shard_map/pallas_call | solution.py:388
  250.2 5.0 %all-to-all-done.3 = bf16[32,12,640]{2,1,0:T(8,128)(2,1)} async-done(((bf16[32,12,640]{2,1,0:T(8,128)(2,1)}), bf16[32,12,640]{2,1,0:T(8,128)(2,1)}, u32[]{:S(2)}, u32[]{:S(2)}) %all-to-all-start.3) | async-done | bytes 491552 | tf_op jit(solution)/shard_map/all_to_all | solution.py:382
  255.2 2.0 reshape.70.returned
  257.2 17.8 %reduce-scatter.5.cloned.1.call-done.given = bf16[256,640]{1,0:T(8,128)(2,1)} async-done(((bf16[2048,640]{1,0:T(8,128)(2,1)}), bf16[256,640]{1,0:T(8,128)(2,1)}) %reduce-scatter.5.cloned.1.call-update) | async-done | bytes 327696 | tf_op jit(solution)/shard_map/reduce_scatter | solution.py:380
  275.0 1.1 copy-done.12
  276.1 1.1 copy-done.18
  278.2 1.6 shard_map.166
  280.1 2.7 collective-permute-start.4
  282.8 1.7 collective-permute-start.5
  284.5 2.8 shard_map.167
  287.4 2.4 shard_map.168
  (86 shorter events, 15.2 us)
Async XLA Ops:
  7.2 13.7 %copy-start = (bf16[1280,1024]{1,0:T(8,128)(2,1)S(1)}, bf16[1280,1024]{1,0:T(8,128)(2,1)}, u32[]{:S(2)}) copy-start(bf16[1280,1024]{1,0:T(8,128)(2,1)} %head.3) | copy-start | bytes 7864324
  7.2 50.9 %all-gather.3.cloned.1.call-start = ((), (), s32[]{:S(2)}) async-start(), calls=%async_computation.6 | async-start | bytes 3133440 | tf_op jit(solution)/shard_map/all_gather | solution.py:335
  8.2 1.1 copy-start.17
  9.9 10.9 %copy-start.30 = (s32[128]{0:T(128)S(1)}, s32[128]{0:T(128)}, u32[]{:S(2)}) copy-start(s32[128]{0:T(128)} %param.22) | copy-start | bytes 1540
  12.0 8.7 %copy-start.38 = (bf16[127,1280]{1,0:T(8,128)(2,1)S(1)}, bf16[127,1280]{1,0:T(8,128)(2,1)}, u32[]{:S(2)}) copy-start(bf16[127,1280]{1,0:T(8,128)(2,1)} %param.19) | copy-start | bytes 975364
  13.0 19.6 %all-to-all-start = ((bf16[32,12,640]{2,1,0:T(8,128)(2,1)}), bf16[32,12,640]{2,1,0:T(8,128)(2,1)}, u32[]{:S(2)}, u32[]{:S(2)}) async-start(bf16[32,12,640]{2,1,0:T(8,128)(2,1)} %reshape.59), calls=%async_computation | async-start | bytes 1310720 | tf_op jit(solution)/shard_map/all_to_all | solution.py:336
  20.7 92.1 %all-gather.5.cloned.1.call-start = ((), (), s32[]{:S(2)}) async-start(), calls=%async_computation.7 | async-start | bytes 4423680 | tf_op jit(solution)/shard_map/all_gather | solution.py:341
  20.8 1.0 copy-start.27
  21.8 36.4 %copy-start.4 = (bf16[384,384]{1,0:T(8,128)(2,1)S(1)}, bf16[384,384]{1,0:T(8,128)(2,1)}, u32[]{:S(2)}) copy-start(bf16[384,384]{1,0:T(8,128)(2,1)} %constant.14.clone.swap) | copy-start | bytes 884740
  34.6 1.0 copy-start.13
  35.6 1.0 copy-start.26
  58.1 167.3 %reduce-scatter.3.cloned.1.call-start = ((), (), s32[]{:S(2)}) async-start(), calls=%async_computation.8 | async-start | bytes 4423680 | tf_op jit(solution)/shard_map/reduce_scatter | solution.py:363
  58.2 1.8 copy-start.32
  95.1 1.9 copy-start.36
  97.1 7.0 %copy-start.37 = (bf16[1,1280,1280]{2,1,0:T(8,128)(2,1)S(1)}, bf16[1,1280,1280]{2,1,0:T(8,128)(2,1)}, u32[]{:S(2)}) copy-start(bf16[1,1280,1280]{2,1,0:T(8,128)(2,1)} %param.18) | copy-start | bytes 9830404
  102.4 30.2 %collective-permute-start = (bf16[272,1024]{1,0:T(8,128)(2,1)S(1)}, bf16[272,1024]{1,0:T(8,128)(2,1)}, u32[]{:S(2)}, u32[]{:S(2)}) collective-permute-start(bf16[272,1024]{1,0:T(8,128)(2,1)S(1)} %shard_map.158.own), channel_id=1, source_target_pairs={{0,1},{1,2},{2,3},{3,0},{4,5},{5,6},{6,7},{7,4},{8,9},{9,10},{10,1... | collective-permute-start | bytes 1671176 | tf_op jit(solution)/shard_map/ppermute | solution.py:331
  112.7 1.4 copy-start.15
  114.2 1.4 copy-start.16
  115.6 2.1 copy-start.31
  117.7 3.2 %copy-start.34 = (f32[1536,1280]{1,0:T(8,128)S(1)}, f32[1536,1280]{1,0:T(8,128)}, u32[]{:S(2)}) copy-start(f32[1536,1280]{1,0:T(8,128)} %fusion.1.partial) | copy-start | bytes 23592964
  128.7 1.9 copy-start.3
  130.6 1.9 copy-start.35
  139.8 1.4 copy-start.2
  141.1 57.6 %all-to-all-start.2 = ((bf16[32,48,640]{2,1,0:T(8,128)(2,1)}), bf16[32,48,640]{2,1,0:T(8,128)(2,1)}, u32[]{:S(2)}, u32[]{:S(2)}) async-start(bf16[32,48,640]{2,1,0:T(8,128)(2,1)} %bitcast.24), calls=%async_computation.2 | async-start | bytes 3932160 | tf_op jit(solution)/shard_map/all_to_all | solution.py:370
  151.6 123.5 %reduce-scatter.5.cloned.1.call-start = ((), (), s32[]{:S(2)}) async-start(), calls=%async_computation.9 | async-start | bytes 2949120 | tf_op jit(solution)/shard_map/reduce_scatter | solution.py:380
  151.6 42.2 %collective-permute-start.1 = (bf16[272,1024]{1,0:T(8,128)(2,1)S(1)}, bf16[272,1024]{1,0:T(8,128)(2,1)S(1)}, u32[]{:S(2)}, u32[]{:S(2)}) collective-permute-start(bf16[272,1024]{1,0:T(8,128)(2,1)S(1)} %shard_map.158.own), channel_id=1, source_target_pairs={{0,2},{1,3},{2,0},{3,1},{4,6},{5,7},{6,4},{7,5},{8,10},{9,11},{10,... | collective-permute-start | bytes 1671176 | tf_op jit(solution)/shard_map/ppermute | solution.py:331
  156.7 41.2 %collective-permute-start.2 = (bf16[272,1024]{1,0:T(8,128)(2,1)S(1)}, bf16[272,1024]{1,0:T(8,128)(2,1)S(1)}, u32[]{:S(2)}, u32[]{:S(2)}) collective-permute-start(bf16[272,1024]{1,0:T(8,128)(2,1)S(1)} %shard_map.158.own), channel_id=1, source_target_pairs={{0,3},{1,0},{2,1},{3,2},{4,7},{5,4},{6,5},{7,6},{8,11},{9,8},{10,9... | collective-permute-start | bytes 1671176 | tf_op jit(solution)/shard_map/ppermute | solution.py:331
  193.8 0.9 copy-start.5
  229.1 1.5 copy-start.1
  230.6 1.0 copy-start.25
  230.6 12.7 %copy-start.39 = (f32[256]{0:T(256)S(1)}, f32[256]{0:T(256)}, u32[]{:S(2)}) copy-start(f32[256]{0:T(256)} %param.15) | copy-start | bytes 3076
  231.6 1.0 copy-start.23
  235.8 19.5 %all-to-all-start.3 = ((bf16[32,12,640]{2,1,0:T(8,128)(2,1)}), bf16[32,12,640]{2,1,0:T(8,128)(2,1)}, u32[]{:S(2)}, u32[]{:S(2)}) async-start(bf16[32,12,640]{2,1,0:T(8,128)(2,1)} %reshape.69), calls=%async_computation.4 | async-start | bytes 1310720 | tf_op jit(solution)/shard_map/all_to_all | solution.py:382
  243.3 31.7 %copy-start.29 = (f32[256,1]{1,0:T(8,128)S(1)}, f32[256,1]{1,0:T(8,128)}, u32[]{:S(2)}) copy-start(f32[256,1]{1,0:T(8,128)} %copy-done.28) | copy-start | bytes 3076
  243.4 1.1 copy-start.6
  244.5 1.1 copy-start.9
  248.6 0.8 copy-start.19
  249.4 0.8 copy-start.21
  275.0 9.5 %copy-start.7 = (bf16[272,1024]{1,0:T(8,128)(2,1)S(1)}, bf16[272,1024]{1,0:T(8,128)(2,1)}, u32[]{:S(2)}) copy-start(bf16[272,1024]{1,0:T(8,128)(2,1)} %copy-done.5) | copy-start | bytes 1671172
  275.0 9.5 %copy-start.10 = (bf16[272,1024]{1,0:T(8,128)(2,1)S(1)}, bf16[272,1024]{1,0:T(8,128)(2,1)}, u32[]{:S(2)}) copy-start(bf16[272,1024]{1,0:T(8,128)(2,1)} %copy-done.8) | copy-start | bytes 1671172
  275.0 1.1 copy-start.12
  276.1 1.1 copy-start.18
  277.2 1.0 copy-start.24
  278.2 6.3 %copy-start.22 = (f32[128,1024]{1,0:T(8,128)S(1)}, f32[128,1024]{1,0:T(8,128)}, u32[]{:S(2)}) copy-start(f32[128,1024]{1,0:T(8,128)} %copy-done.21) | copy-start | bytes 1572868
  278.2 9.2 %copy-start.20 = (f32[128,1024]{1,0:T(8,128)S(1)}, f32[128,1024]{1,0:T(8,128)}, u32[]{:S(2)}) copy-start(f32[128,1024]{1,0:T(8,128)} %copy-done.19) | copy-start | bytes 1572868
  279.8 7.6 %collective-permute-start.3 = (bf16[1,1024]{1,0:T(2,128)(2,1)S(1)}, bf16[1,1024]{1,0:T(2,128)(2,1)S(1)}, u32[]{:S(2)}, u32[]{:S(2)}) collective-permute-start(bf16[1,1024]{1,0:T(2,128)(2,1)S(1)} %get-tuple-element.62.own_image.i0), channel_id=1, source_target_pairs={{0,1},{1,2},{2,3},{3,0},{4,5},{5,6},{6,7},{7,4},{8,9},{9,10},{10,1... | collective-permute-start | bytes 6152 | tf_op jit(solution)/shard_map/ppermute | solution.py:331
  280.1 7.2 %collective-permute-start.4 = (bf16[1,1024]{1,0:T(2,128)(2,1)S(1)}, bf16[1,1024]{1,0:T(2,128)(2,1)S(1)}, u32[]{:S(2)}, u32[]{:S(2)}) collective-permute-start(bf16[1,1024]{1,0:T(2,128)(2,1)S(1)} %get-tuple-element.62.own_image.i0), channel_id=1, source_target_pairs={{0,2},{1,3},{2,0},{3,1},{4,6},{5,7},{6,4},{7,5},{8,10},{9,11},{10,... | collective-permute-start | bytes 6152 | tf_op jit(solution)/shard_map/ppermute | solution.py:331
  282.8 4.6 %collective-permute-start.5 = (bf16[1,1024]{1,0:T(2,128)(2,1)S(1)}, bf16[1,1024]{1,0:T(2,128)(2,1)S(1)}, u32[]{:S(2)}, u32[]{:S(2)}) collective-permute-start(bf16[1,1024]{1,0:T(2,128)(2,1)S(1)} %get-tuple-element.62.own_image.i0), channel_id=1, source_target_pairs={{0,3},{1,0},{2,1},{3,2},{4,7},{5,4},{6,5},{7,6},{8,11},{9,8},{10,9... | collective-permute-start | bytes 6152 | tf_op jit(solution)/shard_map/ppermute | solution.py:331
  (5 other events, 3.7 us)
Sparse Core Ops, SparseCore 0:
  12.2 45.8 all-gather.2
  60.5 52.2 all-gather.4
  132.7 92.6 reduce-scatter.2
  230.7 44.2 reduce-scatter.4

commit v3 on v2

--- a/solution.py
+++ b/solution.py
@@ -35,7 +35,7 @@
 BF16 = jnp.bfloat16
 
 
-def call(kernel, out_shape, scratch=(), aliases=None, flops=0, vmem=24):
+def call(kernel, out_shape, scratch=(), aliases=None, flops=0, vmem=60):
     return pl.pallas_call(
         kernel,
         out_shape=out_shape,
@@ -100,7 +100,7 @@
 
 def route_kernel(tokens, routes, quota, packed, outgoing, position):
     half = packed.shape[1]
-    ids = routes[...]
+    ids = as_column(routes[...].astype(F32)).astype(jnp.int32)
     hit = ids == iota((TOK, EXPERTS), 1)
     onehot = jnp.where(hit, 1.0, 0.0)
     before = dot(
@@ -113,7 +113,8 @@
     far = jnp.where(ids >= PLANE, 1, 0)
     place = (ids - far * PLANE) * (2 * SLOTS) + far * SLOTS
     column = jnp.where(kept, place.astype(F32) + slot, -1.0)
-    position[...] = column
+    placing = as_row(column)
+    position[...] = placing
     id_row = as_row(ids.astype(F32))
     slot_row = as_row(jnp.where(kept, slot, 64.0))
     line = iota((16, TOK), 0)
@@ -122,8 +123,9 @@
     packed[TOK:ROWS, 0:TOK] = jnp.where(
         line == 0, id_row, jnp.where(line == 1, slot_row, 0.0)
     ).astype(BF16)
-    place = as_row(column).astype(jnp.int32)
-    onto = jnp.where(iota((EXPERTS * SLOTS, TOK), 0) == place, 1.0, 0.0).astype(BF16)
+    onto = jnp.where(
+        iota((EXPERTS * SLOTS, TOK), 0) == placing.astype(jnp.int32), 1.0, 0.0
+    ).astype(BF16)
     outgoing[...] = dot(onto, tokens[:, half:]).astype(BF16)
 
 
@@ -179,7 +181,7 @@
 
 
 def expert_right(side, rows, partial, first, second):
-    half, inner = first.shape
+    half, inner = rows.shape[3], first.shape[1]
     spec = pl.BlockSpec
     return pl.pallas_call(
         expert_kernel,
@@ -193,8 +195,8 @@
             in_specs=[
                 spec((2, 1, BLOCK, half), lambda i, side: (i, side[0], 0, 0)),
                 spec((2 * BLOCK, inner), lambda i, side: (i, 0)),
-                spec((half, inner), lambda i, side: (0, 0)),
-                spec((half, inner), lambda i, side: (0, 0)),
+                spec((half, inner), lambda i, side: (1, 0)),
+                spec((half, inner), lambda i, side: (1, 0)),
             ],
             out_specs=[
                 spec((2 * BLOCK, inner), lambda i, side: (i, 0)),
@@ -204,7 +206,7 @@
         cost_estimate=pl.CostEstimate(
             flops=4 * RING * BLOCK * half * inner, bytes_accessed=20 << 20, transcendentals=0
         ),
-        compiler_params=pltpu.CompilerParams(vmem_limit_bytes=32 << 20),
+        compiler_params=pltpu.CompilerParams(vmem_limit_bytes=60 << 20),
     )(side, rows, partial, first, second)
 
 
@@ -222,21 +224,76 @@
         ).astype(BF16)
 
 
-def layer_kernel(tokens, position, gate, returned, given, head, layer_out, own_image):
-    half = given.shape[1]
-    onto = jnp.where(
-        iota((TOK, EXPERTS * SLOTS), 1) == position[...].astype(jnp.int32), 1.0, 0.0
-    ).astype(BF16)
-    left = tokens[:, :half].astype(F32) + gate[...] * given[...].astype(F32)
-    right = tokens[:, half:].astype(F32) + gate[...] * dot(onto, returned[...])
-    layer_out[:, :half] = left.astype(BF16)
-    layer_out[:, half:] = right.astype(BF16)
-    own_left = (jnp.sum(left, axis=0, keepdims=True) / PATCHES).astype(BF16)
-    own_right = (jnp.sum(right, axis=0, keepdims=True) / PATCHES).astype(BF16)
-    own_left = jnp.broadcast_to(own_left.astype(F32), (16, half)).astype(BF16)
-    own_right = jnp.broadcast_to(own_right.astype(F32), (16, half)).astype(BF16)
-    image = dot(own_left, head[:half, :]) + dot(own_right, head[half:, :])
-    own_image[...] = normalize_rows(image)[0:1].astype(BF16)
+def own_rows(layer):
+    own = (jnp.sum(layer, axis=0, keepdims=True) / PATCHES).astype(BF16)
+    return jnp.broadcast_to(own.astype(F32), (16, layer.shape[1])).astype(BF16)
+
+
+def right_kernel(tokens, position, gate, returned, head, layer_out, image):
+    column = as_column(position[...]).astype(jnp.int32)
+    onto = jnp.where(iota((TOK, EXPERTS * SLOTS), 1) == column, 1.0, 0.0).astype(BF16)
+    weight = as_column(gate[...])
+    layer = tokens[...].astype(F32) + weight * dot(onto, returned[...])
+    layer_out[...] = layer.astype(BF16)
+    image[...] = dot(own_rows(layer), head[...])
+
+
+def left_kernel(tokens, gate, given, head, partial, label, other_half, layer_out, own_image):
+    layer = tokens[...].astype(F32) + as_column(gate[...]) * given[...].astype(F32)
+    layer_out[...] = layer.astype(BF16)
+    image = normalize_rows(partial[...] + dot(own_rows(layer), head[...]))[0:1]
+    embed = image.shape[1]
+    own_image[:, :embed] = image.astype(BF16)
+    own_image[:, embed:] = label[:, 0:128].astype(F32).astype(BF16)
+
+
+def whole(shape):
+    return pl.BlockSpec(shape, lambda i: (0,) * len(shape))
+
+
+def part(shape, at):
+    return pl.BlockSpec(shape, lambda i: at)
+
+
+def layer_right(tokens, position, gate, returned, head):
+    half, embed = returned.shape[1], head.shape[1]
+    return pl.pallas_call(
+        right_kernel,
+        grid=(1,),
+        out_shape=(struct(tokens.shape, BF16), struct((16, embed), F32)),
+        in_specs=[
+            part((TOK, half), (0, 1)),
+            whole((1, TOK)),
+            whole((1, TOK)),
+            whole(returned.shape),
+            part((half, embed), (1, 0)),
+        ],
+        out_specs=(part((TOK, half), (0, 1)), whole((16, embed))),
+        cost_estimate=pl.CostEstimate(flops=1 << 28, bytes_accessed=4 << 20, transcendentals=0),
+        compiler_params=pltpu.CompilerParams(vmem_limit_bytes=60 << 20),
+    )(tokens, position, gate, returned, head)
+
+
+def layer_left(tokens, gate, given, head, partial, label, right_done):
+    half, embed = given.shape[1], head.shape[1]
+    return pl.pallas_call(
+        left_kernel,
+        grid=(1,),
+        out_shape=(struct(tokens.shape, BF16), struct((1, embed + 128), BF16)),
+        in_specs=[
+            part((TOK, half), (0, 0)),
+            whole((1, TOK)),
+            whole(given.shape),
+            part((half, embed), (0, 0)),
+            whole((16, embed)),
+            whole(label.shape),
+            pl.BlockSpec(memory_space=pl.ANY),
+        ],
+        out_specs=(part((TOK, half), (0, 0)), whole((1, embed + 128))),
+        input_output_aliases={6: 0},
+        cost_estimate=pl.CostEstimate(flops=1 << 28, bytes_accessed=4 << 20, transcendentals=0),
+        compiler_params=pltpu.CompilerParams(vmem_limit_bytes=24 << 20),
+    )(tokens, gate, given, head, partial, label, right_done)
 
 
 def pack_kernel(pooled, head, text_embed, labels, packed):
@@ -273,10 +330,11 @@
 
 
 def own_row_kernel(own_image, own, s1, s2, s3, loss, image_acc, loss_out, image_out):
-    row = jnp.broadcast_to(own_image[...].astype(F32), (16, own_image.shape[1])).astype(BF16)
+    embed = own.shape[1]
+    row = jnp.broadcast_to(own_image[:, :embed].astype(F32), (16, embed)).astype(BF16)
     label = label_row(own)[0:1, 0:1]
     total = jnp.zeros((16, 1), F32)
-    grad = jnp.zeros((16, own_image.shape[1]), F32)
+    grad = jnp.zeros((16, embed), F32)
     for shard in (own, s1, s2, s3):
         their_text = shard[0:PAIRS, :]
         sign = sign_of(label, label_row(shard))
@@ -288,16 +346,16 @@
     image_out[0:1, :] = grad[0:1]
 
 
-def own_text_kernel(i0, i1, i2, i3, own, s1, s2, s3, text_acc, out):
-    line = iota((16, i0.shape[1]), 0)
-    images = jnp.zeros((16, i0.shape[1]), F32)
+def own_text_kernel(i0, i1, i2, i3, own, text_acc, out):
+    embed = own.shape[1]
+    line = iota((16, embed), 0)
+    place = iota((1, 16), 1)
+    images = jnp.zeros((16, embed), F32)
+    labels = jnp.full((1, 16), -1.0, F32)
     for k, row in enumerate((i0, i1, i2, i3)):
-        images = jnp.where(line == k, row[...].astype(F32), images)
+        images = jnp.where(line == k, row[:, :embed].astype(F32), images)
+        labels = jnp.where(place == k, row[:, embed:].astype(F32)[:, 0:1], labels)
     images = images.astype(BF16)
-    place = iota((1, 16), 1)
-    labels = jnp.full((1, 16), -1.0, F32)
-    for k, shard in enumerate((own, s1, s2, s3)):
-        labels = jnp.where(place == k, label_row(shard)[0:1, 0:1], labels)
     sign = sign_of(as_column(label_row(own)), labels)
     logit = scale_logit * dot_t(own[0:PAIRS, :], images) + shift_logit
     out[...] = text_acc[...] + dot(coefficients(logit, sign), images)
@@ -319,10 +377,10 @@
         (
             struct((ROWS, half), BF16),
             struct((EXPERTS * SLOTS, half), BF16),
-            struct((TOK, 1), F32),
+            struct((1, TOK), F32),
         ),
         flops=1 << 28,
-    )(tokens, routes, expert_quota.reshape(1, EXPERTS))
+    )(tokens, routes.reshape(1, TOK), expert_quota.reshape(1, EXPERTS))
 
     pooled = jnp.concatenate([jnp.zeros((1, width), BF16), other_pooled], axis=0)
     own_pairs = call(pack_kernel, struct((SHARD, embed), BF16), flops=1 << 28)(
@@ -331,13 +389,22 @@
     shift = lambda value, step: lax.ppermute(
         value, "zl", [(i, (i + step) % LOOP) for i in range(LOOP)]
     )
+
+    packed, own_pairs = lax.optimization_barrier((packed, own_pairs))
+
+    def onward(right_going, left_going, hops):
+        return (
+            lax.ppermute(right_going, "zl", [(i, i + 1) for i in range(hops, LOOP - 1)]),
+            lax.ppermute(left_going, "zl", [(i, i - 1) for i in range(1, LOOP - hops)]),
+        )
 
     around = lax.all_gather(packed, Z, axis=0, tiled=True)
     received = lax.all_to_all(
         outgoing.reshape(PLANE, 2 * SLOTS, half), FLAT, split_axis=0, concat_axis=0, tiled=True
     ).reshape(2 * BLOCK, half)
     received = call(turn_kernel, struct((2 * BLOCK, half), BF16), flops=1 << 28)(received, apart)
-    received, around, own_pairs = lax.optimization_barrier((received, around, own_pairs))
+    r1, l1 = onward(own_pairs, own_pairs, 0)
+    received, around, r1, l1 = lax.optimization_barrier((received, around, r1, l1))
     right = lax.all_gather(received, Z, axis=0, tiled=True)
 
     chosen, target = call(
@@ -354,12 +421,13 @@
     first = w_in[0]
     second = w_out[0]
     partial = dot(left, first[:half])
-    partial, own_pairs = lax.optimization_barrier((partial, own_pairs))
-    pairs = [own_pairs] + [shift(own_pairs, step) for step in range(1, LOOP)]
+    partial, r1, l1 = lax.optimization_barrier((partial, r1, l1))
+    r2, l2 = onward(r1, l1, 1)
     hidden, term_right = expert_right(
-        side.reshape(1), right.reshape(RING, 2, BLOCK, half), partial, first[half:], second[half:]
-    )
-    hidden, term_right, pairs[1] = lax.optimization_barrier((hidden, term_right, pairs[1]))
+        side.reshape(1), right.reshape(RING, 2, BLOCK, half), partial, first, second
+    )
+    hidden, term_right, r2, l2 = lax.optimization_barrier((hidden, term_right, r2, l2))
+    r3, l3 = onward(r2, l2, 2)
     result = lax.psum_scatter(
         term_right.reshape(2 * RING * BLOCK, half), Z, scatter_dimension=0, tiled=True
     )
@@ -367,16 +435,17 @@
     leaving = call(unspread_kernel, struct((RING * BLOCK, half), BF16), flops=1 << 30)(
         term_left, swap
     )
+    leaving, r3, l3 = lax.optimization_barrier((leaving, r3, l3))
     back = lax.all_to_all(
         leaving.reshape(PLANE, PIECE, half), FLAT, split_axis=0, concat_axis=0, tiled=True
     ).reshape(RING * BLOCK, half)
-    back, result, *pairs = lax.optimization_barrier((back, result, *pairs))
     by_token = call(
         scatter_kernel,
         struct((RING * TOK, half), BF16),
         scratch=[pltpu.VMEM((RING * BLOCK, half), BF16)],
         flops=1 << 30,
     )(back, swap, target)
+    by_token, result = lax.optimization_barrier((by_token, result))
     given = lax.psum_scatter(by_token, Z, scatter_dimension=0, tiled=True)
     result = call(turn_kernel, struct((2 * BLOCK, half), BF16), flops=1 << 28)(result, together)
     returned = lax.all_to_all(
@@ -385,19 +454,27 @@
 
     square = struct((PAIRS, embed), F32)
     line = struct((1, PAIRS), F32)
+    at = lax.axis_index("zl")
+    pairs = [
+        own_pairs,
+        jnp.where(at == 0, l3, r1),
+        jnp.where(at <= 1, l2, r2),
+        jnp.where(at == 3, r3, l1),
+    ]
     loss, image_acc, text_acc = call(score_kernel, (line, square, square), flops=1 << 30)(*pairs)
-    loss, image_acc, text_acc, returned = lax.optimization_barrier(
-        (loss, image_acc, text_acc, returned)
-    )
-
-    layer_out, own_image = call(
-        layer_kernel, (struct((TOK, width), BF16), struct((1, embed), BF16)), flops=1 << 28
-    )(tokens, position, gate_prob.reshape(TOK, 1), returned, given, head)
+    gate = gate_prob.reshape(1, TOK)
+    layer_out, image_right = layer_right(tokens, position, gate, returned, head)
+    loss, image_acc, text_acc, layer_out, image_right, given = lax.optimization_barrier(
+        (loss, image_acc, text_acc, layer_out, image_right, given)
+    )
+    layer_out, own_image = layer_left(
+        tokens, gate, given, head, image_right, labels.reshape(1, PAIRS), layer_out
+    )
     own_images = [own_image] + [shift(own_image, step) for step in range(1, LOOP)]
-    loss, image_acc = call(own_row_kernel, (line, square), flops=1 << 26)(
+    loss, image_acc = call(own_row_kernel, (line, square), flops=1 << 26, vmem=24)(
         own_image, *pairs, loss, image_acc
     )
-    text_acc = call(own_text_kernel, square, flops=1 << 26)(*own_images, *pairs, text_acc)
+    text_acc = call(own_text_kernel, square, flops=1 << 26, vmem=24)(*own_images, own_pairs, text_acc)
     return (layer_out, loss.reshape(PAIRS), image_acc, text_acc)
 
 

time: 297 us -> 257 us (0.87)
  waiting for transfers between devices: 127 us -> 57.5 us
  blocking collectives: 33.2 us -> 85.1 us
  local copies, waits for them, and re-layouts: 44.6 us -> 9.62 us
  Pallas kernels: 28.7 us -> 52.1 us
  starting transfers between devices: 37.5 us -> 19.6 us
  matrix products: 11.2 us -> 15.6 us
    all_to_all x0 -> x2, blocking collectives: none -> 51.7 us  [the longest x1 32.4 us: shards(): lax.all_to_all(leaving.reshape(PLANE, PIECE, half), FLAT, split_axis=0, c...]
    ppermute x6 -> x3, waiting for transfers between devices: 40 us -> 0.67 us  [shards(): lax.ppermute(value, 'zl', [(i, (i + step) % LOOP) for i in range(LOOP)])]
    unnamed x81 -> x28, local copies, waits for them, and re-layouts: 35.7 us -> 2.94 us
    reduce_scatter x1, waiting for transfers between devices: 26.7 us -> 0.01 us  [shards(): lax.psum_scatter(term_right.reshape(2 * RING * BLOCK, half), Z, scatter_d...]
    all_to_all x2 -> x0, starting transfers between devices: 18.1 us -> none  [the longest x1 10.4 us: shards(): lax.all_to_all(leaving.reshape(PLANE, PIECE, half), FLAT, split_axis=0, c...]
    ppermute x0 -> x6, waiting for transfers between devices: none -> 17.4 us  [the longest x3 17.3 us: onward(): lax.ppermute(left_going, 'zl', [(i, i - 1) for i in range(1, LOOP - hops)])]
    all_to_all x2 -> x0, waiting for transfers between devices: 10.2 us -> none  [the longest x1 10.2 us: shards(): lax.all_to_all(outgoing.reshape(PLANE, 2 * SLOTS, half), FLAT, split_axis...]
    ppermute x0 -> x6, starting transfers between devices: none -> 9.3 us  [the longest x3 5.24 us: onward(): lax.ppermute(right_going, 'zl', [(i, i + 1) for i in range(hops, LOOP - 1)])]
  transfers between devices with their start and end apart: 13 -> 14, of which waited for: 8 -> 7; matrix products, arithmetic and copies ran while one was open for 7% -> 9% of each run, Pallas kernels for 7% -> 17%
where the time goes in v3:
time: 257 us; the launch traced here: 255 us
  blocking collectives  85.1 us (33%)
  waiting for transfers between devices  57.5 us (22%)
  Pallas kernels  52.1 us (20%)
  starting transfers between devices  19.6 us (8%)
  matrix products  15.6 us (6%)
  between operations  13.9 us (5%)
  local copies, waits for them, and re-layouts  9.62 us (4%)
    all_to_all x1, blocking collectives, shards(): lax.all_to_all(chosen.reshape(PLANE, PIECE, half), FLAT, split_axis=0, co...  33.4 us
    all_to_all x1, blocking collectives, shards(): lax.all_to_all(leaving.reshape(PLANE, PIECE, half), FLAT, split_axis=0, c...  32.4 us
    all_gather x1, waiting for transfers between devices, shards(): around = lax.all_gather(packed, Z, axis=0, tiled=True)  22.5 us
    all_to_all x1, blocking collectives, shards(): lax.all_to_all(outgoing.reshape(PLANE, 2 * SLOTS, half), FLAT, split_axis...  19.3 us
    ppermute x3, waiting for transfers between devices, onward(): lax.ppermute(left_going, 'zl', [(i, i - 1) for i in range(1, LOOP - hops)])  17.3 us
    pallas_call x1, Pallas kernels, expert_right(): pl.pallas_call(expert_kernel, out_shape=(struct((RING * BLOCK, inner), BF...  11.4 us
    reduce_scatter x1, waiting for transfers between devices, shards(): given = lax.psum_scatter(by_token, Z, scatter_dimension=0, tiled=True)  10.9 us
    dot_general x1, matrix products, dot(): return jnp.dot(a, b, preferred_element_type=F32)  8.38 us
  transfers between devices with their start and end apart: 14, of which 7 were waited for; matrix products, arithmetic and copies ran while one was open for 9% of the time, Pallas kernels for 17%

profile of v3, /device:TPU:2, one launch (start us, length us, event | category | flops | bytes accessed | tf_op | source)
XLA Modules:
  0.0 255.4 jit_solution(12054455040110789191)
XLA Ops:
  7.2 1.8 concatenate.3.pooled
  9.0 2.6 %shard_map.156 = (bf16[272,640]{1,0:T(8,128)(2,1)}, bf16[384,640]{1,0:T(8,128)(2,1)}, f32[1,256]{1,0:T(1,128)}) custom-call(bf16[256,1280]{1,0:T(8,128)(2,1)} %tokens.5, s32[1,256]{1,0:T(1,128)} %bitcast.35, s32[1,64]{1,0:T(1,128)} %bitcast.36), custom_call_target="tpu_custom_call" | custom-call | flops 268435456 | bytes 4194304 | tf_op jit(solution)/shard_map/pallas_call | solution.py:375
  11.6 3.3 %shard_map.157.own = bf16[272,1024]{1,0:T(8,128)(2,1)} custom-call(bf16[128,1280]{1,0:T(8,128)(2,1)} %concatenate.3.pooled, bf16[1280,1024]{1,0:T(8,128)(2,1)} %head.5, bf16[128,1024]{1,0:T(8,128)(2,1)} %text_embed.1, s32[1,128]{1,0:T(1,128)} %bitcast.25), custom_call_target="tpu_custom_call" | custom-call | flops 268435456 | bytes 4194304 | tf_op jit(solution)/shard_map/pallas_call | solution.py:386
  15.0 0.0 all-gather.5.cloned.1.call-start
  15.0 3.9 %collective-permute-start = (bf16[272,1024]{1,0:T(8,128)(2,1)}, bf16[272,1024]{1,0:T(8,128)(2,1)S(1)}, u32[]{:S(2)}, u32[]{:S(2)}) collective-permute-start(bf16[272,1024]{1,0:T(8,128)(2,1)} %shard_map.157.own), channel_id=1, source_target_pairs={{0,1},{1,2},{2,3},{4,5},{5,6},{6,7},{8,9},{9,10},{10,11},{12,13},{... | collective-permute-start | bytes 1671176 | tf_op jit(solution)/shard_map/ppermute | solution.py:397
  18.9 1.3 collective-permute-start.1
  20.2 0.1 reshape.63
  20.3 19.3 %all_to_all.20 = bf16[32,12,640]{2,1,0:T(8,128)(2,1)S(1)} all-to-all(bf16[32,12,640]{2,1,0:T(8,128)(2,1)S(1)} %reshape.63), channel_id=1, replica_groups=mesh['zh'=2,'y'=4,'x'=4,'c'=2,'zl'=4] {'y','x','c'}, dimensions={0} | all-to-all | bytes 983040 | tf_op jit(solution)/shard_map/all_to_all | solution.py:402
  39.7 0.9 reshape.64.rows
  40.5 2.3 shard_map.158
  42.9 22.5 %all-gather.3.cloned.1.call-done.gathered = bf16[2176,640]{1,0:T(8,128)(2,1)} async-done(((bf16[272,640]{1,0:T(8,128)(2,1)}), bf16[2176,640]{1,0:T(8,128)(2,1)}) %all-gather.3.cloned.1.call-update) | async-done | bytes 2785296 | tf_op jit(solution)/shard_map/all_gather | solution.py:401
  65.5 5.0 %shard_map.159 = (bf16[1536,640]{1,0:T(8,128)(2,1)}, f32[8,256]{1,0:T(8,128)}) custom-call(bf16[2176,640]{1,0:T(8,128)(2,1)} %all-gather.3.cloned.1.call-done.gathered, s32[1,1]{1,0:T(1,128)} %bitcast.6.side, bf16[384,384]{1,0:T(8,128)(2,1)} %constant.24.clone.swap), custom_call_target="tpu_custom_call" | custom-call | flops 1073741824 | bytes 4194304 | tf_op jit(solution)/shard_map/pallas_call | solution.py:410
  70.5 33.4 %all_to_all.21 = bf16[32,48,640]{2,1,0:T(8,128)(2,1)} all-to-all(bf16[32,48,640]{2,1,0:T(8,128)(2,1)} %bitcast.31), channel_id=1, replica_groups=mesh['zh'=2,'y'=4,'x'=4,'c'=2,'zl'=4] {'y','x','c'}, dimensions={0} | all-to-all | bytes 3932160 | tf_op jit(solution)/shard_map/all_to_all | solution.py:416
  103.9 4.2 %shard_map.160 = bf16[1536,640]{1,0:T(8,128)(2,1)} custom-call(bf16[1536,640]{1,0:T(8,128)(2,1)} %bitcast.29, bf16[384,384]{1,0:T(8,128)(2,1)} %constant.24.clone.swap), custom_call_target="tpu_custom_call" | custom-call | flops 1073741824 | bytes 4194304 | tf_op jit(solution)/shard_map/pallas_call | solution.py:419
  108.1 8.4 %fusion.1.partial = f32[1536,1280]{1,0:T(8,128)} fusion(bf16[1536,640]{1,0:T(8,128)(2,1)} %shard_map.160, bf16[1,1280,1280]{2,1,0:T(8,128)(2,1)} %param.17), kind=kOutput, calls=%fused_computation.2 | convolution fusion | flops 2516582400 | bytes 11468800 | tf_op jit(solution)/shard_map/dot_general | solution.py:58
  116.5 0.7 collective-permute-start.2
  117.2 1.3 collective-permute-start.3
  118.5 0.3 all-gather.5.cloned.1.call-done
  118.8 11.4 %shard_map.161 = (bf16[1536,1280]{1,0:T(8,128)(2,1)}, bf16[8,2,192,640]{3,2,1,0:T(8,128)(2,1)}) custom-call(s32[1]{0:T(128)} %bitcast.4.side, bf16[8,2,192,640]{3,2,1,0:T(8,128)(2,1)} %bitcast.32, f32[1536,1280]{1,0:T(8,128)} %fusion.1.partial, bf16[1280,1280]{1,0:T(8,128)(2,1)} %bitcast.33, bf16[1280,1280]{1,0:T(8,128)(2,1)} %bitcast.34), custom_call_target="tpu_custom_call" | custom-call | flops 5033164800 | bytes 20971520 | tf_op jit(solution)/shard_map/pallas_call | solution.py:186
  130.3 5.3 %collective-permute-done.3 = bf16[272,1024]{1,0:T(8,128)(2,1)S(1)} collective-permute-done((bf16[272,1024]{1,0:T(8,128)(2,1)S(1)}, bf16[272,1024]{1,0:T(8,128)(2,1)S(1)}, u32[]{:S(2)}, u32[]{:S(2)}) %collective-permute-start.3) | collective-permute-done | bytes 557088 | tf_op jit(solution)/shard_map/ppermute | solution.py:398
  135.6 0.0 reduce-scatter.5.cloned.1.call-start
  135.7 0.7 collective-permute-start.4
  136.4 1.5 collective-permute-start.5
  137.9 7.2 %convolution_convert_fusion.rows = bf16[1536,640]{1,0:T(8,128)(2,1)} fusion(bf16[1536,1280]{1,0:T(8,128)(2,1)} %get-tuple-element.58, bf16[1,1280,1280]{2,1,0:T(8,128)(2,1)} %param.18), kind=kOutput, calls=%fused_computation | convolution fusion | flops 2517565440 | bytes 7536640 | tf_op jit(solution)/shard_map/dot_general | solution.py:62
  145.1 4.1 %shard_map.162 = bf16[1536,640]{1,0:T(8,128)(2,1)} custom-call(bf16[1536,640]{1,0:T(8,128)(2,1)} %convolution_convert_fusion.rows, bf16[384,384]{1,0:T(8,128)(2,1)} %constant.24.clone.swap), custom_call_target="tpu_custom_call" | custom-call | flops 1073741824 | bytes 4194304 | tf_op jit(solution)/shard_map/pallas_call | solution.py:435
  149.2 12.0 %collective-permute-done.5 = bf16[272,1024]{1,0:T(8,128)(2,1)S(1)} collective-permute-done((bf16[272,1024]{1,0:T(8,128)(2,1)S(1)}, bf16[272,1024]{1,0:T(8,128)(2,1)S(1)}, u32[]{:S(2)}, u32[]{:S(2)}) %collective-permute-start.5) | collective-permute-done | bytes 557088 | tf_op jit(solution)/shard_map/ppermute | solution.py:398
  161.2 32.4 %all_to_all.22 = bf16[32,48,640]{2,1,0:T(8,128)(2,1)} all-to-all(bf16[32,48,640]{2,1,0:T(8,128)(2,1)} %bitcast.27), channel_id=1, replica_groups=mesh['zh'=2,'y'=4,'x'=4,'c'=2,'zl'=4] {'y','x','c'}, dimensions={0} | all-to-all | bytes 3932160 | tf_op jit(solution)/shard_map/all_to_all | solution.py:439
  193.6 5.3 %shard_map.164 = bf16[2048,640]{1,0:T(8,128)(2,1)} custom-call(bf16[1536,640]{1,0:T(8,128)(2,1)} %bitcast.28, bf16[384,384]{1,0:T(8,128)(2,1)} %constant.24.clone.swap, f32[8,256]{1,0:T(8,128)} %get-tuple-element.68.target), custom_call_target="tpu_custom_call" | custom-call | flops 1073741824 | bytes 4194304 | tf_op jit(solution)/shard_map/pallas_call | solution.py:442
  198.9 2.3 shard_map.165
  201.2 2.0 reshape.72
  203.2 5.7 %all-to-all-start.3 = ((bf16[32,12,640]{2,1,0:T(8,128)(2,1)}), bf16[32,12,640]{2,1,0:T(8,128)(2,1)}, u32[]{:S(2)}, u32[]{:S(2)}) async-start(bf16[32,12,640]{2,1,0:T(8,128)(2,1)} %reshape.72), calls=%async_computation.4 | async-start | bytes 1310720 | tf_op jit(solution)/shard_map/all_to_all | solution.py:451
  208.8 0.9 broadcast_select_fusion.1.s2
  209.7 1.1 broadcast_select_fusion
  210.8 4.4 %shard_map.163 = (f32[1,128]{1,0:T(1,128)}, f32[128,1024]{1,0:T(8,128)}, f32[128,1024]{1,0:T(8,128)}) custom-call(bf16[272,1024]{1,0:T(8,128)(2,1)} %shard_map.157.own, bf16[272,1024]{1,0:T(8,128)(2,1)} %get-tuple-element.85.s1, bf16[272,1024]{1,0:T(8,128)(2,1)} %broadcast_select_fusion.1.s2, bf16[272,1024]{1,0:T(8,128)(2,1)} %get-tuple-element.84.s3), custom_call_target="tpu_custom_call" | custom-call | flops 1073741824 | bytes 4194304 | tf_op jit(solution)/shard_map/pallas_call | solution.py:464
  215.2 5.7 %all-to-all-done.3 = bf16[32,12,640]{2,1,0:T(8,128)(2,1)} async-done(((bf16[32,12,640]{2,1,0:T(8,128)(2,1)}), bf16[32,12,640]{2,1,0:T(8,128)(2,1)}, u32[]{:S(2)}, u32[]{:S(2)}) %all-to-all-start.3) | async-done | bytes 491552 | tf_op jit(solution)/shard_map/all_to_all | solution.py:451
  220.9 2.0 reshape.73.returned
  222.9 2.9 %shard_map.166 = (bf16[256,1280]{1,0:T(8,128)(2,1)}, f32[16,1024]{1,0:T(8,128)}) custom-call(bf16[256,1280]{1,0:T(8,128)(2,1)} %tokens.5, f32[1,256]{1,0:T(1,128)} %get-tuple-element.66.position, f32[1,256]{1,0:T(1,128)} %bitcast.23, bf16[384,640]{1,0:T(8,128)(2,1)} %reshape.73.returned, bf16[1280,1024]{1,0:T(8,128)(2,1)} %head.5), custom_call_target="tpu_custom_call" | custom-call | flops 268435456 | bytes 4194304 | tf_op jit(solution)/shard_map/pallas_call | solution.py:260
  225.8 10.9 %reduce-scatter.5.cloned.1.call-done.given = bf16[256,640]{1,0:T(8,128)(2,1)} async-done(((bf16[2048,640]{1,0:T(8,128)(2,1)}), bf16[256,640]{1,0:T(8,128)(2,1)}) %reduce-scatter.5.cloned.1.call-update) | async-done | bytes 327696 | tf_op jit(solution)/shard_map/reduce_scatter | solution.py:449
  236.7 1.1 copy-done.2
  237.8 1.0 copy-done.8
  238.8 0.8 copy-done.9
  239.6 1.0 shard_map.167
  240.6 0.7 collective-permute-start.6
  241.3 2.7 %collective-permute-start.7 = (bf16[1,1152]{1,0:T(2,128)(2,1)S(1)}, bf16[1,1152]{1,0:T(2,128)(2,1)S(1)}, u32[]{:S(2)}, u32[]{:S(2)}) collective-permute-start(bf16[1,1152]{1,0:T(2,128)(2,1)S(1)} %get-tuple-element.78.own_image.i0), channel_id=1, source_target_pairs={{0,2},{1,3},{2,0},{3,1},{4,6},{5,7},{6,4},{7,5},{8,10},{9,11},{10,... | collective-permute-start | bytes 6920 | tf_op jit(solution)/shard_map/ppermute | solution.py:389
  244.0 1.1 collective-permute-start.8
  245.1 1.8 shard_map.168
  246.9 0.7 collective-permute-done.8.i3
  247.6 1.3 shard_map.169
  (38 shorter events, 0.2 us)
Async XLA Ops:
  7.2 58.2 %all-gather.3.cloned.1.call-start = ((), (), s32[]{:S(2)}) async-start(), calls=%async_computation.6 | async-start | bytes 3133440 | tf_op jit(solution)/shard_map/all_gather | solution.py:401
  11.6 8.6 %copy-start.13 = (bf16[384,640]{1,0:T(8,128)(2,1)S(1)}, bf16[384,640]{1,0:T(8,128)(2,1)}, u32[]{:S(2)}) copy-start(bf16[384,640]{1,0:T(8,128)(2,1)} %get-tuple-element.46) | copy-start | bytes 1474564
  15.0 103.9 %all-gather.5.cloned.1.call-start = ((), (), s32[]{:S(2)}) async-start(), calls=%async_computation.7 | async-start | bytes 4423680 | tf_op jit(solution)/shard_map/all_gather | solution.py:408
  15.0 27.8 %collective-permute-start = (bf16[272,1024]{1,0:T(8,128)(2,1)}, bf16[272,1024]{1,0:T(8,128)(2,1)S(1)}, u32[]{:S(2)}, u32[]{:S(2)}) collective-permute-start(bf16[272,1024]{1,0:T(8,128)(2,1)} %shard_map.157.own), channel_id=1, source_target_pairs={{0,1},{1,2},{2,3},{4,5},{5,6},{6,7},{8,9},{9,10},{10,11},{12,13},{... | collective-permute-start | bytes 1671176 | tf_op jit(solution)/shard_map/ppermute | solution.py:397
  18.9 24.0 %collective-permute-start.1 = (bf16[272,1024]{1,0:T(8,128)(2,1)}, bf16[272,1024]{1,0:T(8,128)(2,1)S(1)}, u32[]{:S(2)}, u32[]{:S(2)}) collective-permute-start(bf16[272,1024]{1,0:T(8,128)(2,1)} %shard_map.157.own), channel_id=1, source_target_pairs={{1,0},{2,1},{3,2},{5,4},{6,5},{7,6},{9,8},{10,9},{11,10},{13,12},{... | collective-permute-start | bytes 1671176 | tf_op jit(solution)/shard_map/ppermute | solution.py:398
  65.4 133.4 %reduce-scatter.3.cloned.1.call-start = ((), (), s32[]{:S(2)}) async-start(), calls=%async_computation.8 | async-start | bytes 4423680 | tf_op jit(solution)/shard_map/reduce_scatter | solution.py:431
  116.5 13.7 %collective-permute-start.2 = (bf16[272,1024]{1,0:T(8,128)(2,1)S(1)}, bf16[272,1024]{1,0:T(8,128)(2,1)S(1)}, u32[]{:S(2)}, u32[]{:S(2)}) collective-permute-start(bf16[272,1024]{1,0:T(8,128)(2,1)S(1)} %collective-permute-done), channel_id=1, source_target_pairs={{1,2},{2,3},{5,6},{6,7},{9,10},{10,11},{13,14},{14,15},{17,18},{18... | collective-permute-start | bytes 1671176 | tf_op jit(solution)/shard_map/ppermute | solution.py:397
  117.2 18.4 %collective-permute-start.3 = (bf16[272,1024]{1,0:T(8,128)(2,1)S(1)}, bf16[272,1024]{1,0:T(8,128)(2,1)S(1)}, u32[]{:S(2)}, u32[]{:S(2)}) collective-permute-start(bf16[272,1024]{1,0:T(8,128)(2,1)S(1)} %collective-permute-done.1), channel_id=1, source_target_pairs={{1,0},{2,1},{5,4},{6,5},{9,8},{10,9},{13,12},{14,13},{17,16},{18,1... | collective-permute-start | bytes 1671176 | tf_op jit(solution)/shard_map/ppermute | solution.py:398
  135.6 101.1 %reduce-scatter.5.cloned.1.call-start = ((), (), s32[]{:S(2)}) async-start(), calls=%async_computation.9 | async-start | bytes 2949120 | tf_op jit(solution)/shard_map/reduce_scatter | solution.py:449
  135.7 13.5 %collective-permute-start.4 = (bf16[272,1024]{1,0:T(8,128)(2,1)S(1)}, bf16[272,1024]{1,0:T(8,128)(2,1)S(1)}, u32[]{:S(2)}, u32[]{:S(2)}) collective-permute-start(bf16[272,1024]{1,0:T(8,128)(2,1)S(1)} %collective-permute-done.2), channel_id=1, source_target_pairs={{2,3},{6,7},{10,11},{14,15},{18,19},{22,23},{26,27},{30,31},{34,35... | collective-permute-start | bytes 1671176 | tf_op jit(solution)/shard_map/ppermute | solution.py:397
  136.4 24.8 %collective-permute-start.5 = (bf16[272,1024]{1,0:T(8,128)(2,1)S(1)}, bf16[272,1024]{1,0:T(8,128)(2,1)S(1)}, u32[]{:S(2)}, u32[]{:S(2)}) collective-permute-start(bf16[272,1024]{1,0:T(8,128)(2,1)S(1)} %collective-permute-done.3), channel_id=1, source_target_pairs={{1,0},{5,4},{9,8},{13,12},{17,16},{21,20},{25,24},{29,28},{33,32},... | collective-permute-start | bytes 1671176 | tf_op jit(solution)/shard_map/ppermute | solution.py:398
  203.2 17.7 %all-to-all-start.3 = ((bf16[32,12,640]{2,1,0:T(8,128)(2,1)}), bf16[32,12,640]{2,1,0:T(8,128)(2,1)}, u32[]{:S(2)}, u32[]{:S(2)}) async-start(bf16[32,12,640]{2,1,0:T(8,128)(2,1)} %reshape.72), calls=%async_computation.4 | async-start | bytes 1310720 | tf_op jit(solution)/shard_map/all_to_all | solution.py:451
  215.2 21.5 %copy-start = (bf16[1280,1024]{1,0:T(8,128)(2,1)S(1)}, bf16[1280,1024]{1,0:T(8,128)(2,1)}, u32[]{:S(2)}) copy-start(bf16[1280,1024]{1,0:T(8,128)(2,1)} %head.5) | copy-start | bytes 7864324
  215.2 21.5 %copy-start.10 = (f32[256]{0:T(256)S(1)}, f32[256]{0:T(256)}, u32[]{:S(2)}) copy-start(f32[256]{0:T(256)} %param.15) | copy-start | bytes 3076
  215.2 21.5 %copy-start.11 = (s32[128]{0:T(128)S(1)}, s32[128]{0:T(128)}, u32[]{:S(2)}) copy-start(s32[128]{0:T(128)} %param.22) | copy-start | bytes 1540
  222.9 22.3 %copy-start.12 = (f32[1,128]{1,0:T(1,128)S(1)}, f32[1,128]{1,0:T(1,128)}, u32[]{:S(2)}) copy-start(f32[1,128]{1,0:T(1,128)} %get-tuple-element.79.loss) | copy-start | bytes 1540
  225.7 19.4 %copy-start.1 = (bf16[272,1024]{1,0:T(8,128)(2,1)S(1)}, bf16[272,1024]{1,0:T(8,128)(2,1)}, u32[]{:S(2)}) copy-start(bf16[272,1024]{1,0:T(8,128)(2,1)} %shard_map.157.own) | copy-start | bytes 1671172
  236.7 1.1 copy-start.2
  237.8 1.0 copy-start.8
  238.7 0.8 copy-start.9
  239.6 5.5 %copy-start.3 = (bf16[272,1024]{1,0:T(8,128)(2,1)S(1)}, bf16[272,1024]{1,0:T(8,128)(2,1)}, u32[]{:S(2)}) copy-start(bf16[272,1024]{1,0:T(8,128)(2,1)} %broadcast_select_fusion.1.s2) | copy-start | bytes 1671172
  239.6 5.5 %copy-start.4 = (bf16[272,1024]{1,0:T(8,128)(2,1)S(1)}, bf16[272,1024]{1,0:T(8,128)(2,1)}, u32[]{:S(2)}) copy-start(bf16[272,1024]{1,0:T(8,128)(2,1)} %get-tuple-element.84.s3) | copy-start | bytes 1671172
  239.6 5.5 %copy-start.5 = (bf16[272,1024]{1,0:T(8,128)(2,1)S(1)}, bf16[272,1024]{1,0:T(8,128)(2,1)}, u32[]{:S(2)}) copy-start(bf16[272,1024]{1,0:T(8,128)(2,1)} %get-tuple-element.85.s1) | copy-start | bytes 1671172
  239.6 5.5 %copy-start.6 = (f32[128,1024]{1,0:T(8,128)S(1)}, f32[128,1024]{1,0:T(8,128)}, u32[]{:S(2)}) copy-start(f32[128,1024]{1,0:T(8,128)} %get-tuple-element.80.image_acc) | copy-start | bytes 1572868
  239.6 8.0 %copy-start.7 = (f32[128,1024]{1,0:T(8,128)S(1)}, f32[128,1024]{1,0:T(8,128)}, u32[]{:S(2)}) copy-start(f32[128,1024]{1,0:T(8,128)} %get-tuple-element.83.text_acc) | copy-start | bytes 1572868
  240.6 6.3 %collective-permute-start.6 = (bf16[1,1152]{1,0:T(2,128)(2,1)S(1)}, bf16[1,1152]{1,0:T(2,128)(2,1)S(1)}, u32[]{:S(2)}, u32[]{:S(2)}) collective-permute-start(bf16[1,1152]{1,0:T(2,128)(2,1)S(1)} %get-tuple-element.78.own_image.i0), channel_id=1, source_target_pairs={{0,1},{1,2},{2,3},{3,0},{4,5},{5,6},{6,7},{7,4},{8,9},{9,10},{10,1... | collective-permute-start | bytes 6920 | tf_op jit(solution)/shard_map/ppermute | solution.py:389
  241.3 5.6 %collective-permute-start.7 = (bf16[1,1152]{1,0:T(2,128)(2,1)S(1)}, bf16[1,1152]{1,0:T(2,128)(2,1)S(1)}, u32[]{:S(2)}, u32[]{:S(2)}) collective-permute-start(bf16[1,1152]{1,0:T(2,128)(2,1)S(1)} %get-tuple-element.78.own_image.i0), channel_id=1, source_target_pairs={{0,2},{1,3},{2,0},{3,1},{4,6},{5,7},{6,4},{7,5},{8,10},{9,11},{10,... | collective-permute-start | bytes 6920 | tf_op jit(solution)/shard_map/ppermute | solution.py:389
  244.0 3.6 %collective-permute-start.8 = (bf16[1,1152]{1,0:T(2,128)(2,1)S(1)}, bf16[1,1152]{1,0:T(2,128)(2,1)S(1)}, u32[]{:S(2)}, u32[]{:S(2)}) collective-permute-start(bf16[1,1152]{1,0:T(2,128)(2,1)S(1)} %get-tuple-element.78.own_image.i0), channel_id=1, source_target_pairs={{0,3},{1,0},{2,1},{3,2},{4,7},{5,4},{6,5},{7,6},{8,11},{9,8},{10,9... | collective-permute-start | bytes 6920 | tf_op jit(solution)/shard_map/ppermute | solution.py:389
Sparse Core Ops, SparseCore 0:
  15.1 50.2 all-gather.2
  67.7 51.0 all-gather.4
  135.7 54.3 reduce-scatter.2
  199.0 37.6 reduce-scatter.4

commit v4 on v3

--- a/solution.py
+++ b/solution.py
@@ -292,18 +292,37 @@
         out_specs=(part((TOK, half), (0, 0)), whole((1, embed + 128))),
         input_output_aliases={6: 0},
         cost_estimate=pl.CostEstimate(flops=1 << 28, bytes_accessed=4 << 20, transcendentals=0),
-        compiler_params=pltpu.CompilerParams(vmem_limit_bytes=24 << 20),
+        compiler_params=pltpu.CompilerParams(vmem_limit_bytes=60 << 20),
     )(tokens, gate, given, head, partial, label, right_done)
 
 
 def pack_kernel(pooled, head, text_embed, labels, packed):
     packed[0:PAIRS, :] = normalize_rows(text_embed[...].astype(F32)).astype(BF16)
-    image = normalize_rows(dot(pooled[...], head[...]))
+    image = pltpu.roll(normalize_rows(dot(pooled[...], head[...])), 1, 0)
+    image = jnp.where(iota(image.shape, 0) == 0, 0.0, image)
     packed[PAIRS : 2 * PAIRS, :] = image.astype(BF16)
     packed[2 * PAIRS : SHARD, :] = jnp.zeros((16, packed.shape[1]), BF16)
     packed[2 * PAIRS : SHARD, 0:PAIRS] = jnp.where(
         iota((16, PAIRS), 0) == 0, labels[...].astype(F32), 0.0
     ).astype(BF16)
+
+
+def pack_pairs(pooled, head, text_embed, labels):
+    width, embed = head.shape
+    return pl.pallas_call(
+        pack_kernel,
+        grid=(1,),
+        out_shape=struct((SHARD, embed), BF16),
+        in_specs=[
+            whole((PAIRS, width)),
+            whole(head.shape),
+            whole(text_embed.shape),
+            whole(labels.shape),
+        ],
+        out_specs=whole((SHARD, embed)),
+        cost_estimate=pl.CostEstimate(flops=1 << 28, bytes_accessed=4 << 20, transcendentals=0),
+        compiler_params=pltpu.CompilerParams(vmem_limit_bytes=60 << 20),
+    )(pooled, head, text_embed, labels)
 
 
 def label_row(shard):
@@ -382,15 +401,12 @@
         flops=1 << 28,
     )(tokens, routes.reshape(1, TOK), expert_quota.reshape(1, EXPERTS))
 
-    pooled = jnp.concatenate([jnp.zeros((1, width), BF16), other_pooled], axis=0)
-    own_pairs = call(pack_kernel, struct((SHARD, embed), BF16), flops=1 << 28)(
-        pooled, head, text_embed, labels.reshape(1, PAIRS)
-    )
+    own_pairs = pack_pairs(other_pooled, head, text_embed, labels.reshape(1, PAIRS))
     shift = lambda value, step: lax.ppermute(
         value, "zl", [(i, (i + step) % LOOP) for i in range(LOOP)]
     )
 
-    packed, own_pairs = lax.optimization_barrier((packed, own_pairs))
+    outgoing, own_pairs = lax.optimization_barrier((outgoing, own_pairs))
 
     def onward(right_going, left_going, hops):
         return (
@@ -402,7 +418,9 @@
     received = lax.all_to_all(
         outgoing.reshape(PLANE, 2 * SLOTS, half), FLAT, split_axis=0, concat_axis=0, tiled=True
     ).reshape(2 * BLOCK, half)
-    received = call(turn_kernel, struct((2 * BLOCK, half), BF16), flops=1 << 28)(received, apart)
+    received = call(turn_kernel, struct((2 * BLOCK, half), BF16), flops=1 << 28, vmem=24)(
+        received, apart
+    )
     r1, l1 = onward(own_pairs, own_pairs, 0)
     received, around, r1, l1 = lax.optimization_barrier((received, around, r1, l1))
     right = lax.all_gather(received, Z, axis=0, tiled=True)
@@ -412,30 +430,32 @@
         (struct((RING * BLOCK, half), BF16), struct((RING, TOK), F32)),
         scratch=[pltpu.VMEM((RING * BLOCK, half), BF16)],
         flops=1 << 30,
+        vmem=24,
     )(around, side, swap)
+    target, r1, l1 = lax.optimization_barrier((target, r1, l1))
+    r2, l2 = onward(r1, l1, 1)
     arrived = lax.all_to_all(
         chosen.reshape(PLANE, PIECE, half), FLAT, split_axis=0, concat_axis=0, tiled=True
     ).reshape(RING * BLOCK, half)
-    left = call(spread_kernel, struct((RING * BLOCK, half), BF16), flops=1 << 30)(arrived, swap)
+    left = call(spread_kernel, struct((RING * BLOCK, half), BF16), flops=1 << 30, vmem=24)(arrived, swap)
+
+    left, r2, l2 = lax.optimization_barrier((left, r2, l2))
+    r3, l3 = onward(r2, l2, 2)
 
     first = w_in[0]
     second = w_out[0]
     partial = dot(left, first[:half])
-    partial, r1, l1 = lax.optimization_barrier((partial, r1, l1))
-    r2, l2 = onward(r1, l1, 1)
     hidden, term_right = expert_right(
         side.reshape(1), right.reshape(RING, 2, BLOCK, half), partial, first, second
     )
-    hidden, term_right, r2, l2 = lax.optimization_barrier((hidden, term_right, r2, l2))
-    r3, l3 = onward(r2, l2, 2)
+    hidden, term_right, r3, l3 = lax.optimization_barrier((hidden, term_right, r3, l3))
     result = lax.psum_scatter(
         term_right.reshape(2 * RING * BLOCK, half), Z, scatter_dimension=0, tiled=True
     )
     term_left = lax.optimization_barrier(dot_t(hidden, second[:half]).astype(BF16))
-    leaving = call(unspread_kernel, struct((RING * BLOCK, half), BF16), flops=1 << 30)(
+    leaving = call(unspread_kernel, struct((RING * BLOCK, half), BF16), flops=1 << 30, vmem=24)(
         term_left, swap
     )
-    leaving, r3, l3 = lax.optimization_barrier((leaving, r3, l3))
     back = lax.all_to_all(
         leaving.reshape(PLANE, PIECE, half), FLAT, split_axis=0, concat_axis=0, tiled=True
     ).reshape(RING * BLOCK, half)
@@ -447,7 +467,7 @@
     )(back, swap, target)
     by_token, result = lax.optimization_barrier((by_token, result))
     given = lax.psum_scatter(by_token, Z, scatter_dimension=0, tiled=True)
-    result = call(turn_kernel, struct((2 * BLOCK, half), BF16), flops=1 << 28)(result, together)
+    result = call(turn_kernel, struct((2 * BLOCK, half), BF16), flops=1 << 28, vmem=24)(result, together)
     returned = lax.all_to_all(
         result.reshape(PLANE, 2 * SLOTS, half), FLAT, split_axis=0, concat_axis=0, tiled=True
     ).reshape(2 * BLOCK, half)

time: 257 us -> 269 us (1.047)
  waiting for transfers between devices: 57.5 us -> 107 us
  blocking collectives: 85.1 us -> 52.6 us
  starting transfers between devices: 19.6 us -> 29.9 us
  Pallas kernels: 52.1 us -> 42 us
  matrix products: 15.6 us -> 11.2 us
    all_to_all x1 -> x0, blocking collectives: 33.4 us -> none  [shards(): lax.all_to_all(chosen.reshape(PLANE, PIECE, half), FLAT, split_axis=0, co...]
    all_to_all x0 -> x1, waiting for transfers between devices: none -> 24.3 us  [shards(): lax.all_to_all(chosen.reshape(PLANE, PIECE, half), FLAT, split_axis=0, co...]
    all_gather x1, waiting for transfers between devices: 0.35 us -> 24.2 us  [shards(): right = lax.all_gather(received, Z, axis=0, tiled=True)]
    ppermute x3, waiting for transfers between devices: 17.3 us -> 7.17 us  [onward(): lax.ppermute(left_going, 'zl', [(i, i - 1) for i in range(1, LOOP - hops)])]
    reduce_scatter x1, waiting for transfers between devices: 10.9 us -> 19.8 us  [shards(): given = lax.psum_scatter(by_token, Z, scatter_dimension=0, tiled=True)]
    pallas_call x5, Pallas kernels: 16.3 us -> 7.6 us  [the longest x1 3.39 us: pack_pairs(): pl.pallas_call(pack_kernel, grid=(1,), out_shape=struct((SHARD, embed), B...]
    all_to_all x0 -> x1, starting transfers between devices: none -> 7.62 us  [shards(): lax.all_to_all(chosen.reshape(PLANE, PIECE, half), FLAT, split_axis=0, co...]
    reduce_scatter x1, waiting for transfers between devices: 0.01 us -> 6.71 us  [shards(): lax.psum_scatter(term_right.reshape(2 * RING * BLOCK, half), Z, scatter_d...]
  transfers between devices with their start and end apart: 14 -> 15, of which waited for: 7 -> 8; matrix products, arithmetic and copies ran while one was open for 9% -> 6% of each run, Pallas kernels for 17% -> 13%
where the time goes in v4:
time: 269 us; the launch traced here: 268 us
  waiting for transfers between devices  107 us (40%)
  blocking collectives  52.6 us (20%)
  Pallas kernels  42 us (16%)
  starting transfers between devices  29.9 us (11%)
  between operations  14.1 us (5%)
  matrix products  11.2 us (4%)
  local copies, waits for them, and re-layouts  7.47 us (3%)
  other arithmetic  3.03 us (1%)
    all_to_all x1, blocking collectives, shards(): lax.all_to_all(leaving.reshape(PLANE, PIECE, half), FLAT, split_axis=0, c...  33.3 us
    all_to_all x1, waiting for transfers between devices, shards(): lax.all_to_all(chosen.reshape(PLANE, PIECE, half), FLAT, split_axis=0, co...  24.3 us
    all_gather x1, waiting for transfers between devices, shards(): right = lax.all_gather(received, Z, axis=0, tiled=True)  24.2 us
    all_gather x1, waiting for transfers between devices, shards(): around = lax.all_gather(packed, Z, axis=0, tiled=True)  20.6 us
    reduce_scatter x1, waiting for transfers between devices, shards(): given = lax.psum_scatter(by_token, Z, scatter_dimension=0, tiled=True)  19.8 us
    all_to_all x1, blocking collectives, shards(): lax.all_to_all(outgoing.reshape(PLANE, 2 * SLOTS, half), FLAT, split_axis...  19.3 us
    pallas_call x1, Pallas kernels, expert_right(): pl.pallas_call(expert_kernel, out_shape=(struct((RING * BLOCK, inner), BF...  11.4 us
    all_to_all x1, starting transfers between devices, shards(): lax.all_to_all(chosen.reshape(PLANE, PIECE, half), FLAT, split_axis=0, co...  7.62 us
  transfers between devices with their start and end apart: 15, of which 8 were waited for; matrix products, arithmetic and copies ran while one was open for 6% of the time, Pallas kernels for 13%

profile of v4, /device:TPU:2, one launch (start us, length us, event | category | flops | bytes accessed | tf_op | source)
XLA Modules:
  0.0 267.6 jit_solution(14812717626485104436)
XLA Ops:
  7.2 2.7 shard_map.156
  9.9 3.4 %shard_map.157.own = bf16[272,1024]{1,0:T(8,128)(2,1)} custom-call(bf16[127,1280]{1,0:T(8,128)(2,1)} %pooled.1, bf16[1280,1024]{1,0:T(8,128)(2,1)} %head.5, bf16[128,1024]{1,0:T(8,128)(2,1)} %text_embed.1, s32[1,128]{1,0:T(1,128)} %bitcast.30), custom_call_target="tpu_custom_call" | custom-call | flops 268435456 | bytes 4194304 | tf_op jit(solution)/shard_map/pallas_call | solution.py:312
  13.3 4.8 %collective-permute-start = (bf16[272,1024]{1,0:T(8,128)(2,1)}, bf16[272,1024]{1,0:T(8,128)(2,1)}, u32[]{:S(2)}, u32[]{:S(2)}) collective-permute-start(bf16[272,1024]{1,0:T(8,128)(2,1)} %shard_map.157.own), channel_id=1, source_target_pairs={{0,1},{1,2},{2,3},{4,5},{5,6},{6,7},{8,9},{9,10},{10,11},{12,13},{... | collective-permute-start | bytes 1671176 | tf_op jit(solution)/shard_map/ppermute | solution.py:413
  18.1 1.3 collective-permute-start.1
  19.5 19.3 %all_to_all.20 = bf16[32,12,640]{2,1,0:T(8,128)(2,1)S(1)} all-to-all(bf16[32,12,640]{2,1,0:T(8,128)(2,1)S(1)} %reshape.63), channel_id=1, replica_groups=mesh['zh'=2,'y'=4,'x'=4,'c'=2,'zl'=4] {'y','x','c'}, dimensions={0} | all-to-all | bytes 983040 | tf_op jit(solution)/shard_map/all_to_all | solution.py:418
  38.8 0.1 reshape.64.rows
  39.0 1.2 shard_map.158
  40.2 3.3 %collective-permute-done.1 = bf16[272,1024]{1,0:T(8,128)(2,1)S(1)} collective-permute-done((bf16[272,1024]{1,0:T(8,128)(2,1)}, bf16[272,1024]{1,0:T(8,128)(2,1)S(1)}, u32[]{:S(2)}, u32[]{:S(2)}) %collective-permute-start.1) | collective-permute-done | bytes 557088 | tf_op jit(solution)/shard_map/ppermute | solution.py:414
  43.4 20.6 %all-gather.3.cloned.1.call-done.gathered = bf16[2176,640]{1,0:T(8,128)(2,1)} async-done(((bf16[272,640]{1,0:T(8,128)(2,1)}), bf16[2176,640]{1,0:T(8,128)(2,1)}) %all-gather.3.cloned.1.call-update) | async-done | bytes 2785296 | tf_op jit(solution)/shard_map/all_gather | solution.py:417
  64.1 1.8 copy-done.14
  65.9 1.9 shard_map.159
  67.9 1.3 copy-done.5
  69.2 0.6 copy-done.12
  69.8 7.6 %all-to-all-start.1 = ((bf16[32,48,640]{2,1,0:T(8,128)(2,1)}), bf16[32,48,640]{2,1,0:T(8,128)(2,1)S(1)}, u32[]{:S(2)}, u32[]{:S(2)}) async-start(bf16[32,48,640]{2,1,0:T(8,128)(2,1)} %bitcast.25), calls=%async_computation.1 | async-start | bytes 3932160 | tf_op jit(solution)/shard_map/all_to_all | solution.py:437
  77.5 0.7 collective-permute-start.2
  78.2 1.3 collective-permute-start.3
  79.5 24.3 %all-to-all-done.1 = bf16[32,48,640]{2,1,0:T(8,128)(2,1)S(1)} async-done(((bf16[32,48,640]{2,1,0:T(8,128)(2,1)}), bf16[32,48,640]{2,1,0:T(8,128)(2,1)S(1)}, u32[]{:S(2)}, u32[]{:S(2)}) %all-to-all-start.1) | async-done | bytes 1966112 | tf_op jit(solution)/shard_map/all_to_all | solution.py:437
  103.8 1.3 shard_map.160
  105.1 3.9 %collective-permute-done.3 = bf16[272,1024]{1,0:T(8,128)(2,1)S(1)} collective-permute-done((bf16[272,1024]{1,0:T(8,128)(2,1)}, bf16[272,1024]{1,0:T(8,128)(2,1)S(1)}, u32[]{:S(2)}, u32[]{:S(2)}) %collective-permute-start.3) | collective-permute-done | bytes 557088 | tf_op jit(solution)/shard_map/ppermute | solution.py:414
  109.0 0.7 collective-permute-start.4
  109.7 1.3 collective-permute-start.5
  111.0 5.3 %fusion.1.partial = f32[1536,1280]{1,0:T(8,128)} fusion(bf16[1536,640]{1,0:T(8,128)(2,1)S(1)} %shard_map.160, bf16[1,1280,1280]{2,1,0:T(8,128)(2,1)S(1)} %copy-done.19), kind=kOutput, calls=%fused_computation.2 | convolution fusion | flops 2516582400 | bytes 11468800 | tf_op jit(solution)/shard_map/dot_general | solution.py:58
  116.3 24.2 %all-gather.5.cloned.1.call-done = bf16[3072,640]{1,0:T(8,128)(2,1)} async-done(((bf16[384,640]{1,0:T(8,128)(2,1)}), bf16[3072,640]{1,0:T(8,128)(2,1)}) %all-gather.5.cloned.1.call-update) | async-done | bytes 3932176 | tf_op jit(solution)/shard_map/all_gather | solution.py:426
  140.5 11.4 %shard_map.161 = (bf16[1536,1280]{1,0:T(8,128)(2,1)}, bf16[8,2,192,640]{3,2,1,0:T(8,128)(2,1)}) custom-call(s32[1]{0:T(128)} %bitcast.4.side, bf16[8,2,192,640]{3,2,1,0:T(8,128)(2,1)} %bitcast.32, f32[1536,1280]{1,0:T(8,128)} %fusion.1.partial, bf16[1280,1280]{1,0:T(8,128)(2,1)} %bitcast.33, bf16[1280,1280]{1,0:T(8,128)(2,1)} %bitcast.34), custom_call_target="tpu_custom_call" | custom-call | flops 5033164800 | bytes 20971520 | tf_op jit(solution)/shard_map/pallas_call | solution.py:186
  152.0 0.2 reduce-scatter.5.cloned.1.call-start
  152.2 5.9 %convolution_convert_fusion.rows = bf16[1536,640]{1,0:T(8,128)(2,1)S(1)} fusion(bf16[1536,1280]{1,0:T(8,128)(2,1)} %get-tuple-element.67, bf16[1,1280,1280]{2,1,0:T(8,128)(2,1)} %param.18), kind=kOutput, calls=%fused_computation | convolution fusion | flops 2517565440 | bytes 7536640 | tf_op jit(solution)/shard_map/dot_general | solution.py:62
  158.1 1.3 shard_map.163
  159.4 33.3 %all_to_all.21 = bf16[32,48,640]{2,1,0:T(8,128)(2,1)} all-to-all(bf16[32,48,640]{2,1,0:T(8,128)(2,1)S(1)} %bitcast.24), channel_id=1, replica_groups=mesh['zh'=2,'y'=4,'x'=4,'c'=2,'zl'=4] {'y','x','c'}, dimensions={0} | all-to-all | bytes 3932160 | tf_op jit(solution)/shard_map/all_to_all | solution.py:459
  192.7 5.3 %shard_map.164 = bf16[2048,640]{1,0:T(8,128)(2,1)} custom-call(bf16[1536,640]{1,0:T(8,128)(2,1)} %bitcast.26, bf16[384,384]{1,0:T(8,128)(2,1)} %constant.22.clone.swap, f32[8,256]{1,0:T(8,128)} %copy-done.12), custom_call_target="tpu_custom_call" | custom-call | flops 1073741824 | bytes 4194304 | tf_op jit(solution)/shard_map/pallas_call | solution.py:462
  198.0 6.7 %reduce-scatter.3.cloned.1.call-done.rows = bf16[384,640]{1,0:T(8,128)(2,1)} async-done(((bf16[3072,640]{1,0:T(8,128)(2,1)}), bf16[384,640]{1,0:T(8,128)(2,1)}) %reduce-scatter.3.cloned.1.call-update) | async-done | bytes 491536 | tf_op jit(solution)/shard_map/reduce_scatter | solution.py:452
  204.8 1.0 copy-done.8
  205.7 0.4 shard_map.165
  206.2 0.9 reshape.72
  207.1 7.4 %all-to-all-start.3 = ((bf16[32,12,640]{2,1,0:T(8,128)(2,1)}), bf16[32,12,640]{2,1,0:T(8,128)(2,1)S(1)}, u32[]{:S(2)}, u32[]{:S(2)}) async-start(bf16[32,12,640]{2,1,0:T(8,128)(2,1)} %reshape.72), calls=%async_computation.4 | async-start | bytes 1310720 | tf_op jit(solution)/shard_map/all_to_all | solution.py:471
  214.6 0.9 broadcast_select_fusion.1.s2
  215.4 2.2 broadcast_select_fusion
  217.6 4.4 %shard_map.162 = (f32[1,128]{1,0:T(1,128)}, f32[128,1024]{1,0:T(8,128)}, f32[128,1024]{1,0:T(8,128)}) custom-call(bf16[272,1024]{1,0:T(8,128)(2,1)} %shard_map.157.own, bf16[272,1024]{1,0:T(8,128)(2,1)} %get-tuple-element.85.s1, bf16[272,1024]{1,0:T(8,128)(2,1)} %broadcast_select_fusion.1.s2, bf16[272,1024]{1,0:T(8,128)(2,1)} %get-tuple-element.84.s3), custom_call_target="tpu_custom_call" | custom-call | flops 1073741824 | bytes 4194304 | tf_op jit(solution)/shard_map/pallas_call | solution.py:484
  222.0 4.5 %all-to-all-done.3 = bf16[32,12,640]{2,1,0:T(8,128)(2,1)S(1)} async-done(((bf16[32,12,640]{2,1,0:T(8,128)(2,1)}), bf16[32,12,640]{2,1,0:T(8,128)(2,1)S(1)}, u32[]{:S(2)}, u32[]{:S(2)}) %all-to-all-start.3) | async-done | bytes 491552 | tf_op jit(solution)/shard_map/all_to_all | solution.py:471
  226.5 0.9 reshape.73.returned
  227.3 2.9 %shard_map.166 = (bf16[256,1280]{1,0:T(8,128)(2,1)}, f32[16,1024]{1,0:T(8,128)}) custom-call(bf16[256,1280]{1,0:T(8,128)(2,1)} %tokens.5, f32[1,256]{1,0:T(1,128)} %get-tuple-element.66.position, f32[1,256]{1,0:T(1,128)} %bitcast.28, bf16[384,640]{1,0:T(8,128)(2,1)} %reshape.73.returned, bf16[1280,1024]{1,0:T(8,128)(2,1)} %head.5), custom_call_target="tpu_custom_call" | custom-call | flops 268435456 | bytes 4194304 | tf_op jit(solution)/shard_map/pallas_call | solution.py:260
  230.3 19.8 %reduce-scatter.5.cloned.1.call-done.given = bf16[256,640]{1,0:T(8,128)(2,1)} async-done(((bf16[2048,640]{1,0:T(8,128)(2,1)}), bf16[256,640]{1,0:T(8,128)(2,1)}) %reduce-scatter.5.cloned.1.call-update) | async-done | bytes 327696 | tf_op jit(solution)/shard_map/reduce_scatter | solution.py:469
  250.1 2.7 %shard_map.167 = (bf16[256,1280]{1,0:T(8,128)(2,1)}, bf16[1,1152]{1,0:T(2,128)(2,1)}) custom-call(bf16[256,1280]{1,0:T(8,128)(2,1)} %tokens.5, f32[1,256]{1,0:T(1,128)} %bitcast.29, bf16[256,640]{1,0:T(8,128)(2,1)} %reduce-scatter.5.cloned.1.call-done.given, bf16[1280,1024]{1,0:T(8,128)(2,1)} %head.5, ...), custom_call_target="tpu_custom_call", output_to_operand_aliasing={{0}: (6, {})} | custom-call | flops 268435456 | bytes 4194304 | tf_op jit(solution)/shard_map/pallas_call | solution.py:279
  252.7 0.5 collective-permute-start.6
  253.3 2.7 %collective-permute-start.7 = (bf16[1,1152]{1,0:T(2,128)(2,1)}, bf16[1,1152]{1,0:T(2,128)(2,1)S(1)}, u32[]{:S(2)}, u32[]{:S(2)}) collective-permute-start(bf16[1,1152]{1,0:T(2,128)(2,1)} %get-tuple-element.78.own_image.i0), channel_id=1, source_target_pairs={{0,2},{1,3},{2,0},{3,1},{4,6},{5,7},{6,4},{7,5},{8,10},{9,11},{10,... | collective-permute-start | bytes 6920 | tf_op jit(solution)/shard_map/ppermute | solution.py:405
  256.0 1.3 collective-permute-start.8
  257.3 0.7 copy-done.11
  258.0 1.8 shard_map.168
  259.8 1.3 shard_map.169
  (50 shorter events, 0.4 us)
Async XLA Ops:
  7.2 56.9 %all-gather.3.cloned.1.call-start = ((), (), s32[]{:S(2)}) async-start(), calls=%async_computation.6 | async-start | bytes 3133440 | tf_op jit(solution)/shard_map/all_gather | solution.py:417
  9.9 9.5 %copy-start.18 = (bf16[384,640]{1,0:T(8,128)(2,1)S(1)}, bf16[384,640]{1,0:T(8,128)(2,1)}, u32[]{:S(2)}) copy-start(bf16[384,640]{1,0:T(8,128)(2,1)} %get-tuple-element.46) | copy-start | bytes 1474564
  9.9 130.6 %all-gather.5.cloned.1.call-start = ((), (), s32[]{:S(2)}) async-start(), calls=%async_computation.7 | async-start | bytes 4423680 | tf_op jit(solution)/shard_map/all_gather | solution.py:426
  9.9 29.0 %copy-start.10 = (bf16[384,384]{1,0:T(8,128)(2,1)S(1)}, bf16[384,384]{1,0:T(8,128)(2,1)}, u32[]{:S(2)}) copy-start(bf16[384,384]{1,0:T(8,128)(2,1)} %constant.23.clone.matrix) | copy-start | bytes 884740
  13.3 50.8 %copy-start.1 = (bf16[384,384]{1,0:T(8,128)(2,1)S(1)}, bf16[384,384]{1,0:T(8,128)(2,1)}, u32[]{:S(2)}) copy-start(bf16[384,384]{1,0:T(8,128)(2,1)} %constant.22.clone.swap) | copy-start | bytes 884740
  13.3 26.8 %collective-permute-start = (bf16[272,1024]{1,0:T(8,128)(2,1)}, bf16[272,1024]{1,0:T(8,128)(2,1)}, u32[]{:S(2)}, u32[]{:S(2)}) collective-permute-start(bf16[272,1024]{1,0:T(8,128)(2,1)} %shard_map.157.own), channel_id=1, source_target_pairs={{0,1},{1,2},{2,3},{4,5},{5,6},{6,7},{8,9},{9,10},{10,11},{12,13},{... | collective-permute-start | bytes 1671176 | tf_op jit(solution)/shard_map/ppermute | solution.py:413
  18.1 25.3 %collective-permute-start.1 = (bf16[272,1024]{1,0:T(8,128)(2,1)}, bf16[272,1024]{1,0:T(8,128)(2,1)S(1)}, u32[]{:S(2)}, u32[]{:S(2)}) collective-permute-start(bf16[272,1024]{1,0:T(8,128)(2,1)} %shard_map.157.own), channel_id=1, source_target_pairs={{1,0},{2,1},{3,2},{5,4},{6,5},{7,6},{9,8},{10,9},{11,10},{13,12},{... | collective-permute-start | bytes 1671176 | tf_op jit(solution)/shard_map/ppermute | solution.py:414
  43.4 26.4 %copy-start.15 = (bf16[272,1024]{1,0:T(8,128)(2,1)}, bf16[272,1024]{1,0:T(8,128)(2,1)S(1)}, u32[]{:S(2)}) copy-start(bf16[272,1024]{1,0:T(8,128)(2,1)S(1)} %collective-permute-done.1) | copy-start | bytes 1671172
  64.1 1.8 copy-start.14
  67.9 1.3 copy-start.5
  69.2 0.6 copy-start.12
  69.8 34.0 %all-to-all-start.1 = ((bf16[32,48,640]{2,1,0:T(8,128)(2,1)}), bf16[32,48,640]{2,1,0:T(8,128)(2,1)S(1)}, u32[]{:S(2)}, u32[]{:S(2)}) async-start(bf16[32,48,640]{2,1,0:T(8,128)(2,1)} %bitcast.25), calls=%async_computation.1 | async-start | bytes 3932160 | tf_op jit(solution)/shard_map/all_to_all | solution.py:437
  77.4 127.3 %reduce-scatter.3.cloned.1.call-start = ((), (), s32[]{:S(2)}) async-start(), calls=%async_computation.8 | async-start | bytes 4423680 | tf_op jit(solution)/shard_map/reduce_scatter | solution.py:452
  77.5 27.6 %collective-permute-start.2 = (bf16[272,1024]{1,0:T(8,128)(2,1)}, bf16[272,1024]{1,0:T(8,128)(2,1)S(1)}, u32[]{:S(2)}, u32[]{:S(2)}) collective-permute-start(bf16[272,1024]{1,0:T(8,128)(2,1)} %collective-permute-done), channel_id=1, source_target_pairs={{1,2},{2,3},{5,6},{6,7},{9,10},{10,11},{13,14},{14,15},{17,18},{18... | collective-permute-start | bytes 1671176 | tf_op jit(solution)/shard_map/ppermute | solution.py:413
  78.2 30.8 %collective-permute-start.3 = (bf16[272,1024]{1,0:T(8,128)(2,1)}, bf16[272,1024]{1,0:T(8,128)(2,1)S(1)}, u32[]{:S(2)}, u32[]{:S(2)}) collective-permute-start(bf16[272,1024]{1,0:T(8,128)(2,1)} %copy-done.15), channel_id=1, source_target_pairs={{1,0},{2,1},{5,4},{6,5},{9,8},{10,9},{13,12},{14,13},{17,16},{18,1... | collective-permute-start | bytes 1671176 | tf_op jit(solution)/shard_map/ppermute | solution.py:414
  103.8 7.2 %copy-start.19 = (bf16[1,1280,1280]{2,1,0:T(8,128)(2,1)S(1)}, bf16[1,1280,1280]{2,1,0:T(8,128)(2,1)}, u32[]{:S(2)}) copy-start(bf16[1,1280,1280]{2,1,0:T(8,128)(2,1)} %param.17) | copy-start | bytes 9830404
  109.0 42.9 %collective-permute-start.4 = (bf16[272,1024]{1,0:T(8,128)(2,1)S(1)}, bf16[272,1024]{1,0:T(8,128)(2,1)S(1)}, u32[]{:S(2)}, u32[]{:S(2)}) collective-permute-start(bf16[272,1024]{1,0:T(8,128)(2,1)S(1)} %collective-permute-done.2), channel_id=1, source_target_pairs={{2,3},{6,7},{10,11},{14,15},{18,19},{22,23},{26,27},{30,31},{34,35... | collective-permute-start | bytes 1671176 | tf_op jit(solution)/shard_map/ppermute | solution.py:413
  109.7 42.3 %collective-permute-start.5 = (bf16[272,1024]{1,0:T(8,128)(2,1)S(1)}, bf16[272,1024]{1,0:T(8,128)(2,1)S(1)}, u32[]{:S(2)}, u32[]{:S(2)}) collective-permute-start(bf16[272,1024]{1,0:T(8,128)(2,1)S(1)} %collective-permute-done.3), channel_id=1, source_target_pairs={{1,0},{5,4},{9,8},{13,12},{17,16},{21,20},{25,24},{29,28},{33,32},... | collective-permute-start | bytes 1671176 | tf_op jit(solution)/shard_map/ppermute | solution.py:414
  152.0 6.1 %copy-start.17 = (bf16[272,1024]{1,0:T(8,128)(2,1)}, bf16[272,1024]{1,0:T(8,128)(2,1)S(1)}, u32[]{:S(2)}) copy-start(bf16[272,1024]{1,0:T(8,128)(2,1)S(1)} %collective-permute-done.5) | copy-start | bytes 1671172
  152.0 98.0 %reduce-scatter.5.cloned.1.call-start = ((), (), s32[]{:S(2)}) async-start(), calls=%async_computation.9 | async-start | bytes 2949120 | tf_op jit(solution)/shard_map/reduce_scatter | solution.py:469
  192.7 12.1 %copy-start.9 = (bf16[384,384]{1,0:T(8,128)(2,1)S(1)}, bf16[384,384]{1,0:T(8,128)(2,1)}, u32[]{:S(2)}) copy-start(bf16[384,384]{1,0:T(8,128)(2,1)} %constant.24.clone.matrix) | copy-start | bytes 884740
  204.7 1.0 copy-start.8
  204.7 10.7 %copy-start.16 = (bf16[272,1024]{1,0:T(8,128)(2,1)S(1)}, bf16[272,1024]{1,0:T(8,128)(2,1)}, u32[]{:S(2)}) copy-start(bf16[272,1024]{1,0:T(8,128)(2,1)} %copy-done.15) | copy-start | bytes 1671172
  207.1 19.3 %all-to-all-start.3 = ((bf16[32,12,640]{2,1,0:T(8,128)(2,1)}), bf16[32,12,640]{2,1,0:T(8,128)(2,1)S(1)}, u32[]{:S(2)}, u32[]{:S(2)}) async-start(bf16[32,12,640]{2,1,0:T(8,128)(2,1)} %reshape.72), calls=%async_computation.4 | async-start | bytes 1310720 | tf_op jit(solution)/shard_map/all_to_all | solution.py:471
  230.2 27.0 %copy-start = (bf16[272,1024]{1,0:T(8,128)(2,1)S(1)}, bf16[272,1024]{1,0:T(8,128)(2,1)}, u32[]{:S(2)}) copy-start(bf16[272,1024]{1,0:T(8,128)(2,1)} %shard_map.157.own) | copy-start | bytes 1671172
  230.2 27.0 %copy-start.2 = (bf16[272,1024]{1,0:T(8,128)(2,1)S(1)}, bf16[272,1024]{1,0:T(8,128)(2,1)}, u32[]{:S(2)}) copy-start(bf16[272,1024]{1,0:T(8,128)(2,1)} %broadcast_select_fusion.1.s2) | copy-start | bytes 1671172
  230.2 27.0 %copy-start.3 = (bf16[272,1024]{1,0:T(8,128)(2,1)S(1)}, bf16[272,1024]{1,0:T(8,128)(2,1)}, u32[]{:S(2)}) copy-start(bf16[272,1024]{1,0:T(8,128)(2,1)} %get-tuple-element.84.s3) | copy-start | bytes 1671172
  230.2 27.0 %copy-start.4 = (bf16[272,1024]{1,0:T(8,128)(2,1)S(1)}, bf16[272,1024]{1,0:T(8,128)(2,1)}, u32[]{:S(2)}) copy-start(bf16[272,1024]{1,0:T(8,128)(2,1)} %get-tuple-element.85.s1) | copy-start | bytes 1671172
  230.3 27.0 %copy-start.6 = (f32[128,1024]{1,0:T(8,128)S(1)}, f32[128,1024]{1,0:T(8,128)}, u32[]{:S(2)}) copy-start(f32[128,1024]{1,0:T(8,128)} %get-tuple-element.80.image_acc) | copy-start | bytes 1572868
  230.3 27.0 %copy-start.13 = (f32[1,128]{1,0:T(1,128)S(1)}, f32[1,128]{1,0:T(1,128)}, u32[]{:S(2)}) copy-start(f32[1,128]{1,0:T(1,128)} %get-tuple-element.79.loss) | copy-start | bytes 1540
  250.1 9.8 %copy-start.7 = (f32[128,1024]{1,0:T(8,128)S(1)}, f32[128,1024]{1,0:T(8,128)}, u32[]{:S(2)}) copy-start(f32[128,1024]{1,0:T(8,128)} %get-tuple-element.83.text_acc) | copy-start | bytes 1572868
  252.7 7.0 %collective-permute-start.6 = (bf16[1,1152]{1,0:T(2,128)(2,1)}, bf16[1,1152]{1,0:T(2,128)(2,1)S(1)}, u32[]{:S(2)}, u32[]{:S(2)}) collective-permute-start(bf16[1,1152]{1,0:T(2,128)(2,1)} %get-tuple-element.78.own_image.i0), channel_id=1, source_target_pairs={{0,1},{1,2},{2,3},{3,0},{4,5},{5,6},{6,7},{7,4},{8,9},{9,10},{10,1... | collective-permute-start | bytes 6920 | tf_op jit(solution)/shard_map/ppermute | solution.py:405
  253.3 6.5 %collective-permute-start.7 = (bf16[1,1152]{1,0:T(2,128)(2,1)}, bf16[1,1152]{1,0:T(2,128)(2,1)S(1)}, u32[]{:S(2)}, u32[]{:S(2)}) collective-permute-start(bf16[1,1152]{1,0:T(2,128)(2,1)} %get-tuple-element.78.own_image.i0), channel_id=1, source_target_pairs={{0,2},{1,3},{2,0},{3,1},{4,6},{5,7},{6,4},{7,5},{8,10},{9,11},{10,... | collective-permute-start | bytes 6920 | tf_op jit(solution)/shard_map/ppermute | solution.py:405
  256.0 3.8 %collective-permute-start.8 = (bf16[1,1152]{1,0:T(2,128)(2,1)}, bf16[1,1152]{1,0:T(2,128)(2,1)S(1)}, u32[]{:S(2)}, u32[]{:S(2)}) collective-permute-start(bf16[1,1152]{1,0:T(2,128)(2,1)} %get-tuple-element.78.own_image.i0), channel_id=1, source_target_pairs={{0,3},{1,0},{2,1},{3,2},{4,7},{5,4},{6,5},{7,6},{8,11},{9,8},{10,9... | collective-permute-start | bytes 6920 | tf_op jit(solution)/shard_map/ppermute | solution.py:405
  257.3 0.7 copy-start.11
Sparse Core Ops, SparseCore 0:
  10.4 53.6 all-gather.2
  66.4 74.0 all-gather.4
  152.1 52.5 reduce-scatter.2
  207.1 42.8 reduce-scatter.4

commit v5 on v4

--- a/solution.py
+++ b/solution.py
@@ -406,12 +406,11 @@
         value, "zl", [(i, (i + step) % LOOP) for i in range(LOOP)]
     )
 
-    outgoing, own_pairs = lax.optimization_barrier((outgoing, own_pairs))
-
-    def onward(right_going, left_going, hops):
+
+    def both(right_going, left_going, senders, hops):
         return (
-            lax.ppermute(right_going, "zl", [(i, i + 1) for i in range(hops, LOOP - 1)]),
-            lax.ppermute(left_going, "zl", [(i, i - 1) for i in range(1, LOOP - hops)]),
+            lax.ppermute(right_going, "zl", [(i, i + hops) for i in senders]),
+            lax.ppermute(left_going, "zl", [(LOOP - 1 - i, LOOP - 1 - i - hops) for i in senders]),
         )
 
     around = lax.all_gather(packed, Z, axis=0, tiled=True)
@@ -421,8 +420,7 @@
     received = call(turn_kernel, struct((2 * BLOCK, half), BF16), flops=1 << 28, vmem=24)(
         received, apart
     )
-    r1, l1 = onward(own_pairs, own_pairs, 0)
-    received, around, r1, l1 = lax.optimization_barrier((received, around, r1, l1))
+    received, around, own_pairs = lax.optimization_barrier((received, around, own_pairs))
     right = lax.all_gather(received, Z, axis=0, tiled=True)
 
     chosen, target = call(
@@ -430,25 +428,22 @@
         (struct((RING * BLOCK, half), BF16), struct((RING, TOK), F32)),
         scratch=[pltpu.VMEM((RING * BLOCK, half), BF16)],
         flops=1 << 30,
-        vmem=24,
     )(around, side, swap)
-    target, r1, l1 = lax.optimization_barrier((target, r1, l1))
-    r2, l2 = onward(r1, l1, 1)
     arrived = lax.all_to_all(
         chosen.reshape(PLANE, PIECE, half), FLAT, split_axis=0, concat_axis=0, tiled=True
     ).reshape(RING * BLOCK, half)
     left = call(spread_kernel, struct((RING * BLOCK, half), BF16), flops=1 << 30, vmem=24)(arrived, swap)
 
-    left, r2, l2 = lax.optimization_barrier((left, r2, l2))
-    r3, l3 = onward(r2, l2, 2)
 
     first = w_in[0]
     second = w_out[0]
     partial = dot(left, first[:half])
+    partial, own_pairs = lax.optimization_barrier((partial, own_pairs))
+    r1, l1 = both(own_pairs, own_pairs, (0, 1, 2), 1)
     hidden, term_right = expert_right(
         side.reshape(1), right.reshape(RING, 2, BLOCK, half), partial, first, second
     )
-    hidden, term_right, r3, l3 = lax.optimization_barrier((hidden, term_right, r3, l3))
+    hidden, term_right, r1, l1 = lax.optimization_barrier((hidden, term_right, r1, l1))
     result = lax.psum_scatter(
         term_right.reshape(2 * RING * BLOCK, half), Z, scatter_dimension=0, tiled=True
     )
@@ -465,7 +460,11 @@
         scratch=[pltpu.VMEM((RING * BLOCK, half), BF16)],
         flops=1 << 30,
     )(back, swap, target)
-    by_token, result = lax.optimization_barrier((by_token, result))
+    by_token, result, r1, l1, own_pairs = lax.optimization_barrier(
+        (by_token, result, r1, l1, own_pairs)
+    )
+    r2, l2 = both(r1, l1, (1, 2), 1)
+    r3, l3 = both(own_pairs, own_pairs, (0,), 3)
     given = lax.psum_scatter(by_token, Z, scatter_dimension=0, tiled=True)
     result = call(turn_kernel, struct((2 * BLOCK, half), BF16), flops=1 << 28, vmem=24)(result, together)
     returned = lax.all_to_all(

time: 269 us -> 263 us (0.978)
  waiting for transfers between devices: 107 us -> 82.7 us
  blocking collectives: 52.6 us -> 66.4 us
  starting transfers between devices: 29.9 us -> 33.8 us
  Pallas kernels: 42 us -> 45 us
    all_gather x1, waiting for transfers between devices: 24.2 us -> 2.94 us  [shards(): right = lax.all_gather(received, Z, axis=0, tiled=True)]
    ppermute x6, waiting for transfers between devices: 7.17 us -> 24.7 us  [the longest x3 24.7 us: both(): lax.ppermute(left_going, 'zl', [(LOOP - 1 - i, LOOP - 1 - i - hops) for i...]
    all_to_all x1, waiting for transfers between devices: 24.3 us -> 8.47 us  [shards(): lax.all_to_all(outgoing.reshape(PLANE, 2 * SLOTS, half), FLAT, split_axis...]
    reduce_scatter x1, waiting for transfers between devices: 19.8 us -> 4.39 us  [shards(): given = lax.psum_scatter(by_token, Z, scatter_dimension=0, tiled=True)]
    all_to_all x1, blocking collectives: 19.3 us -> 33.5 us  [shards(): lax.all_to_all(chosen.reshape(PLANE, PIECE, half), FLAT, split_axis=0, co...]
    unnamed x40 -> x28, local copies, waits for them, and re-layouts: 5.42 us -> 1.39 us
    ppermute x6, starting transfers between devices: 10 us -> 14 us  [the longest x3 10.1 us: both(): lax.ppermute(right_going, 'zl', [(i, i + hops) for i in senders])]
    reduce_scatter x1, waiting for transfers between devices: 6.71 us -> 10.5 us  [shards(): lax.psum_scatter(term_right.reshape(2 * RING * BLOCK, half), Z, scatter_d...]
  transfers between devices with their start and end apart: 15 -> 15, of which waited for: 8 -> 10; matrix products, arithmetic and copies ran while one was open for 6% -> 7% of each run, Pallas kernels for 13% -> 15%
where the time goes in v5:
time: 263 us; the launch traced here: 262 us
  waiting for transfers between devices  82.7 us (31%)
  blocking collectives  66.4 us (25%)
  Pallas kernels  45 us (17%)
  starting transfers between devices  33.8 us (13%)
  between operations  14 us (5%)
  matrix products  11.2 us (4%)
  local copies, waits for them, and re-layouts  5.3 us (2%)
  other arithmetic  3.67 us (1%)
    all_to_all x1, blocking collectives, shards(): lax.all_to_all(chosen.reshape(PLANE, PIECE, half), FLAT, split_axis=0, co...  33.5 us
    all_to_all x1, blocking collectives, shards(): lax.all_to_all(leaving.reshape(PLANE, PIECE, half), FLAT, split_axis=0, c...  32.9 us
    ppermute x3, waiting for transfers between devices, both(): lax.ppermute(left_going, 'zl', [(LOOP - 1 - i, LOOP - 1 - i - hops) for i...  24.7 us
    all_gather x1, waiting for transfers between devices, shards(): around = lax.all_gather(packed, Z, axis=0, tiled=True)  23.6 us
    pallas_call x1, Pallas kernels, expert_right(): pl.pallas_call(expert_kernel, out_shape=(struct((RING * BLOCK, inner), BF...  11.4 us
    reduce_scatter x1, waiting for transfers between devices, shards(): lax.psum_scatter(term_right.reshape(2 * RING * BLOCK, half), Z, scatter_d...  10.5 us
    ppermute x3, starting transfers between devices, both(): lax.ppermute(right_going, 'zl', [(i, i + hops) for i in senders])  10.1 us
    all_to_all x1, waiting for transfers between devices, shards(): lax.all_to_all(outgoing.reshape(PLANE, 2 * SLOTS, half), FLAT, split_axis...  8.47 us
  transfers between devices with their start and end apart: 15, of which 10 were waited for; matrix products, arithmetic and copies ran while one was open for 7% of the time, Pallas kernels for 15%

profile of v5, /device:TPU:2, one launch (start us, length us, event | category | flops | bytes accessed | tf_op | source)
XLA Modules:
  0.0 262.0 jit_solution(6050230285534470953)
XLA Ops:
  7.2 2.7 %shard_map.156 = (bf16[272,640]{1,0:T(8,128)(2,1)}, bf16[384,640]{1,0:T(8,128)(2,1)}, f32[1,256]{1,0:T(1,128)}) custom-call(bf16[256,1280]{1,0:T(8,128)(2,1)} %tokens.5, s32[1,256]{1,0:T(1,128)} %bitcast.35, s32[1,64]{1,0:T(1,128)} %bitcast.36), custom_call_target="tpu_custom_call" | custom-call | flops 268435456 | bytes 4194304 | tf_op jit(solution)/shard_map/pallas_call | solution.py:394
  9.9 2.0 reshape.62
  11.8 7.6 %all-to-all-start = ((bf16[32,12,640]{2,1,0:T(8,128)(2,1)}), bf16[32,12,640]{2,1,0:T(8,128)(2,1)S(1)}, u32[]{:S(2)}, u32[]{:S(2)}) async-start(bf16[32,12,640]{2,1,0:T(8,128)(2,1)} %reshape.62), calls=%async_computation | async-start | bytes 1310720 | tf_op jit(solution)/shard_map/all_to_all | solution.py:417
  19.5 3.4 %shard_map.158.own = bf16[272,1024]{1,0:T(8,128)(2,1)} custom-call(bf16[127,1280]{1,0:T(8,128)(2,1)} %pooled.1, bf16[1280,1024]{1,0:T(8,128)(2,1)} %head.5, bf16[128,1024]{1,0:T(8,128)(2,1)} %text_embed.1, s32[1,128]{1,0:T(1,128)} %bitcast.30), custom_call_target="tpu_custom_call" | custom-call | flops 268435456 | bytes 4194304 | tf_op jit(solution)/shard_map/pallas_call | solution.py:312
  22.9 8.5 %all-to-all-done = bf16[32,12,640]{2,1,0:T(8,128)(2,1)S(1)} async-done(((bf16[32,12,640]{2,1,0:T(8,128)(2,1)}), bf16[32,12,640]{2,1,0:T(8,128)(2,1)S(1)}, u32[]{:S(2)}, u32[]{:S(2)}) %all-to-all-start) | async-done | bytes 491552 | tf_op jit(solution)/shard_map/all_to_all | solution.py:417
  31.5 1.2 shard_map.157
  32.7 23.6 %all-gather.3.cloned.1.call-done.gathered = bf16[2176,640]{1,0:T(8,128)(2,1)} async-done(((bf16[272,640]{1,0:T(8,128)(2,1)}), bf16[2176,640]{1,0:T(8,128)(2,1)}) %all-gather.3.cloned.1.call-update) | async-done | bytes 2785296 | tf_op jit(solution)/shard_map/all_gather | solution.py:416
  56.4 5.0 %shard_map.159 = (bf16[1536,640]{1,0:T(8,128)(2,1)}, f32[8,256]{1,0:T(8,128)}) custom-call(bf16[2176,640]{1,0:T(8,128)(2,1)} %all-gather.3.cloned.1.call-done.gathered, s32[1,1]{1,0:T(1,128)} %bitcast.6.side, bf16[384,384]{1,0:T(8,128)(2,1)} %constant.22.clone.swap), custom_call_target="tpu_custom_call" | custom-call | flops 1073741824 | bytes 4194304 | tf_op jit(solution)/shard_map/pallas_call | solution.py:426
  61.4 33.5 %all_to_all.20 = bf16[32,48,640]{2,1,0:T(8,128)(2,1)S(1)} all-to-all(bf16[32,48,640]{2,1,0:T(8,128)(2,1)} %bitcast.27), channel_id=1, replica_groups=mesh['zh'=2,'y'=4,'x'=4,'c'=2,'zl'=4] {'y','x','c'}, dimensions={0} | all-to-all | bytes 3932160 | tf_op jit(solution)/shard_map/all_to_all | solution.py:432
  94.9 1.3 shard_map.160
  96.2 0.7 copy-done.13
  96.9 5.3 %fusion.1.partial = f32[1536,1280]{1,0:T(8,128)} fusion(bf16[1536,640]{1,0:T(8,128)(2,1)S(1)} %shard_map.160, bf16[1,1280,1280]{2,1,0:T(8,128)(2,1)S(1)} %copy-done.13), kind=kOutput, calls=%fused_computation.2 | convolution fusion | flops 2516582400 | bytes 11468800 | tf_op jit(solution)/shard_map/dot_general | solution.py:58
  102.2 3.6 %collective-permute-start = (bf16[272,1024]{1,0:T(8,128)(2,1)S(1)}, bf16[272,1024]{1,0:T(8,128)(2,1)S(1)}, u32[]{:S(2)}, u32[]{:S(2)}) collective-permute-start(bf16[272,1024]{1,0:T(8,128)(2,1)S(1)} %copy-done), channel_id=1, source_target_pairs={{0,1},{1,2},{2,3},{4,5},{5,6},{6,7},{8,9},{9,10},{10,11},{12,13},{... | collective-permute-start | bytes 1671176 | tf_op jit(solution)/shard_map/ppermute | solution.py:412
  105.7 1.3 collective-permute-start.1
  107.0 2.9 %all-gather.5.cloned.1.call-done = bf16[3072,640]{1,0:T(8,128)(2,1)} async-done(((bf16[384,640]{1,0:T(8,128)(2,1)}), bf16[3072,640]{1,0:T(8,128)(2,1)}) %all-gather.5.cloned.1.call-update) | async-done | bytes 3932176 | tf_op jit(solution)/shard_map/all_gather | solution.py:424
  110.0 11.4 %shard_map.161 = (bf16[1536,1280]{1,0:T(8,128)(2,1)}, bf16[8,2,192,640]{3,2,1,0:T(8,128)(2,1)}) custom-call(s32[1]{0:T(128)} %bitcast.1.side, bf16[8,2,192,640]{3,2,1,0:T(8,128)(2,1)} %bitcast.32, f32[1536,1280]{1,0:T(8,128)} %fusion.1.partial, bf16[1280,1280]{1,0:T(8,128)(2,1)} %bitcast.33, bf16[1280,1280]{1,0:T(8,128)(2,1)} %bitcast.34), custom_call_target="tpu_custom_call" | custom-call | flops 5033164800 | bytes 20971520 | tf_op jit(solution)/shard_map/pallas_call | solution.py:186
  121.4 0.7 collective-permute-done.1
  122.1 0.2 reduce-scatter.5.cloned.1.call-start
  122.3 5.9 %convolution_convert_fusion.rows = bf16[1536,640]{1,0:T(8,128)(2,1)S(1)} fusion(bf16[1536,1280]{1,0:T(8,128)(2,1)} %get-tuple-element.50, bf16[1,1280,1280]{2,1,0:T(8,128)(2,1)} %param.18), kind=kOutput, calls=%fused_computation | convolution fusion | flops 2517565440 | bytes 7536640 | tf_op jit(solution)/shard_map/dot_general | solution.py:62
  128.2 1.3 shard_map.162
  129.5 32.9 %all_to_all.21 = bf16[32,48,640]{2,1,0:T(8,128)(2,1)} all-to-all(bf16[32,48,640]{2,1,0:T(8,128)(2,1)S(1)} %bitcast.24), channel_id=1, replica_groups=mesh['zh'=2,'y'=4,'x'=4,'c'=2,'zl'=4] {'y','x','c'}, dimensions={0} | all-to-all | bytes 3932160 | tf_op jit(solution)/shard_map/all_to_all | solution.py:454
  162.4 5.3 %shard_map.163 = bf16[2048,640]{1,0:T(8,128)(2,1)} custom-call(bf16[1536,640]{1,0:T(8,128)(2,1)} %bitcast.25, bf16[384,384]{1,0:T(8,128)(2,1)} %constant.22.clone.swap, f32[8,256]{1,0:T(8,128)} %get-tuple-element.51.target), custom_call_target="tpu_custom_call" | custom-call | flops 1073741824 | bytes 4194304 | tf_op jit(solution)/shard_map/pallas_call | solution.py:457
  167.7 10.5 %reduce-scatter.3.cloned.1.call-done.rows = bf16[384,640]{1,0:T(8,128)(2,1)} async-done(((bf16[3072,640]{1,0:T(8,128)(2,1)}), bf16[384,640]{1,0:T(8,128)(2,1)}) %reduce-scatter.3.cloned.1.call-update) | async-done | bytes 491536 | tf_op jit(solution)/shard_map/reduce_scatter | solution.py:447
  178.3 5.1 %collective-permute-start.5 = (bf16[272,1024]{1,0:T(8,128)(2,1)S(1)}, bf16[272,1024]{1,0:T(8,128)(2,1)S(1)}, u32[]{:S(2)}, u32[]{:S(2)}) collective-permute-start(bf16[272,1024]{1,0:T(8,128)(2,1)S(1)} %copy-done), channel_id=1, source_target_pairs={{0,3},{4,7},{8,11},{12,15},{16,19},{20,23},{24,27},{28,31},{32,35}... | collective-permute-start | bytes 1671176 | tf_op jit(solution)/shard_map/ppermute | solution.py:412
  183.4 0.4 shard_map.165
  183.8 0.9 reshape.72
  184.8 7.4 %all-to-all-start.3 = ((bf16[32,12,640]{2,1,0:T(8,128)(2,1)}), bf16[32,12,640]{2,1,0:T(8,128)(2,1)S(1)}, u32[]{:S(2)}, u32[]{:S(2)}) async-start(bf16[32,12,640]{2,1,0:T(8,128)(2,1)} %reshape.72), calls=%async_computation.4 | async-start | bytes 1310720 | tf_op jit(solution)/shard_map/all_to_all | solution.py:470
  192.2 1.3 collective-permute-start.2
  193.5 1.3 collective-permute-start.3
  194.8 1.5 collective-permute-start.4
  196.3 7.8 %all-to-all-done.3 = bf16[32,12,640]{2,1,0:T(8,128)(2,1)S(1)} async-done(((bf16[32,12,640]{2,1,0:T(8,128)(2,1)}), bf16[32,12,640]{2,1,0:T(8,128)(2,1)S(1)}, u32[]{:S(2)}, u32[]{:S(2)}) %all-to-all-start.3) | async-done | bytes 491552 | tf_op jit(solution)/shard_map/all_to_all | solution.py:470
  204.1 0.9 reshape.73.returned
  205.0 2.9 %shard_map.166 = (bf16[256,1280]{1,0:T(8,128)(2,1)}, f32[16,1024]{1,0:T(8,128)}) custom-call(bf16[256,1280]{1,0:T(8,128)(2,1)} %tokens.5, f32[1,256]{1,0:T(1,128)} %get-tuple-element.61.position, f32[1,256]{1,0:T(1,128)} %bitcast.28, bf16[384,640]{1,0:T(8,128)(2,1)} %reshape.73.returned, bf16[1280,1024]{1,0:T(8,128)(2,1)} %head.5), custom_call_target="tpu_custom_call" | custom-call | flops 268435456 | bytes 4194304 | tf_op jit(solution)/shard_map/pallas_call | solution.py:260
  207.9 0.9 broadcast_select_fusion.s3
  208.7 11.1 %collective-permute-done.2 = bf16[272,1024]{1,0:T(8,128)(2,1)S(1)} collective-permute-done((bf16[272,1024]{1,0:T(8,128)(2,1)S(1)}, bf16[272,1024]{1,0:T(8,128)(2,1)S(1)}, u32[]{:S(2)}, u32[]{:S(2)}) %collective-permute-start.2) | collective-permute-done | bytes 557088 | tf_op jit(solution)/shard_map/ppermute | solution.py:413
  219.9 0.9 broadcast_select_fusion.2.s1
  220.7 12.9 %collective-permute-done.3 = bf16[272,1024]{1,0:T(8,128)(2,1)} collective-permute-done((bf16[272,1024]{1,0:T(8,128)(2,1)S(1)}, bf16[272,1024]{1,0:T(8,128)(2,1)}, u32[]{:S(2)}, u32[]{:S(2)}) %collective-permute-start.3) | collective-permute-done | bytes 557088 | tf_op jit(solution)/shard_map/ppermute | solution.py:413
  233.6 1.9 broadcast_select_fusion.1.s2
  235.5 4.4 %shard_map.164 = (f32[1,128]{1,0:T(1,128)}, f32[128,1024]{1,0:T(8,128)}, f32[128,1024]{1,0:T(8,128)}) custom-call(bf16[272,1024]{1,0:T(8,128)(2,1)} %shard_map.158.own, bf16[272,1024]{1,0:T(8,128)(2,1)} %broadcast_select_fusion.2.s1, bf16[272,1024]{1,0:T(8,128)(2,1)} %broadcast_select_fusion.1.s2, bf16[272,1024]{1,0:T(8,128)(2,1)} %broadcast_select_fusion.s3), custom_call_target="tpu_custom_call" | custom-call | flops 1073741824 | bytes 4194304 | tf_op jit(solution)/shard_map/pallas_call | solution.py:483
  240.0 4.4 %reduce-scatter.5.cloned.1.call-done.given = bf16[256,640]{1,0:T(8,128)(2,1)} async-done(((bf16[2048,640]{1,0:T(8,128)(2,1)}), bf16[256,640]{1,0:T(8,128)(2,1)}) %reduce-scatter.5.cloned.1.call-update) | async-done | bytes 327696 | tf_op jit(solution)/shard_map/reduce_scatter | solution.py:468
  244.4 2.7 %shard_map.167 = (bf16[256,1280]{1,0:T(8,128)(2,1)}, bf16[1,1152]{1,0:T(2,128)(2,1)}) custom-call(bf16[256,1280]{1,0:T(8,128)(2,1)} %tokens.5, f32[1,256]{1,0:T(1,128)} %bitcast.29, bf16[256,640]{1,0:T(8,128)(2,1)} %reduce-scatter.5.cloned.1.call-done.given, bf16[1280,1024]{1,0:T(8,128)(2,1)} %head.5, ...), custom_call_target="tpu_custom_call", output_to_operand_aliasing={{0}: (6, {})} | custom-call | flops 268435456 | bytes 4194304 | tf_op jit(solution)/shard_map/pallas_call | solution.py:279
  247.1 0.7 collective-permute-start.6
  247.7 2.7 %collective-permute-start.7 = (bf16[1,1152]{1,0:T(2,128)(2,1)}, bf16[1,1152]{1,0:T(2,128)(2,1)S(1)}, u32[]{:S(2)}, u32[]{:S(2)}) collective-permute-start(bf16[1,1152]{1,0:T(2,128)(2,1)} %get-tuple-element.70.own_image.i0), channel_id=1, source_target_pairs={{0,2},{1,3},{2,0},{3,1},{4,6},{5,7},{6,4},{7,5},{8,10},{9,11},{10,... | collective-permute-start | bytes 6920 | tf_op jit(solution)/shard_map/ppermute | solution.py:405
  250.4 1.1 collective-permute-start.8
  251.5 0.7 copy-done.11
  252.2 1.8 shard_map.168
  254.0 0.2 collective-permute-done.8.i3
  254.2 1.3 shard_map.169
  (39 shorter events, 0.4 us)
Async XLA Ops:
  7.2 49.1 %all-gather.3.cloned.1.call-start = ((), (), s32[]{:S(2)}) async-start(), calls=%async_computation.6 | async-start | bytes 3133440 | tf_op jit(solution)/shard_map/all_gather | solution.py:416
  11.8 19.5 %all-to-all-start = ((bf16[32,12,640]{2,1,0:T(8,128)(2,1)}), bf16[32,12,640]{2,1,0:T(8,128)(2,1)S(1)}, u32[]{:S(2)}, u32[]{:S(2)}) async-start(bf16[32,12,640]{2,1,0:T(8,128)(2,1)} %reshape.62), calls=%async_computation | async-start | bytes 1310720 | tf_op jit(solution)/shard_map/all_to_all | solution.py:417
  19.5 12.0 %copy-start.10 = (bf16[384,384]{1,0:T(8,128)(2,1)S(1)}, bf16[384,384]{1,0:T(8,128)(2,1)}, u32[]{:S(2)}) copy-start(bf16[384,384]{1,0:T(8,128)(2,1)} %constant.23.clone.matrix) | copy-start | bytes 884740
  19.5 90.5 %all-gather.5.cloned.1.call-start = ((), (), s32[]{:S(2)}) async-start(), calls=%async_computation.7 | async-start | bytes 4423680 | tf_op jit(solution)/shard_map/all_gather | solution.py:424
  56.3 122.0 %reduce-scatter.3.cloned.1.call-start = ((), (), s32[]{:S(2)}) async-start(), calls=%async_computation.8 | async-start | bytes 4423680 | tf_op jit(solution)/shard_map/reduce_scatter | solution.py:447
  61.4 33.5 %copy-start.2 = (bf16[384,384]{1,0:T(8,128)(2,1)S(1)}, bf16[384,384]{1,0:T(8,128)(2,1)}, u32[]{:S(2)}) copy-start(bf16[384,384]{1,0:T(8,128)(2,1)} %constant.22.clone.swap) | copy-start | bytes 884740
  94.9 2.0 copy-start.13
  96.9 5.3 %copy-start = (bf16[272,1024]{1,0:T(8,128)(2,1)S(1)}, bf16[272,1024]{1,0:T(8,128)(2,1)}, u32[]{:S(2)}) copy-start(bf16[272,1024]{1,0:T(8,128)(2,1)} %shard_map.158.own) | copy-start | bytes 1671172
  102.2 19.2 %collective-permute-start = (bf16[272,1024]{1,0:T(8,128)(2,1)S(1)}, bf16[272,1024]{1,0:T(8,128)(2,1)S(1)}, u32[]{:S(2)}, u32[]{:S(2)}) collective-permute-start(bf16[272,1024]{1,0:T(8,128)(2,1)S(1)} %copy-done), channel_id=1, source_target_pairs={{0,1},{1,2},{2,3},{4,5},{5,6},{6,7},{8,9},{9,10},{10,11},{12,13},{... | collective-permute-start | bytes 1671176 | tf_op jit(solution)/shard_map/ppermute | solution.py:412
  105.7 16.4 %collective-permute-start.1 = (bf16[272,1024]{1,0:T(8,128)(2,1)S(1)}, bf16[272,1024]{1,0:T(8,128)(2,1)S(1)}, u32[]{:S(2)}, u32[]{:S(2)}) collective-permute-start(bf16[272,1024]{1,0:T(8,128)(2,1)S(1)} %copy-done), channel_id=1, source_target_pairs={{3,2},{2,1},{1,0},{7,6},{6,5},{5,4},{11,10},{10,9},{9,8},{15,14},{... | collective-permute-start | bytes 1671176 | tf_op jit(solution)/shard_map/ppermute | solution.py:413
  122.1 122.2 %reduce-scatter.5.cloned.1.call-start = ((), (), s32[]{:S(2)}) async-start(), calls=%async_computation.9 | async-start | bytes 2949120 | tf_op jit(solution)/shard_map/reduce_scatter | solution.py:468
  162.4 20.9 %copy-start.9 = (bf16[384,384]{1,0:T(8,128)(2,1)S(1)}, bf16[384,384]{1,0:T(8,128)(2,1)}, u32[]{:S(2)}) copy-start(bf16[384,384]{1,0:T(8,128)(2,1)} %constant.24.clone.matrix) | copy-start | bytes 884740
  178.3 5.1 %copy-start.8 = (bf16[384,640]{1,0:T(8,128)(2,1)S(1)}, bf16[384,640]{1,0:T(8,128)(2,1)}, u32[]{:S(2)}) copy-start(bf16[384,640]{1,0:T(8,128)(2,1)} %reduce-scatter.3.cloned.1.call-done.rows) | copy-start | bytes 1474564
  178.3 29.6 %collective-permute-start.5 = (bf16[272,1024]{1,0:T(8,128)(2,1)S(1)}, bf16[272,1024]{1,0:T(8,128)(2,1)S(1)}, u32[]{:S(2)}, u32[]{:S(2)}) collective-permute-start(bf16[272,1024]{1,0:T(8,128)(2,1)S(1)} %copy-done), channel_id=1, source_target_pairs={{0,3},{4,7},{8,11},{12,15},{16,19},{20,23},{24,27},{28,31},{32,35}... | collective-permute-start | bytes 1671176 | tf_op jit(solution)/shard_map/ppermute | solution.py:412
  184.8 19.3 %all-to-all-start.3 = ((bf16[32,12,640]{2,1,0:T(8,128)(2,1)}), bf16[32,12,640]{2,1,0:T(8,128)(2,1)S(1)}, u32[]{:S(2)}, u32[]{:S(2)}) async-start(bf16[32,12,640]{2,1,0:T(8,128)(2,1)} %reshape.72), calls=%async_computation.4 | async-start | bytes 1310720 | tf_op jit(solution)/shard_map/all_to_all | solution.py:470
  192.2 27.7 %collective-permute-start.2 = (bf16[272,1024]{1,0:T(8,128)(2,1)S(1)}, bf16[272,1024]{1,0:T(8,128)(2,1)S(1)}, u32[]{:S(2)}, u32[]{:S(2)}) collective-permute-start(bf16[272,1024]{1,0:T(8,128)(2,1)S(1)} %copy-done), channel_id=1, source_target_pairs={{3,0},{7,4},{11,8},{15,12},{19,16},{23,20},{27,24},{31,28},{35,32}... | collective-permute-start | bytes 1671176 | tf_op jit(solution)/shard_map/ppermute | solution.py:413
  193.5 40.1 %collective-permute-start.3 = (bf16[272,1024]{1,0:T(8,128)(2,1)S(1)}, bf16[272,1024]{1,0:T(8,128)(2,1)}, u32[]{:S(2)}, u32[]{:S(2)}) collective-permute-start(bf16[272,1024]{1,0:T(8,128)(2,1)S(1)} %collective-permute-done.1), channel_id=1, source_target_pairs={{2,1},{1,0},{6,5},{5,4},{10,9},{9,8},{14,13},{13,12},{18,17},{17,1... | collective-permute-start | bytes 1671176 | tf_op jit(solution)/shard_map/ppermute | solution.py:413
  194.8 38.8 %collective-permute-start.4 = (bf16[272,1024]{1,0:T(8,128)(2,1)S(1)}, bf16[272,1024]{1,0:T(8,128)(2,1)}, u32[]{:S(2)}, u32[]{:S(2)}) collective-permute-start(bf16[272,1024]{1,0:T(8,128)(2,1)S(1)} %collective-permute-done), channel_id=1, source_target_pairs={{1,2},{2,3},{5,6},{6,7},{9,10},{10,11},{13,14},{14,15},{17,18},{18... | collective-permute-start | bytes 1671176 | tf_op jit(solution)/shard_map/ppermute | solution.py:412
  239.9 11.6 %copy-start.1 = (bf16[272,1024]{1,0:T(8,128)(2,1)S(1)}, bf16[272,1024]{1,0:T(8,128)(2,1)}, u32[]{:S(2)}) copy-start(bf16[272,1024]{1,0:T(8,128)(2,1)} %shard_map.158.own) | copy-start | bytes 1671172
  239.9 11.6 %copy-start.3 = (bf16[272,1024]{1,0:T(8,128)(2,1)S(1)}, bf16[272,1024]{1,0:T(8,128)(2,1)}, u32[]{:S(2)}) copy-start(bf16[272,1024]{1,0:T(8,128)(2,1)} %broadcast_select_fusion.s3) | copy-start | bytes 1671172
  239.9 11.6 %copy-start.4 = (bf16[272,1024]{1,0:T(8,128)(2,1)S(1)}, bf16[272,1024]{1,0:T(8,128)(2,1)}, u32[]{:S(2)}) copy-start(bf16[272,1024]{1,0:T(8,128)(2,1)} %broadcast_select_fusion.2.s1) | copy-start | bytes 1671172
  239.9 11.6 %copy-start.5 = (bf16[272,1024]{1,0:T(8,128)(2,1)S(1)}, bf16[272,1024]{1,0:T(8,128)(2,1)}, u32[]{:S(2)}) copy-start(bf16[272,1024]{1,0:T(8,128)(2,1)} %broadcast_select_fusion.1.s2) | copy-start | bytes 1671172
  239.9 11.6 %copy-start.6 = (f32[128,1024]{1,0:T(8,128)S(1)}, f32[128,1024]{1,0:T(8,128)}, u32[]{:S(2)}) copy-start(f32[128,1024]{1,0:T(8,128)} %get-tuple-element.72.image_acc) | copy-start | bytes 1572868
  240.0 11.6 %copy-start.12 = (f32[1,128]{1,0:T(1,128)S(1)}, f32[1,128]{1,0:T(1,128)}, u32[]{:S(2)}) copy-start(f32[1,128]{1,0:T(1,128)} %get-tuple-element.71.loss) | copy-start | bytes 1540
  244.4 9.8 %copy-start.7 = (f32[128,1024]{1,0:T(8,128)S(1)}, f32[128,1024]{1,0:T(8,128)}, u32[]{:S(2)}) copy-start(f32[128,1024]{1,0:T(8,128)} %get-tuple-element.75.text_acc) | copy-start | bytes 1572868
  247.1 7.0 %collective-permute-start.6 = (bf16[1,1152]{1,0:T(2,128)(2,1)}, bf16[1,1152]{1,0:T(2,128)(2,1)S(1)}, u32[]{:S(2)}, u32[]{:S(2)}) collective-permute-start(bf16[1,1152]{1,0:T(2,128)(2,1)} %get-tuple-element.70.own_image.i0), channel_id=1, source_target_pairs={{0,1},{1,2},{2,3},{3,0},{4,5},{5,6},{6,7},{7,4},{8,9},{9,10},{10,1... | collective-permute-start | bytes 6920 | tf_op jit(solution)/shard_map/ppermute | solution.py:405
  247.7 6.3 %collective-permute-start.7 = (bf16[1,1152]{1,0:T(2,128)(2,1)}, bf16[1,1152]{1,0:T(2,128)(2,1)S(1)}, u32[]{:S(2)}, u32[]{:S(2)}) collective-permute-start(bf16[1,1152]{1,0:T(2,128)(2,1)} %get-tuple-element.70.own_image.i0), channel_id=1, source_target_pairs={{0,2},{1,3},{2,0},{3,1},{4,6},{5,7},{6,4},{7,5},{8,10},{9,11},{10,... | collective-permute-start | bytes 6920 | tf_op jit(solution)/shard_map/ppermute | solution.py:405
  250.4 3.8 %collective-permute-start.8 = (bf16[1,1152]{1,0:T(2,128)(2,1)}, bf16[1,1152]{1,0:T(2,128)(2,1)S(1)}, u32[]{:S(2)}, u32[]{:S(2)}) collective-permute-start(bf16[1,1152]{1,0:T(2,128)(2,1)} %get-tuple-element.70.own_image.i0), channel_id=1, source_target_pairs={{0,3},{1,0},{2,1},{3,2},{4,7},{5,4},{6,5},{7,6},{8,11},{9,8},{10,9... | collective-permute-start | bytes 6920 | tf_op jit(solution)/shard_map/ppermute | solution.py:405
  251.5 0.7 copy-start.11
Sparse Core Ops, SparseCore 0:
  10.4 45.8 all-gather.2
  58.7 51.2 all-gather.4
  122.2 55.9 reduce-scatter.2
  180.7 63.6 reduce-scatter.4

commit v6 on v5

--- a/solution.py
+++ b/solution.py
@@ -471,6 +471,8 @@
         result.reshape(PLANE, 2 * SLOTS, half), FLAT, split_axis=0, concat_axis=0, tiled=True
     ).reshape(2 * BLOCK, half)
 
+    returned, r2, l2, r3, l3 = lax.optimization_barrier((returned, r2, l2, r3, l3))
+
     square = struct((PAIRS, embed), F32)
     line = struct((1, PAIRS), F32)
     at = lax.axis_index("zl")

time: 263 us -> 255 us (0.970)
  waiting for transfers between devices: 82.7 us -> 75.2 us
    ppermute x3, waiting for transfers between devices: 24.7 us -> 5.04 us  [both(): lax.ppermute(left_going, 'zl', [(LOOP - 1 - i, LOOP - 1 - i - hops) for i...]
    reduce_scatter x1, waiting for transfers between devices: 4.39 us -> 12.7 us  [shards(): given = lax.psum_scatter(by_token, Z, scatter_dimension=0, tiled=True)]
    all_to_all x1, waiting for transfers between devices: 7.78 us -> 11.9 us  [shards(): lax.all_to_all(result.reshape(PLANE, 2 * SLOTS, half), FLAT, split_axis=0...]
  transfers between devices with their start and end apart: 15 -> 15, of which waited for: 10 -> 8; matrix products, arithmetic and copies ran while one was open for 7% -> 7% of each run, Pallas kernels for 15% -> 15%
where the time goes in v6:
time: 255 us; the launch traced here: 254 us
  waiting for transfers between devices  75.2 us (29%)
  blocking collectives  66.4 us (26%)
  Pallas kernels  45.1 us (18%)
  starting transfers between devices  33.3 us (13%)
  between operations  14 us (5%)
  matrix products  11.2 us (4%)
  local copies, waits for them, and re-layouts  5.3 us (2%)
  other arithmetic  3.05 us (1%)
    all_to_all x1, blocking collectives, shards(): lax.all_to_all(chosen.reshape(PLANE, PIECE, half), FLAT, split_axis=0, co...  33.5 us
    all_to_all x1, blocking collectives, shards(): lax.all_to_all(leaving.reshape(PLANE, PIECE, half), FLAT, split_axis=0, c...  32.9 us
    all_gather x1, waiting for transfers between devices, shards(): around = lax.all_gather(packed, Z, axis=0, tiled=True)  23.6 us
    reduce_scatter x1, waiting for transfers between devices, shards(): given = lax.psum_scatter(by_token, Z, scatter_dimension=0, tiled=True)  12.7 us
    all_to_all x1, waiting for transfers between devices, shards(): lax.all_to_all(result.reshape(PLANE, 2 * SLOTS, half), FLAT, split_axis=0...  11.9 us
    pallas_call x1, Pallas kernels, expert_right(): pl.pallas_call(expert_kernel, out_shape=(struct((RING * BLOCK, inner), BF...  11.4 us
    reduce_scatter x1, waiting for transfers between devices, shards(): lax.psum_scatter(term_right.reshape(2 * RING * BLOCK, half), Z, scatter_d...  10.6 us
    ppermute x3, starting transfers between devices, both(): lax.ppermute(right_going, 'zl', [(i, i + hops) for i in senders])  10.1 us
  transfers between devices with their start and end apart: 15, of which 8 were waited for; matrix products, arithmetic and copies ran while one was open for 7% of the time, Pallas kernels for 15%

profile of v6, /device:TPU:2, one launch (start us, length us, event | category | flops | bytes accessed | tf_op | source)
XLA Modules:
  0.0 253.6 jit_solution(2559418579372329754)
XLA Ops:
  7.2 2.7 %shard_map.156 = (bf16[272,640]{1,0:T(8,128)(2,1)}, bf16[384,640]{1,0:T(8,128)(2,1)}, f32[1,256]{1,0:T(1,128)}) custom-call(bf16[256,1280]{1,0:T(8,128)(2,1)} %tokens.5, s32[1,256]{1,0:T(1,128)} %bitcast.35, s32[1,64]{1,0:T(1,128)} %bitcast.36), custom_call_target="tpu_custom_call" | custom-call | flops 268435456 | bytes 4194304 | tf_op jit(solution)/shard_map/pallas_call | solution.py:394
  9.9 2.0 reshape.62
  11.8 7.6 %all-to-all-start = ((bf16[32,12,640]{2,1,0:T(8,128)(2,1)}), bf16[32,12,640]{2,1,0:T(8,128)(2,1)S(1)}, u32[]{:S(2)}, u32[]{:S(2)}) async-start(bf16[32,12,640]{2,1,0:T(8,128)(2,1)} %reshape.62), calls=%async_computation | async-start | bytes 1310720 | tf_op jit(solution)/shard_map/all_to_all | solution.py:417
  19.5 0.0 all-gather.5.cloned.1.call-start
  19.5 3.4 %shard_map.158.own = bf16[272,1024]{1,0:T(8,128)(2,1)} custom-call(bf16[127,1280]{1,0:T(8,128)(2,1)} %pooled.1, bf16[1280,1024]{1,0:T(8,128)(2,1)} %head.5, bf16[128,1024]{1,0:T(8,128)(2,1)} %text_embed.1, s32[1,128]{1,0:T(1,128)} %bitcast.30), custom_call_target="tpu_custom_call" | custom-call | flops 268435456 | bytes 4194304 | tf_op jit(solution)/shard_map/pallas_call | solution.py:312
  22.9 8.5 %all-to-all-done = bf16[32,12,640]{2,1,0:T(8,128)(2,1)S(1)} async-done(((bf16[32,12,640]{2,1,0:T(8,128)(2,1)}), bf16[32,12,640]{2,1,0:T(8,128)(2,1)S(1)}, u32[]{:S(2)}, u32[]{:S(2)}) %all-to-all-start) | async-done | bytes 491552 | tf_op jit(solution)/shard_map/all_to_all | solution.py:417
  31.4 0.1 reshape.63.rows
  31.5 1.2 shard_map.157
  32.7 23.6 %all-gather.3.cloned.1.call-done.gathered = bf16[2176,640]{1,0:T(8,128)(2,1)} async-done(((bf16[272,640]{1,0:T(8,128)(2,1)}), bf16[2176,640]{1,0:T(8,128)(2,1)}) %all-gather.3.cloned.1.call-update) | async-done | bytes 2785296 | tf_op jit(solution)/shard_map/all_gather | solution.py:416
  56.3 0.0 reduce-scatter.3.cloned.1.call-start
  56.4 5.0 %shard_map.159 = (bf16[1536,640]{1,0:T(8,128)(2,1)}, f32[8,256]{1,0:T(8,128)}) custom-call(bf16[2176,640]{1,0:T(8,128)(2,1)} %all-gather.3.cloned.1.call-done.gathered, s32[1,1]{1,0:T(1,128)} %bitcast.6.side, bf16[384,384]{1,0:T(8,128)(2,1)} %constant.22.clone.swap), custom_call_target="tpu_custom_call" | custom-call | flops 1073741824 | bytes 4194304 | tf_op jit(solution)/shard_map/pallas_call | solution.py:426
  61.4 33.5 %all_to_all.20 = bf16[32,48,640]{2,1,0:T(8,128)(2,1)S(1)} all-to-all(bf16[32,48,640]{2,1,0:T(8,128)(2,1)} %bitcast.27), channel_id=1, replica_groups=mesh['zh'=2,'y'=4,'x'=4,'c'=2,'zl'=4] {'y','x','c'}, dimensions={0} | all-to-all | bytes 3932160 | tf_op jit(solution)/shard_map/all_to_all | solution.py:432
  94.9 1.3 shard_map.160
  96.2 0.7 copy-done.15
  96.9 5.3 %fusion.1.partial = f32[1536,1280]{1,0:T(8,128)} fusion(bf16[1536,640]{1,0:T(8,128)(2,1)S(1)} %shard_map.160, bf16[1,1280,1280]{2,1,0:T(8,128)(2,1)S(1)} %copy-done.15), kind=kOutput, calls=%fused_computation.2 | convolution fusion | flops 2516582400 | bytes 11468800 | tf_op jit(solution)/shard_map/dot_general | solution.py:58
  102.2 3.6 %collective-permute-start = (bf16[272,1024]{1,0:T(8,128)(2,1)S(1)}, bf16[272,1024]{1,0:T(8,128)(2,1)S(1)}, u32[]{:S(2)}, u32[]{:S(2)}) collective-permute-start(bf16[272,1024]{1,0:T(8,128)(2,1)S(1)} %copy-done), channel_id=1, source_target_pairs={{0,1},{1,2},{2,3},{4,5},{5,6},{6,7},{8,9},{9,10},{10,11},{12,13},{... | collective-permute-start | bytes 1671176 | tf_op jit(solution)/shard_map/ppermute | solution.py:412
  105.7 1.3 collective-permute-start.1
  107.0 2.9 %all-gather.5.cloned.1.call-done = bf16[3072,640]{1,0:T(8,128)(2,1)} async-done(((bf16[384,640]{1,0:T(8,128)(2,1)}), bf16[3072,640]{1,0:T(8,128)(2,1)}) %all-gather.5.cloned.1.call-update) | async-done | bytes 3932176 | tf_op jit(solution)/shard_map/all_gather | solution.py:424
  110.0 11.4 %shard_map.161 = (bf16[1536,1280]{1,0:T(8,128)(2,1)}, bf16[8,2,192,640]{3,2,1,0:T(8,128)(2,1)}) custom-call(s32[1]{0:T(128)} %bitcast.1.side, bf16[8,2,192,640]{3,2,1,0:T(8,128)(2,1)} %bitcast.32, f32[1536,1280]{1,0:T(8,128)} %fusion.1.partial, bf16[1280,1280]{1,0:T(8,128)(2,1)} %bitcast.33, bf16[1280,1280]{1,0:T(8,128)(2,1)} %bitcast.34), custom_call_target="tpu_custom_call" | custom-call | flops 5033164800 | bytes 20971520 | tf_op jit(solution)/shard_map/pallas_call | solution.py:186
  121.4 0.7 collective-permute-done.1
  122.1 0.2 reduce-scatter.5.cloned.1.call-start
  122.3 5.9 %convolution_convert_fusion.rows = bf16[1536,640]{1,0:T(8,128)(2,1)S(1)} fusion(bf16[1536,1280]{1,0:T(8,128)(2,1)} %get-tuple-element.55, bf16[1,1280,1280]{2,1,0:T(8,128)(2,1)} %param.18), kind=kOutput, calls=%fused_computation | convolution fusion | flops 2517565440 | bytes 7536640 | tf_op jit(solution)/shard_map/dot_general | solution.py:62
  128.3 1.3 shard_map.162
  129.5 32.9 %all_to_all.21 = bf16[32,48,640]{2,1,0:T(8,128)(2,1)} all-to-all(bf16[32,48,640]{2,1,0:T(8,128)(2,1)S(1)} %bitcast.24), channel_id=1, replica_groups=mesh['zh'=2,'y'=4,'x'=4,'c'=2,'zl'=4] {'y','x','c'}, dimensions={0} | all-to-all | bytes 3932160 | tf_op jit(solution)/shard_map/all_to_all | solution.py:454
  162.5 5.3 %shard_map.163 = bf16[2048,640]{1,0:T(8,128)(2,1)} custom-call(bf16[1536,640]{1,0:T(8,128)(2,1)} %bitcast.25, bf16[384,384]{1,0:T(8,128)(2,1)} %constant.22.clone.swap, f32[8,256]{1,0:T(8,128)} %get-tuple-element.56.target), custom_call_target="tpu_custom_call" | custom-call | flops 1073741824 | bytes 4194304 | tf_op jit(solution)/shard_map/pallas_call | solution.py:457
  167.8 10.6 %reduce-scatter.3.cloned.1.call-done.rows = bf16[384,640]{1,0:T(8,128)(2,1)} async-done(((bf16[3072,640]{1,0:T(8,128)(2,1)}), bf16[384,640]{1,0:T(8,128)(2,1)}) %reduce-scatter.3.cloned.1.call-update) | async-done | bytes 491536 | tf_op jit(solution)/shard_map/reduce_scatter | solution.py:447
  178.3 0.8 collective-permute-start.2
  179.2 1.3 collective-permute-start.3
  180.5 5.7 %collective-permute-start.4 = (bf16[272,1024]{1,0:T(8,128)(2,1)S(1)}, bf16[272,1024]{1,0:T(8,128)(2,1)}, u32[]{:S(2)}, u32[]{:S(2)}) collective-permute-start(bf16[272,1024]{1,0:T(8,128)(2,1)S(1)} %copy-done), channel_id=1, source_target_pairs={{0,3},{4,7},{8,11},{12,15},{16,19},{20,23},{24,27},{28,31},{32,35}... | collective-permute-start | bytes 1671176 | tf_op jit(solution)/shard_map/ppermute | solution.py:412
  186.2 1.3 collective-permute-start.5
  187.5 0.4 shard_map.164
  187.9 0.9 reshape.72
  188.8 7.4 %all-to-all-start.3 = ((bf16[32,12,640]{2,1,0:T(8,128)(2,1)}), bf16[32,12,640]{2,1,0:T(8,128)(2,1)S(1)}, u32[]{:S(2)}, u32[]{:S(2)}) async-start(bf16[32,12,640]{2,1,0:T(8,128)(2,1)} %reshape.72), calls=%async_computation.4 | async-start | bytes 1310720 | tf_op jit(solution)/shard_map/all_to_all | solution.py:470
  196.3 11.9 %all-to-all-done.3 = bf16[32,12,640]{2,1,0:T(8,128)(2,1)S(1)} async-done(((bf16[32,12,640]{2,1,0:T(8,128)(2,1)}), bf16[32,12,640]{2,1,0:T(8,128)(2,1)S(1)}, u32[]{:S(2)}, u32[]{:S(2)}) %all-to-all-start.3) | async-done | bytes 491552 | tf_op jit(solution)/shard_map/all_to_all | solution.py:470
  208.2 0.9 reshape.73.returned
  209.1 4.3 %collective-permute-done.3 = bf16[272,1024]{1,0:T(8,128)(2,1)S(1)} collective-permute-done((bf16[272,1024]{1,0:T(8,128)(2,1)}, bf16[272,1024]{1,0:T(8,128)(2,1)S(1)}, u32[]{:S(2)}, u32[]{:S(2)}) %collective-permute-start.3) | collective-permute-done | bytes 557088 | tf_op jit(solution)/shard_map/ppermute | solution.py:413
  213.4 2.9 %shard_map.166 = (bf16[256,1280]{1,0:T(8,128)(2,1)}, f32[16,1024]{1,0:T(8,128)}) custom-call(bf16[256,1280]{1,0:T(8,128)(2,1)} %tokens.5, f32[1,256]{1,0:T(1,128)} %get-tuple-element.71.position, f32[1,256]{1,0:T(1,128)} %bitcast.28, bf16[384,640]{1,0:T(8,128)(2,1)} %reshape.73.returned, bf16[1280,1024]{1,0:T(8,128)(2,1)} %head.5), custom_call_target="tpu_custom_call" | custom-call | flops 268435456 | bytes 4194304 | tf_op jit(solution)/shard_map/pallas_call | solution.py:260
  216.3 0.9 broadcast_select_fusion.1.s2
  217.2 2.2 broadcast_select_fusion
  219.4 4.4 %shard_map.165 = (f32[1,128]{1,0:T(1,128)}, f32[128,1024]{1,0:T(8,128)}, f32[128,1024]{1,0:T(8,128)}) custom-call(bf16[272,1024]{1,0:T(8,128)(2,1)} %shard_map.158.own, bf16[272,1024]{1,0:T(8,128)(2,1)} %get-tuple-element.87.s1, bf16[272,1024]{1,0:T(8,128)(2,1)} %broadcast_select_fusion.1.s2, bf16[272,1024]{1,0:T(8,128)(2,1)} %get-tuple-element.86.s3), custom_call_target="tpu_custom_call" | custom-call | flops 1073741824 | bytes 4194304 | tf_op jit(solution)/shard_map/pallas_call | solution.py:485
  223.8 12.7 %reduce-scatter.5.cloned.1.call-done.given = bf16[256,640]{1,0:T(8,128)(2,1)} async-done(((bf16[2048,640]{1,0:T(8,128)(2,1)}), bf16[256,640]{1,0:T(8,128)(2,1)}) %reduce-scatter.5.cloned.1.call-update) | async-done | bytes 327696 | tf_op jit(solution)/shard_map/reduce_scatter | solution.py:468
  236.5 2.7 %shard_map.167 = (bf16[256,1280]{1,0:T(8,128)(2,1)}, bf16[1,1152]{1,0:T(2,128)(2,1)}) custom-call(bf16[256,1280]{1,0:T(8,128)(2,1)} %tokens.5, f32[1,256]{1,0:T(1,128)} %bitcast.29, bf16[256,640]{1,0:T(8,128)(2,1)} %reduce-scatter.5.cloned.1.call-done.given, bf16[1280,1024]{1,0:T(8,128)(2,1)} %head.5, ...), custom_call_target="tpu_custom_call", output_to_operand_aliasing={{0}: (6, {})} | custom-call | flops 268435456 | bytes 4194304 | tf_op jit(solution)/shard_map/pallas_call | solution.py:279
  239.2 0.3 collective-permute-start.6
  239.4 2.2 collective-permute-start.7
  241.6 1.5 collective-permute-start.8
  243.2 0.7 copy-done.11
  243.9 1.8 shard_map.168
  245.7 1.3 shard_map.169
  (42 shorter events, 0.2 us)
Async XLA Ops:
  7.2 49.1 %all-gather.3.cloned.1.call-start = ((), (), s32[]{:S(2)}) async-start(), calls=%async_computation.6 | async-start | bytes 3133440 | tf_op jit(solution)/shard_map/all_gather | solution.py:416
  11.8 19.5 %all-to-all-start = ((bf16[32,12,640]{2,1,0:T(8,128)(2,1)}), bf16[32,12,640]{2,1,0:T(8,128)(2,1)S(1)}, u32[]{:S(2)}, u32[]{:S(2)}) async-start(bf16[32,12,640]{2,1,0:T(8,128)(2,1)} %reshape.62), calls=%async_computation | async-start | bytes 1310720 | tf_op jit(solution)/shard_map/all_to_all | solution.py:417
  19.5 12.0 %copy-start.10 = (bf16[384,384]{1,0:T(8,128)(2,1)S(1)}, bf16[384,384]{1,0:T(8,128)(2,1)}, u32[]{:S(2)}) copy-start(bf16[384,384]{1,0:T(8,128)(2,1)} %constant.23.clone.matrix) | copy-start | bytes 884740
  19.5 90.5 %all-gather.5.cloned.1.call-start = ((), (), s32[]{:S(2)}) async-start(), calls=%async_computation.7 | async-start | bytes 4423680 | tf_op jit(solution)/shard_map/all_gather | solution.py:424
  56.3 122.0 %reduce-scatter.3.cloned.1.call-start = ((), (), s32[]{:S(2)}) async-start(), calls=%async_computation.8 | async-start | bytes 4423680 | tf_op jit(solution)/shard_map/reduce_scatter | solution.py:447
  61.4 33.5 %copy-start.2 = (bf16[384,384]{1,0:T(8,128)(2,1)S(1)}, bf16[384,384]{1,0:T(8,128)(2,1)}, u32[]{:S(2)}) copy-start(bf16[384,384]{1,0:T(8,128)(2,1)} %constant.22.clone.swap) | copy-start | bytes 884740
  94.9 2.0 copy-start.15
  96.9 5.3 %copy-start = (bf16[272,1024]{1,0:T(8,128)(2,1)S(1)}, bf16[272,1024]{1,0:T(8,128)(2,1)}, u32[]{:S(2)}) copy-start(bf16[272,1024]{1,0:T(8,128)(2,1)} %shard_map.158.own) | copy-start | bytes 1671172
  102.2 19.2 %collective-permute-start = (bf16[272,1024]{1,0:T(8,128)(2,1)S(1)}, bf16[272,1024]{1,0:T(8,128)(2,1)S(1)}, u32[]{:S(2)}, u32[]{:S(2)}) collective-permute-start(bf16[272,1024]{1,0:T(8,128)(2,1)S(1)} %copy-done), channel_id=1, source_target_pairs={{0,1},{1,2},{2,3},{4,5},{5,6},{6,7},{8,9},{9,10},{10,11},{12,13},{... | collective-permute-start | bytes 1671176 | tf_op jit(solution)/shard_map/ppermute | solution.py:412
  105.7 16.4 %collective-permute-start.1 = (bf16[272,1024]{1,0:T(8,128)(2,1)S(1)}, bf16[272,1024]{1,0:T(8,128)(2,1)S(1)}, u32[]{:S(2)}, u32[]{:S(2)}) collective-permute-start(bf16[272,1024]{1,0:T(8,128)(2,1)S(1)} %copy-done), channel_id=1, source_target_pairs={{3,2},{2,1},{1,0},{7,6},{6,5},{5,4},{11,10},{10,9},{9,8},{15,14},{... | collective-permute-start | bytes 1671176 | tf_op jit(solution)/shard_map/ppermute | solution.py:413
  122.1 6.2 %copy-start.13 = (bf16[272,1024]{1,0:T(8,128)(2,1)}, bf16[272,1024]{1,0:T(8,128)(2,1)S(1)}, u32[]{:S(2)}) copy-start(bf16[272,1024]{1,0:T(8,128)(2,1)S(1)} %collective-permute-done.1) | copy-start | bytes 1671172
  122.1 114.3 %reduce-scatter.5.cloned.1.call-start = ((), (), s32[]{:S(2)}) async-start(), calls=%async_computation.9 | async-start | bytes 2949120 | tf_op jit(solution)/shard_map/reduce_scatter | solution.py:468
  162.5 25.0 %copy-start.9 = (bf16[384,384]{1,0:T(8,128)(2,1)S(1)}, bf16[384,384]{1,0:T(8,128)(2,1)}, u32[]{:S(2)}) copy-start(bf16[384,384]{1,0:T(8,128)(2,1)} %constant.24.clone.matrix) | copy-start | bytes 884740
  178.3 9.1 %copy-start.8 = (bf16[384,640]{1,0:T(8,128)(2,1)S(1)}, bf16[384,640]{1,0:T(8,128)(2,1)}, u32[]{:S(2)}) copy-start(bf16[384,640]{1,0:T(8,128)(2,1)} %reduce-scatter.3.cloned.1.call-done.rows) | copy-start | bytes 1474564
  178.3 30.7 %collective-permute-start.2 = (bf16[272,1024]{1,0:T(8,128)(2,1)S(1)}, bf16[272,1024]{1,0:T(8,128)(2,1)S(1)}, u32[]{:S(2)}, u32[]{:S(2)}) collective-permute-start(bf16[272,1024]{1,0:T(8,128)(2,1)S(1)} %collective-permute-done), channel_id=1, source_target_pairs={{1,2},{2,3},{5,6},{6,7},{9,10},{10,11},{13,14},{14,15},{17,18},{18... | collective-permute-start | bytes 1671176 | tf_op jit(solution)/shard_map/ppermute | solution.py:412
  179.2 34.2 %collective-permute-start.3 = (bf16[272,1024]{1,0:T(8,128)(2,1)}, bf16[272,1024]{1,0:T(8,128)(2,1)S(1)}, u32[]{:S(2)}, u32[]{:S(2)}) collective-permute-start(bf16[272,1024]{1,0:T(8,128)(2,1)} %copy-done.13), channel_id=1, source_target_pairs={{2,1},{1,0},{6,5},{5,4},{10,9},{9,8},{14,13},{13,12},{18,17},{17,1... | collective-permute-start | bytes 1671176 | tf_op jit(solution)/shard_map/ppermute | solution.py:413
  180.5 33.0 %collective-permute-start.4 = (bf16[272,1024]{1,0:T(8,128)(2,1)S(1)}, bf16[272,1024]{1,0:T(8,128)(2,1)}, u32[]{:S(2)}, u32[]{:S(2)}) collective-permute-start(bf16[272,1024]{1,0:T(8,128)(2,1)S(1)} %copy-done), channel_id=1, source_target_pairs={{0,3},{4,7},{8,11},{12,15},{16,19},{20,23},{24,27},{28,31},{32,35}... | collective-permute-start | bytes 1671176 | tf_op jit(solution)/shard_map/ppermute | solution.py:412
  186.2 27.3 %collective-permute-start.5 = (bf16[272,1024]{1,0:T(8,128)(2,1)S(1)}, bf16[272,1024]{1,0:T(8,128)(2,1)}, u32[]{:S(2)}, u32[]{:S(2)}) collective-permute-start(bf16[272,1024]{1,0:T(8,128)(2,1)S(1)} %copy-done), channel_id=1, source_target_pairs={{3,0},{7,4},{11,8},{15,12},{19,16},{23,20},{27,24},{31,28},{35,32}... | collective-permute-start | bytes 1671176 | tf_op jit(solution)/shard_map/ppermute | solution.py:413
  188.8 19.3 %all-to-all-start.3 = ((bf16[32,12,640]{2,1,0:T(8,128)(2,1)}), bf16[32,12,640]{2,1,0:T(8,128)(2,1)S(1)}, u32[]{:S(2)}, u32[]{:S(2)}) async-start(bf16[32,12,640]{2,1,0:T(8,128)(2,1)} %reshape.72), calls=%async_computation.4 | async-start | bytes 1310720 | tf_op jit(solution)/shard_map/all_to_all | solution.py:470
  209.1 8.1 %copy-start.14 = (bf16[272,1024]{1,0:T(8,128)(2,1)S(1)}, bf16[272,1024]{1,0:T(8,128)(2,1)}, u32[]{:S(2)}) copy-start(bf16[272,1024]{1,0:T(8,128)(2,1)} %copy-done.13) | copy-start | bytes 1671172
  223.8 19.4 %copy-start.1 = (bf16[272,1024]{1,0:T(8,128)(2,1)S(1)}, bf16[272,1024]{1,0:T(8,128)(2,1)}, u32[]{:S(2)}) copy-start(bf16[272,1024]{1,0:T(8,128)(2,1)} %shard_map.158.own) | copy-start | bytes 1671172
  223.8 19.4 %copy-start.3 = (bf16[272,1024]{1,0:T(8,128)(2,1)S(1)}, bf16[272,1024]{1,0:T(8,128)(2,1)}, u32[]{:S(2)}) copy-start(bf16[272,1024]{1,0:T(8,128)(2,1)} %broadcast_select_fusion.1.s2) | copy-start | bytes 1671172
  223.8 19.4 %copy-start.4 = (bf16[272,1024]{1,0:T(8,128)(2,1)S(1)}, bf16[272,1024]{1,0:T(8,128)(2,1)}, u32[]{:S(2)}) copy-start(bf16[272,1024]{1,0:T(8,128)(2,1)} %get-tuple-element.86.s3) | copy-start | bytes 1671172
  223.8 19.4 %copy-start.5 = (bf16[272,1024]{1,0:T(8,128)(2,1)S(1)}, bf16[272,1024]{1,0:T(8,128)(2,1)}, u32[]{:S(2)}) copy-start(bf16[272,1024]{1,0:T(8,128)(2,1)} %get-tuple-element.87.s1) | copy-start | bytes 1671172
  223.8 19.4 %copy-start.6 = (f32[128,1024]{1,0:T(8,128)S(1)}, f32[128,1024]{1,0:T(8,128)}, u32[]{:S(2)}) copy-start(f32[128,1024]{1,0:T(8,128)} %get-tuple-element.82.image_acc) | copy-start | bytes 1572868
  223.8 19.4 %copy-start.12 = (f32[1,128]{1,0:T(1,128)S(1)}, f32[1,128]{1,0:T(1,128)}, u32[]{:S(2)}) copy-start(f32[1,128]{1,0:T(1,128)} %get-tuple-element.81.loss) | copy-start | bytes 1540
  236.5 9.2 %copy-start.7 = (f32[128,1024]{1,0:T(8,128)S(1)}, f32[128,1024]{1,0:T(8,128)}, u32[]{:S(2)}) copy-start(f32[128,1024]{1,0:T(8,128)} %get-tuple-element.85.text_acc) | copy-start | bytes 1572868
  239.2 6.5 %collective-permute-start.6 = (bf16[1,1152]{1,0:T(2,128)(2,1)}, bf16[1,1152]{1,0:T(2,128)(2,1)S(1)}, u32[]{:S(2)}, u32[]{:S(2)}) collective-permute-start(bf16[1,1152]{1,0:T(2,128)(2,1)} %get-tuple-element.80.own_image.i0), channel_id=1, source_target_pairs={{0,1},{1,2},{2,3},{3,0},{4,5},{5,6},{6,7},{7,4},{8,9},{9,10},{10,1... | collective-permute-start | bytes 6920 | tf_op jit(solution)/shard_map/ppermute | solution.py:405
  239.4 6.3 %collective-permute-start.7 = (bf16[1,1152]{1,0:T(2,128)(2,1)}, bf16[1,1152]{1,0:T(2,128)(2,1)S(1)}, u32[]{:S(2)}, u32[]{:S(2)}) collective-permute-start(bf16[1,1152]{1,0:T(2,128)(2,1)} %get-tuple-element.80.own_image.i0), channel_id=1, source_target_pairs={{0,2},{1,3},{2,0},{3,1},{4,6},{5,7},{6,4},{7,5},{8,10},{9,11},{10,... | collective-permute-start | bytes 6920 | tf_op jit(solution)/shard_map/ppermute | solution.py:405
  241.6 4.1 %collective-permute-start.8 = (bf16[1,1152]{1,0:T(2,128)(2,1)}, bf16[1,1152]{1,0:T(2,128)(2,1)S(1)}, u32[]{:S(2)}, u32[]{:S(2)}) collective-permute-start(bf16[1,1152]{1,0:T(2,128)(2,1)} %get-tuple-element.80.own_image.i0), channel_id=1, source_target_pairs={{0,3},{1,0},{2,1},{3,2},{4,7},{5,4},{6,5},{7,6},{8,11},{9,8},{10,9... | collective-permute-start | bytes 6920 | tf_op jit(solution)/shard_map/ppermute | solution.py:405
  243.2 0.7 copy-start.11
Sparse Core Ops, SparseCore 0:
  10.4 45.8 all-gather.2
  58.7 51.2 all-gather.4
  122.2 56.0 reduce-scatter.2
  180.7 55.7 reduce-scatter.4

commit v7 on v6

--- a/solution.py
+++ b/solution.py
@@ -444,12 +444,16 @@
         side.reshape(1), right.reshape(RING, 2, BLOCK, half), partial, first, second
     )
     hidden, term_right, r1, l1 = lax.optimization_barrier((hidden, term_right, r1, l1))
+    right_texts, left_texts = both(r1[:PAIRS], l1[:PAIRS], (1, 2), 1)
     result = lax.psum_scatter(
         term_right.reshape(2 * RING * BLOCK, half), Z, scatter_dimension=0, tiled=True
     )
     term_left = lax.optimization_barrier(dot_t(hidden, second[:half]).astype(BF16))
     leaving = call(unspread_kernel, struct((RING * BLOCK, half), BF16), flops=1 << 30, vmem=24)(
         term_left, swap
+    )
+    leaving, right_texts, left_texts = lax.optimization_barrier(
+        (leaving, right_texts, left_texts)
     )
     back = lax.all_to_all(
         leaving.reshape(PLANE, PIECE, half), FLAT, split_axis=0, concat_axis=0, tiled=True
@@ -460,10 +464,10 @@
         scratch=[pltpu.VMEM((RING * BLOCK, half), BF16)],
         flops=1 << 30,
     )(back, swap, target)
-    by_token, result, r1, l1, own_pairs = lax.optimization_barrier(
-        (by_token, result, r1, l1, own_pairs)
-    )
-    r2, l2 = both(r1, l1, (1, 2), 1)
+    by_token, result, right_rest, left_rest, own_pairs = lax.optimization_barrier(
+        (by_token, result, r1[PAIRS:], l1[PAIRS:], own_pairs)
+    )
+    r2, l2 = both(right_rest, left_rest, (1, 2), 1)
     r3, l3 = both(own_pairs, own_pairs, (0,), 3)
     given = lax.psum_scatter(by_token, Z, scatter_dimension=0, tiled=True)
     result = call(turn_kernel, struct((2 * BLOCK, half), BF16), flops=1 << 28, vmem=24)(result, together)
@@ -472,6 +476,8 @@
     ).reshape(2 * BLOCK, half)
 
     returned, r2, l2, r3, l3 = lax.optimization_barrier((returned, r2, l2, r3, l3))
+    r2 = jnp.concatenate([right_texts, r2], axis=0)
+    l2 = jnp.concatenate([left_texts, l2], axis=0)
 
     square = struct((PAIRS, embed), F32)
     line = struct((1, PAIRS), F32)

time: 255 us -> 254 us (level)
  blocking collectives: 66.4 us -> 33.5 us
  waiting for transfers between devices: 75.2 us -> 94.8 us
  starting transfers between devices: 33.3 us -> 40.6 us
  local copies, waits for them, and re-layouts: 5.3 us -> 9.94 us
    all_to_all x1 -> x0, blocking collectives: 32.9 us -> none  [shards(): lax.all_to_all(leaving.reshape(PLANE, PIECE, half), FLAT, split_axis=0, c...]
    all_to_all x0 -> x1, waiting for transfers between devices: none -> 23.9 us  [shards(): lax.all_to_all(leaving.reshape(PLANE, PIECE, half), FLAT, split_axis=0, c...]
    all_to_all x0 -> x1, starting transfers between devices: none -> 7.78 us  [shards(): lax.all_to_all(leaving.reshape(PLANE, PIECE, half), FLAT, split_axis=0, c...]
    reduce_scatter x1, waiting for transfers between devices: 10.6 us -> 2.9 us  [shards(): lax.psum_scatter(term_right.reshape(2 * RING * BLOCK, half), Z, scatter_d...]
    ppermute x3 -> x4, waiting for transfers between devices: 5.04 us -> 11.6 us  [both(): lax.ppermute(left_going, 'zl', [(LOOP - 1 - i, LOOP - 1 - i - hops) for i...]
    reduce_scatter x1, waiting for transfers between devices: 12.7 us -> 9.51 us  [shards(): given = lax.psum_scatter(by_token, Z, scatter_dimension=0, tiled=True)]
    ppermute x3 -> x4, starting transfers between devices: 3.86 us -> 5.35 us  [both(): lax.ppermute(left_going, 'zl', [(LOOP - 1 - i, LOOP - 1 - i - hops) for i...]
    ppermute x3 -> x4, starting transfers between devices: 10.1 us -> 9.98 us  [both(): lax.ppermute(right_going, 'zl', [(i, i + hops) for i in senders])]
  transfers between devices with their start and end apart: 15 -> 18, of which waited for: 8 -> 12; matrix products, arithmetic and copies ran while one was open for 7% -> 8% of each run, Pallas kernels for 15% -> 16%
where the time goes in v7:
time: 254 us; the launch traced here: 253 us
  waiting for transfers between devices  94.8 us (37%)
  Pallas kernels  46.6 us (18%)
  starting transfers between devices  40.6 us (16%)
  blocking collectives  33.5 us (13%)
  between operations  14 us (6%)
  matrix products  11.2 us (4%)
  local copies, waits for them, and re-layouts  9.94 us (4%)
    all_to_all x1, blocking collectives, shards(): lax.all_to_all(chosen.reshape(PLANE, PIECE, half), FLAT, split_axis=0, co...  33.5 us
    all_to_all x1, waiting for transfers between devices, shards(): lax.all_to_all(leaving.reshape(PLANE, PIECE, half), FLAT, split_axis=0, c...  23.9 us
    all_gather x1, waiting for transfers between devices, shards(): around = lax.all_gather(packed, Z, axis=0, tiled=True)  23.6 us
    ppermute x4, waiting for transfers between devices, both(): lax.ppermute(left_going, 'zl', [(LOOP - 1 - i, LOOP - 1 - i - hops) for i...  11.6 us
    pallas_call x1, Pallas kernels, expert_right(): pl.pallas_call(expert_kernel, out_shape=(struct((RING * BLOCK, inner), BF...  11.4 us
    ppermute x4, starting transfers between devices, both(): lax.ppermute(right_going, 'zl', [(i, i + hops) for i in senders])  9.98 us
    all_to_all x1, waiting for transfers between devices, shards(): lax.all_to_all(result.reshape(PLANE, 2 * SLOTS, half), FLAT, split_axis=0...  9.9 us
    reduce_scatter x1, waiting for transfers between devices, shards(): given = lax.psum_scatter(by_token, Z, scatter_dimension=0, tiled=True)  9.51 us
  transfers between devices with their start and end apart: 18, of which 12 were waited for; matrix products, arithmetic and copies ran while one was open for 8% of the time, Pallas kernels for 16%

profile of v7, /device:TPU:2, one launch (start us, length us, event | category | flops | bytes accessed | tf_op | source)
XLA Modules:
  0.0 252.7 jit_solution(5047095957700704918)
XLA Ops:
  7.2 2.7 %shard_map.156 = (bf16[272,640]{1,0:T(8,128)(2,1)}, bf16[384,640]{1,0:T(8,128)(2,1)}, f32[1,256]{1,0:T(1,128)}) custom-call(bf16[256,1280]{1,0:T(8,128)(2,1)} %tokens.5, s32[1,256]{1,0:T(1,128)} %bitcast.34, s32[1,64]{1,0:T(1,128)} %bitcast.35), custom_call_target="tpu_custom_call" | custom-call | flops 268435456 | bytes 4194304 | tf_op jit(solution)/shard_map/pallas_call | solution.py:394
  9.9 2.0 reshape.62
  11.8 7.6 %all-to-all-start = ((bf16[32,12,640]{2,1,0:T(8,128)(2,1)}), bf16[32,12,640]{2,1,0:T(8,128)(2,1)S(1)}, u32[]{:S(2)}, u32[]{:S(2)}) async-start(bf16[32,12,640]{2,1,0:T(8,128)(2,1)} %reshape.62), calls=%async_computation | async-start | bytes 1310720 | tf_op jit(solution)/shard_map/all_to_all | solution.py:417
  19.5 3.4 %shard_map.158.own = bf16[272,1024]{1,0:T(8,128)(2,1)} custom-call(bf16[127,1280]{1,0:T(8,128)(2,1)} %pooled.1, bf16[1280,1024]{1,0:T(8,128)(2,1)} %head.5, bf16[128,1024]{1,0:T(8,128)(2,1)} %text_embed.1, s32[1,128]{1,0:T(1,128)} %bitcast.29), custom_call_target="tpu_custom_call" | custom-call | flops 268435456 | bytes 4194304 | tf_op jit(solution)/shard_map/pallas_call | solution.py:312
  22.9 8.5 %all-to-all-done = bf16[32,12,640]{2,1,0:T(8,128)(2,1)S(1)} async-done(((bf16[32,12,640]{2,1,0:T(8,128)(2,1)}), bf16[32,12,640]{2,1,0:T(8,128)(2,1)S(1)}, u32[]{:S(2)}, u32[]{:S(2)}) %all-to-all-start) | async-done | bytes 491552 | tf_op jit(solution)/shard_map/all_to_all | solution.py:417
  31.5 1.2 shard_map.157
  32.7 23.6 %all-gather.3.cloned.1.call-done.gathered = bf16[2176,640]{1,0:T(8,128)(2,1)} async-done(((bf16[272,640]{1,0:T(8,128)(2,1)}), bf16[2176,640]{1,0:T(8,128)(2,1)}) %all-gather.3.cloned.1.call-update) | async-done | bytes 2785296 | tf_op jit(solution)/shard_map/all_gather | solution.py:416
  56.4 5.0 %shard_map.159 = (bf16[1536,640]{1,0:T(8,128)(2,1)}, f32[8,256]{1,0:T(8,128)}) custom-call(bf16[2176,640]{1,0:T(8,128)(2,1)} %all-gather.3.cloned.1.call-done.gathered, s32[1,1]{1,0:T(1,128)} %bitcast.6.side, bf16[384,384]{1,0:T(8,128)(2,1)} %constant.22.clone.swap), custom_call_target="tpu_custom_call" | custom-call | flops 1073741824 | bytes 4194304 | tf_op jit(solution)/shard_map/pallas_call | solution.py:426
  61.4 33.5 %all_to_all.20 = bf16[32,48,640]{2,1,0:T(8,128)(2,1)S(1)} all-to-all(bf16[32,48,640]{2,1,0:T(8,128)(2,1)} %bitcast.26), channel_id=1, replica_groups=mesh['zh'=2,'y'=4,'x'=4,'c'=2,'zl'=4] {'y','x','c'}, dimensions={0} | all-to-all | bytes 3932160 | tf_op jit(solution)/shard_map/all_to_all | solution.py:432
  94.9 1.3 shard_map.160
  96.9 5.3 %fusion.1.partial = f32[1536,1280]{1,0:T(8,128)} fusion(bf16[1536,640]{1,0:T(8,128)(2,1)S(1)} %shard_map.160, bf16[1,1280,1280]{2,1,0:T(8,128)(2,1)S(1)} %copy-done.20), kind=kOutput, calls=%fused_computation.2 | convolution fusion | flops 2516582400 | bytes 11468800 | tf_op jit(solution)/shard_map/dot_general | solution.py:58
  102.2 3.6 %collective-permute-start = (bf16[272,1024]{1,0:T(8,128)(2,1)S(1)}, bf16[272,1024]{1,0:T(8,128)(2,1)S(1)}, u32[]{:S(2)}, u32[]{:S(2)}) collective-permute-start(bf16[272,1024]{1,0:T(8,128)(2,1)S(1)} %copy-done), channel_id=1, source_target_pairs={{0,1},{1,2},{2,3},{4,5},{5,6},{6,7},{8,9},{9,10},{10,11},{12,13},{... | collective-permute-start | bytes 1671176 | tf_op jit(solution)/shard_map/ppermute | solution.py:412
  105.7 1.3 collective-permute-start.1
  107.0 2.9 %all-gather.5.cloned.1.call-done = bf16[3072,640]{1,0:T(8,128)(2,1)} async-done(((bf16[384,640]{1,0:T(8,128)(2,1)}), bf16[3072,640]{1,0:T(8,128)(2,1)}) %all-gather.5.cloned.1.call-update) | async-done | bytes 3932176 | tf_op jit(solution)/shard_map/all_gather | solution.py:424
  110.0 11.4 %shard_map.161 = (bf16[1536,1280]{1,0:T(8,128)(2,1)}, bf16[8,2,192,640]{3,2,1,0:T(8,128)(2,1)}) custom-call(s32[1]{0:T(128)} %bitcast.1.side, bf16[8,2,192,640]{3,2,1,0:T(8,128)(2,1)} %bitcast.31, f32[1536,1280]{1,0:T(8,128)} %fusion.1.partial, bf16[1280,1280]{1,0:T(8,128)(2,1)} %bitcast.32, bf16[1280,1280]{1,0:T(8,128)(2,1)} %bitcast.33), custom_call_target="tpu_custom_call" | custom-call | flops 5033164800 | bytes 20971520 | tf_op jit(solution)/shard_map/pallas_call | solution.py:186
  121.4 0.7 collective-permute-done.1
  123.0 1.5 collective-permute-start.3
  124.5 5.9 %convolution_convert_fusion.rows = bf16[1536,640]{1,0:T(8,128)(2,1)S(1)} fusion(bf16[1536,1280]{1,0:T(8,128)(2,1)} %get-tuple-element.58, bf16[1,1280,1280]{2,1,0:T(8,128)(2,1)} %param.18), kind=kOutput, calls=%fused_computation | convolution fusion | flops 2517565440 | bytes 7536640 | tf_op jit(solution)/shard_map/dot_general | solution.py:62
  130.3 2.6 %shard_map.162 = bf16[1536,640]{1,0:T(8,128)(2,1)} custom-call(bf16[1536,640]{1,0:T(8,128)(2,1)S(1)} %convolution_convert_fusion.rows, bf16[384,384]{1,0:T(8,128)(2,1)S(1)} %copy-done.2), custom_call_target="tpu_custom_call" | custom-call | flops 1073741824 | bytes 4194304 | tf_op jit(solution)/shard_map/pallas_call | solution.py:452
  133.0 0.9 collective-permute-done.3
  133.9 0.7 copy-done.18
  134.6 7.8 %all-to-all-start.2 = ((bf16[32,48,640]{2,1,0:T(8,128)(2,1)}), bf16[32,48,640]{2,1,0:T(8,128)(2,1)S(1)}, u32[]{:S(2)}, u32[]{:S(2)}) async-start(bf16[32,48,640]{2,1,0:T(8,128)(2,1)} %bitcast.13), calls=%async_computation.2 | async-start | bytes 3932160 | tf_op jit(solution)/shard_map/all_to_all | solution.py:458
  142.4 0.8 slice.30
  143.2 1.7 slice.31
  144.9 23.9 %all-to-all-done.2 = bf16[32,48,640]{2,1,0:T(8,128)(2,1)S(1)} async-done(((bf16[32,48,640]{2,1,0:T(8,128)(2,1)}), bf16[32,48,640]{2,1,0:T(8,128)(2,1)S(1)}, u32[]{:S(2)}, u32[]{:S(2)}) %all-to-all-start.2) | async-done | bytes 1966112 | tf_op jit(solution)/shard_map/all_to_all | solution.py:458
  168.8 1.3 copy-done.13
  170.1 5.3 %shard_map.163 = bf16[2048,640]{1,0:T(8,128)(2,1)} custom-call(bf16[1536,640]{1,0:T(8,128)(2,1)} %bitcast.24, bf16[384,384]{1,0:T(8,128)(2,1)} %constant.22.clone.swap, f32[8,256]{1,0:T(8,128)} %get-tuple-element.62.target), custom_call_target="tpu_custom_call" | custom-call | flops 1073741824 | bytes 4194304 | tf_op jit(solution)/shard_map/pallas_call | solution.py:461
  175.4 2.9 %reduce-scatter.3.cloned.1.call-done.rows = bf16[384,640]{1,0:T(8,128)(2,1)} async-done(((bf16[3072,640]{1,0:T(8,128)(2,1)}), bf16[384,640]{1,0:T(8,128)(2,1)}) %reduce-scatter.3.cloned.1.call-update) | async-done | bytes 491536 | tf_op jit(solution)/shard_map/reduce_scatter | solution.py:448
  178.3 5.1 %collective-permute-start.6 = (bf16[272,1024]{1,0:T(8,128)(2,1)S(1)}, bf16[272,1024]{1,0:T(8,128)(2,1)S(1)}, u32[]{:S(2)}, u32[]{:S(2)}) collective-permute-start(bf16[272,1024]{1,0:T(8,128)(2,1)S(1)} %copy-done), channel_id=1, source_target_pairs={{0,3},{4,7},{8,11},{12,15},{16,19},{20,23},{24,27},{28,31},{32,35}... | collective-permute-start | bytes 1671176 | tf_op jit(solution)/shard_map/ppermute | solution.py:412
  183.4 1.3 collective-permute-start.7
  185.2 0.9 reshape.72
  186.1 7.4 %all-to-all-start.3 = ((bf16[32,12,640]{2,1,0:T(8,128)(2,1)}), bf16[32,12,640]{2,1,0:T(8,128)(2,1)S(1)}, u32[]{:S(2)}, u32[]{:S(2)}) async-start(bf16[32,12,640]{2,1,0:T(8,128)(2,1)} %reshape.72), calls=%async_computation.4 | async-start | bytes 1310720 | tf_op jit(solution)/shard_map/all_to_all | solution.py:474
  193.5 0.7 collective-permute-start.4
  194.2 1.3 collective-permute-start.5
  195.5 9.9 %all-to-all-done.3 = bf16[32,12,640]{2,1,0:T(8,128)(2,1)S(1)} async-done(((bf16[32,12,640]{2,1,0:T(8,128)(2,1)}), bf16[32,12,640]{2,1,0:T(8,128)(2,1)S(1)}, u32[]{:S(2)}, u32[]{:S(2)}) %all-to-all-start.3) | async-done | bytes 491552 | tf_op jit(solution)/shard_map/all_to_all | solution.py:474
  205.4 0.9 reshape.73.returned
  206.3 10.0 %collective-permute-done.5 = bf16[144,1024]{1,0:T(8,128)(2,1)S(1)} collective-permute-done((bf16[144,1024]{1,0:T(8,128)(2,1)}, bf16[144,1024]{1,0:T(8,128)(2,1)S(1)}, u32[]{:S(2)}, u32[]{:S(2)}) %collective-permute-start.5) | collective-permute-done | bytes 294944 | tf_op jit(solution)/shard_map/ppermute | solution.py:413
  216.3 2.9 %shard_map.166 = (bf16[256,1280]{1,0:T(8,128)(2,1)}, f32[16,1024]{1,0:T(8,128)}) custom-call(bf16[256,1280]{1,0:T(8,128)(2,1)} %tokens.5, f32[1,256]{1,0:T(1,128)} %get-tuple-element.77.position, f32[1,256]{1,0:T(1,128)} %bitcast.27, bf16[384,640]{1,0:T(8,128)(2,1)} %reshape.73.returned, bf16[1280,1024]{1,0:T(8,128)(2,1)} %head.5), custom_call_target="tpu_custom_call" | custom-call | flops 268435456 | bytes 4194304 | tf_op jit(solution)/shard_map/pallas_call | solution.py:260
  219.2 1.0 maximum_select_fusion.s2
  220.2 1.1 broadcast_select_fusion
  221.3 4.4 %shard_map.165 = (f32[1,128]{1,0:T(1,128)}, f32[128,1024]{1,0:T(8,128)}, f32[128,1024]{1,0:T(8,128)}) custom-call(bf16[272,1024]{1,0:T(8,128)(2,1)} %shard_map.158.own, bf16[272,1024]{1,0:T(8,128)(2,1)} %get-tuple-element.93.s1, bf16[272,1024]{1,0:T(8,128)(2,1)} %maximum_select_fusion.s2, bf16[272,1024]{1,0:T(8,128)(2,1)} %get-tuple-element.92.s3), custom_call_target="tpu_custom_call" | custom-call | flops 1073741824 | bytes 4194304 | tf_op jit(solution)/shard_map/pallas_call | solution.py:491
  225.7 9.5 %reduce-scatter.5.cloned.1.call-done.given = bf16[256,640]{1,0:T(8,128)(2,1)} async-done(((bf16[2048,640]{1,0:T(8,128)(2,1)}), bf16[256,640]{1,0:T(8,128)(2,1)}) %reduce-scatter.5.cloned.1.call-update) | async-done | bytes 327696 | tf_op jit(solution)/shard_map/reduce_scatter | solution.py:472
  235.3 2.8 %shard_map.167 = (bf16[256,1280]{1,0:T(8,128)(2,1)}, bf16[1,1152]{1,0:T(2,128)(2,1)}) custom-call(bf16[256,1280]{1,0:T(8,128)(2,1)} %tokens.5, f32[1,256]{1,0:T(1,128)} %bitcast.28, bf16[256,640]{1,0:T(8,128)(2,1)} %reduce-scatter.5.cloned.1.call-done.given, bf16[1280,1024]{1,0:T(8,128)(2,1)} %head.5, ...), custom_call_target="tpu_custom_call", output_to_operand_aliasing={{0}: (6, {})} | custom-call | flops 268435456 | bytes 4194304 | tf_op jit(solution)/shard_map/pallas_call | solution.py:279
  238.1 2.0 collective-permute-start.8
  241.1 1.8 shard_map.168
  242.9 0.9 collective-permute-done.8.i1
  243.8 1.1 collective-permute-done.9.i2
  244.8 1.3 shard_map.169
  (61 shorter events, 3.3 us)
Async XLA Ops:
  7.2 49.1 %all-gather.3.cloned.1.call-start = ((), (), s32[]{:S(2)}) async-start(), calls=%async_computation.6 | async-start | bytes 3133440 | tf_op jit(solution)/shard_map/all_gather | solution.py:416
  11.8 19.5 %all-to-all-start = ((bf16[32,12,640]{2,1,0:T(8,128)(2,1)}), bf16[32,12,640]{2,1,0:T(8,128)(2,1)S(1)}, u32[]{:S(2)}, u32[]{:S(2)}) async-start(bf16[32,12,640]{2,1,0:T(8,128)(2,1)} %reshape.62), calls=%async_computation | async-start | bytes 1310720 | tf_op jit(solution)/shard_map/all_to_all | solution.py:417
  19.5 90.5 %all-gather.5.cloned.1.call-start = ((), (), s32[]{:S(2)}) async-start(), calls=%async_computation.7 | async-start | bytes 4423680 | tf_op jit(solution)/shard_map/all_gather | solution.py:424
  19.5 12.0 %copy-start.10 = (bf16[384,384]{1,0:T(8,128)(2,1)S(1)}, bf16[384,384]{1,0:T(8,128)(2,1)}, u32[]{:S(2)}) copy-start(bf16[384,384]{1,0:T(8,128)(2,1)} %constant.23.clone.matrix) | copy-start | bytes 884740
  56.3 122.0 %reduce-scatter.3.cloned.1.call-start = ((), (), s32[]{:S(2)}) async-start(), calls=%async_computation.8 | async-start | bytes 4423680 | tf_op jit(solution)/shard_map/reduce_scatter | solution.py:448
  61.4 33.5 %copy-start.2 = (bf16[384,384]{1,0:T(8,128)(2,1)S(1)}, bf16[384,384]{1,0:T(8,128)(2,1)}, u32[]{:S(2)}) copy-start(bf16[384,384]{1,0:T(8,128)(2,1)} %constant.22.clone.swap) | copy-start | bytes 884740
  94.9 2.0 copy-start.20
  96.9 5.3 %copy-start = (bf16[272,1024]{1,0:T(8,128)(2,1)S(1)}, bf16[272,1024]{1,0:T(8,128)(2,1)}, u32[]{:S(2)}) copy-start(bf16[272,1024]{1,0:T(8,128)(2,1)} %shard_map.158.own) | copy-start | bytes 1671172
  102.2 19.2 %collective-permute-start = (bf16[272,1024]{1,0:T(8,128)(2,1)S(1)}, bf16[272,1024]{1,0:T(8,128)(2,1)S(1)}, u32[]{:S(2)}, u32[]{:S(2)}) collective-permute-start(bf16[272,1024]{1,0:T(8,128)(2,1)S(1)} %copy-done), channel_id=1, source_target_pairs={{0,1},{1,2},{2,3},{4,5},{5,6},{6,7},{8,9},{9,10},{10,11},{12,13},{... | collective-permute-start | bytes 1671176 | tf_op jit(solution)/shard_map/ppermute | solution.py:412
  105.7 16.4 %collective-permute-start.1 = (bf16[272,1024]{1,0:T(8,128)(2,1)S(1)}, bf16[272,1024]{1,0:T(8,128)(2,1)S(1)}, u32[]{:S(2)}, u32[]{:S(2)}) collective-permute-start(bf16[272,1024]{1,0:T(8,128)(2,1)S(1)} %copy-done), channel_id=1, source_target_pairs={{3,2},{2,1},{1,0},{7,6},{6,5},{5,4},{11,10},{10,9},{9,8},{15,14},{... | collective-permute-start | bytes 1671176 | tf_op jit(solution)/shard_map/ppermute | solution.py:413
  122.1 0.8 copy-start.14
  122.2 10.8 %collective-permute-start.2 = (bf16[128,1024]{1,0:T(8,128)(2,1)S(1)}, bf16[128,1024]{1,0:T(8,128)(2,1)S(1)}, u32[]{:S(2)}, u32[]{:S(2)}) collective-permute-start(bf16[128,1024]{1,0:T(8,128)(2,1)S(1)} %slice.28), channel_id=1, source_target_pairs={{1,2},{2,3},{5,6},{6,7},{9,10},{10,11},{13,14},{14,15},{17,18},{18... | collective-permute-start | bytes 786440 | tf_op jit(solution)/shard_map/ppermute | solution.py:412
  123.0 10.9 %collective-permute-start.3 = (bf16[128,1024]{1,0:T(8,128)(2,1)S(1)}, bf16[128,1024]{1,0:T(8,128)(2,1)S(1)}, u32[]{:S(2)}, u32[]{:S(2)}) collective-permute-start(bf16[128,1024]{1,0:T(8,128)(2,1)S(1)} %slice.29), channel_id=1, source_target_pairs={{2,1},{1,0},{6,5},{5,4},{10,9},{9,8},{14,13},{13,12},{18,17},{17,1... | collective-permute-start | bytes 786440 | tf_op jit(solution)/shard_map/ppermute | solution.py:413
  133.0 0.9 copy-start.16
  133.9 0.7 copy-start.18
  134.6 34.2 %all-to-all-start.2 = ((bf16[32,48,640]{2,1,0:T(8,128)(2,1)}), bf16[32,48,640]{2,1,0:T(8,128)(2,1)S(1)}, u32[]{:S(2)}, u32[]{:S(2)}) async-start(bf16[32,48,640]{2,1,0:T(8,128)(2,1)} %bitcast.13), calls=%async_computation.2 | async-start | bytes 3932160 | tf_op jit(solution)/shard_map/all_to_all | solution.py:458
  142.4 92.9 %reduce-scatter.5.cloned.1.call-start = ((), (), s32[]{:S(2)}) async-start(), calls=%async_computation.9 | async-start | bytes 2949120 | tf_op jit(solution)/shard_map/reduce_scatter | solution.py:472
  168.8 1.3 copy-start.13
  175.4 9.3 %copy-start.9 = (bf16[384,384]{1,0:T(8,128)(2,1)S(1)}, bf16[384,384]{1,0:T(8,128)(2,1)}, u32[]{:S(2)}) copy-start(bf16[384,384]{1,0:T(8,128)(2,1)} %constant.24.clone.matrix) | copy-start | bytes 884740
  178.3 6.4 %copy-start.8 = (bf16[384,640]{1,0:T(8,128)(2,1)S(1)}, bf16[384,640]{1,0:T(8,128)(2,1)}, u32[]{:S(2)}) copy-start(bf16[384,640]{1,0:T(8,128)(2,1)} %reduce-scatter.3.cloned.1.call-done.rows) | copy-start | bytes 1474564
  178.3 37.9 %collective-permute-start.6 = (bf16[272,1024]{1,0:T(8,128)(2,1)S(1)}, bf16[272,1024]{1,0:T(8,128)(2,1)S(1)}, u32[]{:S(2)}, u32[]{:S(2)}) collective-permute-start(bf16[272,1024]{1,0:T(8,128)(2,1)S(1)} %copy-done), channel_id=1, source_target_pairs={{0,3},{4,7},{8,11},{12,15},{16,19},{20,23},{24,27},{28,31},{32,35}... | collective-permute-start | bytes 1671176 | tf_op jit(solution)/shard_map/ppermute | solution.py:412
  183.4 32.9 %collective-permute-start.7 = (bf16[272,1024]{1,0:T(8,128)(2,1)S(1)}, bf16[272,1024]{1,0:T(8,128)(2,1)S(1)}, u32[]{:S(2)}, u32[]{:S(2)}) collective-permute-start(bf16[272,1024]{1,0:T(8,128)(2,1)S(1)} %copy-done), channel_id=1, source_target_pairs={{3,0},{7,4},{11,8},{15,12},{19,16},{23,20},{27,24},{31,28},{35,32}... | collective-permute-start | bytes 1671176 | tf_op jit(solution)/shard_map/ppermute | solution.py:413
  186.1 19.3 %all-to-all-start.3 = ((bf16[32,12,640]{2,1,0:T(8,128)(2,1)}), bf16[32,12,640]{2,1,0:T(8,128)(2,1)S(1)}, u32[]{:S(2)}, u32[]{:S(2)}) async-start(bf16[32,12,640]{2,1,0:T(8,128)(2,1)} %reshape.72), calls=%async_computation.4 | async-start | bytes 1310720 | tf_op jit(solution)/shard_map/all_to_all | solution.py:474
  193.5 12.8 %collective-permute-start.4 = (bf16[144,1024]{1,0:T(8,128)(2,1)}, bf16[144,1024]{1,0:T(8,128)(2,1)S(1)}, u32[]{:S(2)}, u32[]{:S(2)}) collective-permute-start(bf16[144,1024]{1,0:T(8,128)(2,1)} %slice.30), channel_id=1, source_target_pairs={{1,2},{2,3},{5,6},{6,7},{9,10},{10,11},{13,14},{14,15},{17,18},{18... | collective-permute-start | bytes 884744 | tf_op jit(solution)/shard_map/ppermute | solution.py:412
  194.2 22.1 %collective-permute-start.5 = (bf16[144,1024]{1,0:T(8,128)(2,1)}, bf16[144,1024]{1,0:T(8,128)(2,1)S(1)}, u32[]{:S(2)}, u32[]{:S(2)}) collective-permute-start(bf16[144,1024]{1,0:T(8,128)(2,1)} %slice.31), channel_id=1, source_target_pairs={{2,1},{1,0},{6,5},{5,4},{10,9},{9,8},{14,13},{13,12},{18,17},{17,1... | collective-permute-start | bytes 884744 | tf_op jit(solution)/shard_map/ppermute | solution.py:413
  206.3 12.9 %copy-start.17 = (bf16[128,1024]{1,0:T(8,128)(2,1)S(1)}, bf16[128,1024]{1,0:T(8,128)(2,1)}, u32[]{:S(2)}) copy-start(bf16[128,1024]{1,0:T(8,128)(2,1)} %copy-done.16) | copy-start | bytes 786436
  206.3 12.9 %copy-start.19 = (bf16[128,1024]{1,0:T(8,128)(2,1)S(1)}, bf16[128,1024]{1,0:T(8,128)(2,1)}, u32[]{:S(2)}) copy-start(bf16[128,1024]{1,0:T(8,128)(2,1)} %copy-done.18) | copy-start | bytes 786436
  216.3 4.0 %copy-start.15 = (bf16[272,1024]{1,0:T(8,128)(2,1)S(1)}, bf16[272,1024]{1,0:T(8,128)(2,1)}, u32[]{:S(2)}) copy-start(bf16[272,1024]{1,0:T(8,128)(2,1)} %copy-done.14) | copy-start | bytes 1671172
  235.2 5.1 %copy-start.1 = (bf16[272,1024]{1,0:T(8,128)(2,1)S(1)}, bf16[272,1024]{1,0:T(8,128)(2,1)}, u32[]{:S(2)}) copy-start(bf16[272,1024]{1,0:T(8,128)(2,1)} %shard_map.158.own) | copy-start | bytes 1671172
  235.2 5.1 %copy-start.3 = (bf16[272,1024]{1,0:T(8,128)(2,1)S(1)}, bf16[272,1024]{1,0:T(8,128)(2,1)}, u32[]{:S(2)}) copy-start(bf16[272,1024]{1,0:T(8,128)(2,1)} %maximum_select_fusion.s2) | copy-start | bytes 1671172
  235.3 5.1 %copy-start.4 = (bf16[272,1024]{1,0:T(8,128)(2,1)S(1)}, bf16[272,1024]{1,0:T(8,128)(2,1)}, u32[]{:S(2)}) copy-start(bf16[272,1024]{1,0:T(8,128)(2,1)} %get-tuple-element.92.s3) | copy-start | bytes 1671172
  235.3 5.1 %copy-start.5 = (bf16[272,1024]{1,0:T(8,128)(2,1)S(1)}, bf16[272,1024]{1,0:T(8,128)(2,1)}, u32[]{:S(2)}) copy-start(bf16[272,1024]{1,0:T(8,128)(2,1)} %get-tuple-element.93.s1) | copy-start | bytes 1671172
  235.3 5.1 %copy-start.6 = (f32[128,1024]{1,0:T(8,128)S(1)}, f32[128,1024]{1,0:T(8,128)}, u32[]{:S(2)}) copy-start(f32[128,1024]{1,0:T(8,128)} %get-tuple-element.88.image_acc) | copy-start | bytes 1572868
  235.3 5.1 %copy-start.12 = (f32[1,128]{1,0:T(1,128)S(1)}, f32[1,128]{1,0:T(1,128)}, u32[]{:S(2)}) copy-start(f32[1,128]{1,0:T(1,128)} %get-tuple-element.87.loss) | copy-start | bytes 1540
  238.1 6.8 %copy-start.7 = (f32[128,1024]{1,0:T(8,128)S(1)}, f32[128,1024]{1,0:T(8,128)}, u32[]{:S(2)}) copy-start(f32[128,1024]{1,0:T(8,128)} %get-tuple-element.91.text_acc) | copy-start | bytes 1572868
  238.1 4.8 %collective-permute-start.10 = (bf16[1,1152]{1,0:T(2,128)(2,1)}, bf16[1,1152]{1,0:T(2,128)(2,1)S(1)}, u32[]{:S(2)}, u32[]{:S(2)}) collective-permute-start(bf16[1,1152]{1,0:T(2,128)(2,1)} %get-tuple-element.86.own_image.i0), channel_id=1, source_target_pairs={{0,3},{1,0},{2,1},{3,2},{4,7},{5,4},{6,5},{7,6},{8,11},{9,8},{10,9... | collective-permute-start | bytes 6920 | tf_op jit(solution)/shard_map/ppermute | solution.py:405
  238.1 5.7 %collective-permute-start.8 = (bf16[1,1152]{1,0:T(2,128)(2,1)}, bf16[1,1152]{1,0:T(2,128)(2,1)S(1)}, u32[]{:S(2)}, u32[]{:S(2)}) collective-permute-start(bf16[1,1152]{1,0:T(2,128)(2,1)} %get-tuple-element.86.own_image.i0), channel_id=1, source_target_pairs={{0,1},{1,2},{2,3},{3,0},{4,5},{5,6},{6,7},{7,4},{8,9},{9,10},{10,1... | collective-permute-start | bytes 6920 | tf_op jit(solution)/shard_map/ppermute | solution.py:405
  240.1 4.7 %collective-permute-start.9 = (bf16[1,1152]{1,0:T(2,128)(2,1)}, bf16[1,1152]{1,0:T(2,128)(2,1)S(1)}, u32[]{:S(2)}, u32[]{:S(2)}) collective-permute-start(bf16[1,1152]{1,0:T(2,128)(2,1)} %get-tuple-element.86.own_image.i0), channel_id=1, source_target_pairs={{0,2},{1,3},{2,0},{3,1},{4,6},{5,7},{6,4},{7,5},{8,10},{9,11},{10,... | collective-permute-start | bytes 6920 | tf_op jit(solution)/shard_map/ppermute | solution.py:405
  240.4 0.7 copy-start.11
Sparse Core Ops, SparseCore 0:
  10.4 45.8 all-gather.2
  58.7 51.2 all-gather.4
  122.3 55.9 reduce-scatter.2
  180.7 54.4 reduce-scatter.4

commit v8 on v5

--- a/solution.py
+++ b/solution.py
@@ -98,7 +98,7 @@
     return np.eye(2 * BLOCK, dtype=np.float32)[order].astype(jnp.bfloat16)
 
 
-def route_kernel(tokens, routes, quota, packed, outgoing, position):
+def route_kernel(tokens, routes, quota, packed, position):
     half = packed.shape[1]
     ids = as_column(routes[...].astype(F32)).astype(jnp.int32)
     hit = ids == iota((TOK, EXPERTS), 1)
@@ -118,15 +118,41 @@
     id_row = as_row(ids.astype(F32))
     slot_row = as_row(jnp.where(kept, slot, 64.0))
     line = iota((16, TOK), 0)
-    packed[0:TOK, :] = tokens[:, :half]
+    packed[0:TOK, :] = tokens[...]
     packed[TOK:ROWS, :] = jnp.zeros((16, half), BF16)
     packed[TOK:ROWS, 0:TOK] = jnp.where(
         line == 0, id_row, jnp.where(line == 1, slot_row, 0.0)
     ).astype(BF16)
-    onto = jnp.where(
-        iota((EXPERTS * SLOTS, TOK), 0) == placing.astype(jnp.int32), 1.0, 0.0
-    ).astype(BF16)
-    outgoing[...] = dot(onto, tokens[:, half:]).astype(BF16)
+
+
+def dispatch_kernel(tokens, position, outgoing):
+    place = position[...].astype(jnp.int32)
+    onto = jnp.where(iota((EXPERTS * SLOTS, TOK), 0) == place, 1.0, 0.0).astype(BF16)
+    outgoing[...] = dot(onto, tokens[...]).astype(BF16)
+
+
+def dispatch(tokens, position, half):
+    return pl.pallas_call(
+        dispatch_kernel,
+        grid=(1,),
+        out_shape=struct((EXPERTS * SLOTS, half), BF16),
+        in_specs=[part((TOK, half), (0, 1)), whole((1, TOK))],
+        out_specs=whole((EXPERTS * SLOTS, half)),
+        cost_estimate=pl.CostEstimate(flops=1 << 28, bytes_accessed=1 << 20, transcendentals=0),
+        compiler_params=pltpu.CompilerParams(vmem_limit_bytes=60 << 20),
+    )(tokens, position)
+
+
+def route(tokens, routes, quota, half):
+    return pl.pallas_call(
+        route_kernel,
+        grid=(1,),
+        out_shape=(struct((ROWS, half), BF16), struct((1, TOK), F32)),
+        in_specs=[part((TOK, half), (0, 0)), whole((1, TOK)), whole((1, EXPERTS))],
+        out_specs=(whole((ROWS, half)), whole((1, TOK))),
+        cost_estimate=pl.CostEstimate(flops=1 << 24, bytes_accessed=1 << 20, transcendentals=0),
+        compiler_params=pltpu.CompilerParams(vmem_limit_bytes=60 << 20),
+    )(tokens, routes, quota)
 
 
 def choose_kernel(gathered, side, swap, chosen, target, held):
@@ -391,15 +417,10 @@
     together = jnp.asarray(half_matrix().T)
     side = lax.axis_index("zh").astype(jnp.int32).reshape(1, 1)
 
-    packed, outgoing, position = call(
-        route_kernel,
-        (
-            struct((ROWS, half), BF16),
-            struct((EXPERTS * SLOTS, half), BF16),
-            struct((1, TOK), F32),
-        ),
-        flops=1 << 28,
-    )(tokens, routes.reshape(1, TOK), expert_quota.reshape(1, EXPERTS))
+    packed, position = route(
+        tokens, routes.reshape(1, TOK), expert_quota.reshape(1, EXPERTS), half
+    )
+    outgoing = dispatch(tokens, position, half)
 
     own_pairs = pack_pairs(other_pooled, head, text_embed, labels.reshape(1, PAIRS))
     shift = lambda value, step: lax.ppermute(
@@ -444,6 +465,7 @@
         side.reshape(1), right.reshape(RING, 2, BLOCK, half), partial, first, second
     )
     hidden, term_right, r1, l1 = lax.optimization_barrier((hidden, term_right, r1, l1))
+    r2, l2 = both(r1, l1, (1, 2), 1)
     result = lax.psum_scatter(
         term_right.reshape(2 * RING * BLOCK, half), Z, scatter_dimension=0, tiled=True
     )
@@ -451,6 +473,7 @@
     leaving = call(unspread_kernel, struct((RING * BLOCK, half), BF16), flops=1 << 30, vmem=24)(
         term_left, swap
     )
+    leaving, r2, l2 = lax.optimization_barrier((leaving, r2, l2))
     back = lax.all_to_all(
         leaving.reshape(PLANE, PIECE, half), FLAT, split_axis=0, concat_axis=0, tiled=True
     ).reshape(RING * BLOCK, half)
@@ -460,16 +483,15 @@
         scratch=[pltpu.VMEM((RING * BLOCK, half), BF16)],
         flops=1 << 30,
     )(back, swap, target)
-    by_token, result, r1, l1, own_pairs = lax.optimization_barrier(
-        (by_token, result, r1, l1, own_pairs)
-    )
-    r2, l2 = both(r1, l1, (1, 2), 1)
+    by_token, result, own_pairs = lax.optimization_barrier((by_token, result, own_pairs))
     r3, l3 = both(own_pairs, own_pairs, (0,), 3)
     given = lax.psum_scatter(by_token, Z, scatter_dimension=0, tiled=True)
     result = call(turn_kernel, struct((2 * BLOCK, half), BF16), flops=1 << 28, vmem=24)(result, together)
     returned = lax.all_to_all(
         result.reshape(PLANE, 2 * SLOTS, half), FLAT, split_axis=0, concat_axis=0, tiled=True
     ).reshape(2 * BLOCK, half)
+
+    returned, r3, l3 = lax.optimization_barrier((returned, r3, l3))
 
     square = struct((PAIRS, embed), F32)
     line = struct((1, PAIRS), F32)

time: 263 us -> 255 us (0.970)
  waiting for transfers between devices: 82.7 us -> 73.9 us
    reduce_scatter x1, waiting for transfers between devices: 4.39 us -> 17 us  [shards(): given = lax.psum_scatter(by_token, Z, scatter_dimension=0, tiled=True)]
    ppermute x3, waiting for transfers between devices: 24.7 us -> 12.4 us  [both(): lax.ppermute(left_going, 'zl', [(LOOP - 1 - i, LOOP - 1 - i - hops) for i...]
    reduce_scatter x1, waiting for transfers between devices: 10.5 us -> 0.01 us  [shards(): lax.psum_scatter(term_right.reshape(2 * RING * BLOCK, half), Z, scatter_d...]
    ppermute x3, starting transfers between devices: 10.1 us -> 6.49 us  [both(): lax.ppermute(right_going, 'zl', [(i, i + hops) for i in senders])]
    all_to_all x1, waiting for transfers between devices: 7.78 us -> 11 us  [shards(): lax.all_to_all(result.reshape(PLANE, 2 * SLOTS, half), FLAT, split_axis=0...]
  transfers between devices with their start and end apart: 15 -> 15, of which waited for: 10 -> 7; matrix products, arithmetic and copies ran while one was open for 7% -> 7% of each run, Pallas kernels for 15% -> 16%
where the time goes in v8:
time: 255 us; the launch traced here: 254 us
  waiting for transfers between devices  73.9 us (29%)
  blocking collectives  67.6 us (27%)
  Pallas kernels  46.6 us (18%)
  starting transfers between devices  32.8 us (13%)
  between operations  14 us (5%)
  matrix products  11.2 us (4%)
  local copies, waits for them, and re-layouts  5.3 us (2%)
  other arithmetic  3.05 us (1%)
    all_to_all x1, blocking collectives, shards(): lax.all_to_all(leaving.reshape(PLANE, PIECE, half), FLAT, split_axis=0, c...  34.1 us
    all_to_all x1, blocking collectives, shards(): lax.all_to_all(chosen.reshape(PLANE, PIECE, half), FLAT, split_axis=0, co...  33.5 us
    all_gather x1, waiting for transfers between devices, shards(): around = lax.all_gather(packed, Z, axis=0, tiled=True)  22.1 us
    reduce_scatter x1, waiting for transfers between devices, shards(): given = lax.psum_scatter(by_token, Z, scatter_dimension=0, tiled=True)  17 us
    ppermute x3, waiting for transfers between devices, both(): lax.ppermute(left_going, 'zl', [(LOOP - 1 - i, LOOP - 1 - i - hops) for i...  12.4 us
    pallas_call x1, Pallas kernels, expert_right(): pl.pallas_call(expert_kernel, out_shape=(struct((RING * BLOCK, inner), BF...  11.4 us
    all_to_all x1, waiting for transfers between devices, shards(): lax.all_to_all(result.reshape(PLANE, 2 * SLOTS, half), FLAT, split_axis=0...  11 us
    all_to_all x1, starting transfers between devices, shards(): lax.all_to_all(result.reshape(PLANE, 2 * SLOTS, half), FLAT, split_axis=0...  9.02 us
  transfers between devices with their start and end apart: 15, of which 7 were waited for; matrix products, arithmetic and copies ran while one was open for 7% of the time, Pallas kernels for 16%

profile of v8, /device:TPU:2, one launch (start us, length us, event | category | flops | bytes accessed | tf_op | source)
XLA Modules:
  0.0 254.5 jit_solution(2406627961155312561)
XLA Ops:
  7.2 2.1 shard_map.156
  9.3 2.1 shard_map.157
  11.4 2.0 reshape.62
  13.4 7.6 %all-to-all-start = ((bf16[32,12,640]{2,1,0:T(8,128)(2,1)}), bf16[32,12,640]{2,1,0:T(8,128)(2,1)S(1)}, u32[]{:S(2)}, u32[]{:S(2)}) async-start(bf16[32,12,640]{2,1,0:T(8,128)(2,1)} %reshape.62), calls=%async_computation | async-start | bytes 1310720 | tf_op jit(solution)/shard_map/all_to_all | solution.py:438
  21.0 0.0 all-gather.5.cloned.1.call-start
  21.1 3.4 %shard_map.159.own = bf16[272,1024]{1,0:T(8,128)(2,1)} custom-call(bf16[127,1280]{1,0:T(8,128)(2,1)} %pooled.1, bf16[1280,1024]{1,0:T(8,128)(2,1)} %head.5, bf16[128,1024]{1,0:T(8,128)(2,1)} %text_embed.1, s32[1,128]{1,0:T(1,128)} %bitcast.30), custom_call_target="tpu_custom_call" | custom-call | flops 268435456 | bytes 4194304 | tf_op jit(solution)/shard_map/pallas_call | solution.py:338
  24.4 8.5 %all-to-all-done = bf16[32,12,640]{2,1,0:T(8,128)(2,1)S(1)} async-done(((bf16[32,12,640]{2,1,0:T(8,128)(2,1)}), bf16[32,12,640]{2,1,0:T(8,128)(2,1)S(1)}, u32[]{:S(2)}, u32[]{:S(2)}) %all-to-all-start) | async-done | bytes 491552 | tf_op jit(solution)/shard_map/all_to_all | solution.py:438
  32.9 0.1 reshape.63.rows
  33.0 1.2 shard_map.158
  34.2 22.1 %all-gather.3.cloned.1.call-done.gathered = bf16[2176,640]{1,0:T(8,128)(2,1)} async-done(((bf16[272,640]{1,0:T(8,128)(2,1)}), bf16[2176,640]{1,0:T(8,128)(2,1)}) %all-gather.3.cloned.1.call-update) | async-done | bytes 2785296 | tf_op jit(solution)/shard_map/all_gather | solution.py:437
  56.3 0.0 reduce-scatter.3.cloned.1.call-start
  56.4 5.0 %shard_map.160 = (bf16[1536,640]{1,0:T(8,128)(2,1)}, f32[8,256]{1,0:T(8,128)}) custom-call(bf16[2176,640]{1,0:T(8,128)(2,1)} %all-gather.3.cloned.1.call-done.gathered, s32[1,1]{1,0:T(1,128)} %bitcast.6.side, bf16[384,384]{1,0:T(8,128)(2,1)} %constant.22.clone.swap), custom_call_target="tpu_custom_call" | custom-call | flops 1073741824 | bytes 4194304 | tf_op jit(solution)/shard_map/pallas_call | solution.py:447
  61.4 33.5 %all_to_all.20 = bf16[32,48,640]{2,1,0:T(8,128)(2,1)S(1)} all-to-all(bf16[32,48,640]{2,1,0:T(8,128)(2,1)} %bitcast.27), channel_id=1, replica_groups=mesh['zh'=2,'y'=4,'x'=4,'c'=2,'zl'=4] {'y','x','c'}, dimensions={0} | all-to-all | bytes 3932160 | tf_op jit(solution)/shard_map/all_to_all | solution.py:453
  94.9 1.3 shard_map.161
  96.2 0.7 copy-done.15
  96.9 5.3 %fusion.1.partial = f32[1536,1280]{1,0:T(8,128)} fusion(bf16[1536,640]{1,0:T(8,128)(2,1)S(1)} %shard_map.161, bf16[1,1280,1280]{2,1,0:T(8,128)(2,1)S(1)} %copy-done.15), kind=kOutput, calls=%fused_computation.2 | convolution fusion | flops 2516582400 | bytes 11468800 | tf_op jit(solution)/shard_map/dot_general | solution.py:58
  102.2 3.6 %collective-permute-start = (bf16[272,1024]{1,0:T(8,128)(2,1)S(1)}, bf16[272,1024]{1,0:T(8,128)(2,1)S(1)}, u32[]{:S(2)}, u32[]{:S(2)}) collective-permute-start(bf16[272,1024]{1,0:T(8,128)(2,1)S(1)} %copy-done), channel_id=1, source_target_pairs={{0,1},{1,2},{2,3},{4,5},{5,6},{6,7},{8,9},{9,10},{10,11},{12,13},{... | collective-permute-start | bytes 1671176 | tf_op jit(solution)/shard_map/ppermute | solution.py:433
  105.7 1.3 collective-permute-start.1
  107.0 2.9 %all-gather.5.cloned.1.call-done = bf16[3072,640]{1,0:T(8,128)(2,1)} async-done(((bf16[384,640]{1,0:T(8,128)(2,1)}), bf16[3072,640]{1,0:T(8,128)(2,1)}) %all-gather.5.cloned.1.call-update) | async-done | bytes 3932176 | tf_op jit(solution)/shard_map/all_gather | solution.py:445
  110.0 11.4 %shard_map.162 = (bf16[1536,1280]{1,0:T(8,128)(2,1)}, bf16[8,2,192,640]{3,2,1,0:T(8,128)(2,1)}) custom-call(s32[1]{0:T(128)} %bitcast.1.side, bf16[8,2,192,640]{3,2,1,0:T(8,128)(2,1)} %bitcast.34, f32[1536,1280]{1,0:T(8,128)} %fusion.1.partial, bf16[1280,1280]{1,0:T(8,128)(2,1)} %bitcast.35, bf16[1280,1280]{1,0:T(8,128)(2,1)} %bitcast.36), custom_call_target="tpu_custom_call" | custom-call | flops 5033164800 | bytes 20971520 | tf_op jit(solution)/shard_map/pallas_call | solution.py:212
  121.4 0.7 collective-permute-done.1
  122.1 0.0 reduce-scatter.5.cloned.1.call-start
  122.2 0.7 collective-permute-start.2
  122.9 1.5 collective-permute-start.3
  124.4 5.9 %convolution_convert_fusion.rows = bf16[1536,640]{1,0:T(8,128)(2,1)S(1)} fusion(bf16[1536,1280]{1,0:T(8,128)(2,1)} %get-tuple-element.53, bf16[1,1280,1280]{2,1,0:T(8,128)(2,1)} %param.18), kind=kOutput, calls=%fused_computation | convolution fusion | flops 2517565440 | bytes 7536640 | tf_op jit(solution)/shard_map/dot_general | solution.py:62
  130.3 1.3 shard_map.163
  131.6 11.7 %collective-permute-done.3 = bf16[272,1024]{1,0:T(8,128)(2,1)S(1)} collective-permute-done((bf16[272,1024]{1,0:T(8,128)(2,1)S(1)}, bf16[272,1024]{1,0:T(8,128)(2,1)S(1)}, u32[]{:S(2)}, u32[]{:S(2)}) %collective-permute-start.3) | collective-permute-done | bytes 557088 | tf_op jit(solution)/shard_map/ppermute | solution.py:434
  143.2 34.1 %all_to_all.21 = bf16[32,48,640]{2,1,0:T(8,128)(2,1)} all-to-all(bf16[32,48,640]{2,1,0:T(8,128)(2,1)S(1)} %bitcast.23), channel_id=1, replica_groups=mesh['zh'=2,'y'=4,'x'=4,'c'=2,'zl'=4] {'y','x','c'}, dimensions={0} | all-to-all | bytes 3932160 | tf_op jit(solution)/shard_map/all_to_all | solution.py:477
  177.3 5.3 %shard_map.164 = bf16[2048,640]{1,0:T(8,128)(2,1)} custom-call(bf16[1536,640]{1,0:T(8,128)(2,1)} %bitcast.25, bf16[384,384]{1,0:T(8,128)(2,1)} %constant.22.clone.swap, f32[8,256]{1,0:T(8,128)} %get-tuple-element.57.target), custom_call_target="tpu_custom_call" | custom-call | flops 1073741824 | bytes 4194304 | tf_op jit(solution)/shard_map/pallas_call | solution.py:480
  182.7 2.2 collective-permute-start.4
  184.9 1.3 collective-permute-start.5
  186.2 0.4 shard_map.165
  186.6 0.9 reshape.72
  187.6 9.0 %all-to-all-start.3 = ((bf16[32,12,640]{2,1,0:T(8,128)(2,1)}), bf16[32,12,640]{2,1,0:T(8,128)(2,1)S(1)}, u32[]{:S(2)}, u32[]{:S(2)}) async-start(bf16[32,12,640]{2,1,0:T(8,128)(2,1)} %reshape.72), calls=%async_computation.4 | async-start | bytes 1310720 | tf_op jit(solution)/shard_map/all_to_all | solution.py:490
  196.6 0.9 broadcast_select_fusion.1.s2
  197.5 11.0 %all-to-all-done.3 = bf16[32,12,640]{2,1,0:T(8,128)(2,1)S(1)} async-done(((bf16[32,12,640]{2,1,0:T(8,128)(2,1)}), bf16[32,12,640]{2,1,0:T(8,128)(2,1)S(1)}, u32[]{:S(2)}, u32[]{:S(2)}) %all-to-all-start.3) | async-done | bytes 491552 | tf_op jit(solution)/shard_map/all_to_all | solution.py:490
  208.5 0.9 reshape.73.returned
  209.4 2.9 %shard_map.167 = (bf16[256,1280]{1,0:T(8,128)(2,1)}, f32[16,1024]{1,0:T(8,128)}) custom-call(bf16[256,1280]{1,0:T(8,128)(2,1)} %tokens.7, f32[1,256]{1,0:T(1,128)} %get-tuple-element.43.position, f32[1,256]{1,0:T(1,128)} %bitcast.28, bf16[384,640]{1,0:T(8,128)(2,1)} %reshape.73.returned, bf16[1280,1024]{1,0:T(8,128)(2,1)} %head.5), custom_call_target="tpu_custom_call" | custom-call | flops 268435456 | bytes 4194304 | tf_op jit(solution)/shard_map/pallas_call | solution.py:286
  212.3 2.2 broadcast_select_fusion
  214.5 4.4 %shard_map.166 = (f32[1,128]{1,0:T(1,128)}, f32[128,1024]{1,0:T(8,128)}, f32[128,1024]{1,0:T(8,128)}) custom-call(bf16[272,1024]{1,0:T(8,128)(2,1)} %shard_map.159.own, bf16[272,1024]{1,0:T(8,128)(2,1)} %get-tuple-element.83.s1, bf16[272,1024]{1,0:T(8,128)(2,1)} %broadcast_select_fusion.1.s2, bf16[272,1024]{1,0:T(8,128)(2,1)} %get-tuple-element.82.s3), custom_call_target="tpu_custom_call" | custom-call | flops 1073741824 | bytes 4194304 | tf_op jit(solution)/shard_map/pallas_call | solution.py:505
  218.9 17.0 %reduce-scatter.5.cloned.1.call-done.given = bf16[256,640]{1,0:T(8,128)(2,1)} async-done(((bf16[2048,640]{1,0:T(8,128)(2,1)}), bf16[256,640]{1,0:T(8,128)(2,1)}) %reduce-scatter.5.cloned.1.call-update) | async-done | bytes 327696 | tf_op jit(solution)/shard_map/reduce_scatter | solution.py:488
  235.9 2.7 %shard_map.168 = (bf16[256,1280]{1,0:T(8,128)(2,1)}, bf16[1,1152]{1,0:T(2,128)(2,1)}) custom-call(bf16[256,1280]{1,0:T(8,128)(2,1)} %tokens.7, f32[1,256]{1,0:T(1,128)} %bitcast.29, bf16[256,640]{1,0:T(8,128)(2,1)} %reduce-scatter.5.cloned.1.call-done.given, bf16[1280,1024]{1,0:T(8,128)(2,1)} %head.5, ...), custom_call_target="tpu_custom_call", output_to_operand_aliasing={{0}: (6, {})} | custom-call | flops 268435456 | bytes 4194304 | tf_op jit(solution)/shard_map/pallas_call | solution.py:305
  238.6 1.2 collective-permute-start.6
  239.9 2.7 %collective-permute-start.7 = (bf16[1,1152]{1,0:T(2,128)(2,1)}, bf16[1,1152]{1,0:T(2,128)(2,1)S(1)}, u32[]{:S(2)}, u32[]{:S(2)}) collective-permute-start(bf16[1,1152]{1,0:T(2,128)(2,1)} %get-tuple-element.76.own_image.i0), channel_id=1, source_target_pairs={{0,2},{1,3},{2,0},{3,1},{4,6},{5,7},{6,4},{7,5},{8,10},{9,11},{10,... | collective-permute-start | bytes 6920 | tf_op jit(solution)/shard_map/ppermute | solution.py:426
  242.5 1.6 collective-permute-start.8
  244.1 0.7 copy-done.11
  244.8 1.8 shard_map.169
  246.6 1.3 shard_map.170
  (43 shorter events, 0.2 us)
Async XLA Ops:
  7.2 49.1 %all-gather.3.cloned.1.call-start = ((), (), s32[]{:S(2)}) async-start(), calls=%async_computation.6 | async-start | bytes 3133440 | tf_op jit(solution)/shard_map/all_gather | solution.py:437
  13.4 19.5 %all-to-all-start = ((bf16[32,12,640]{2,1,0:T(8,128)(2,1)}), bf16[32,12,640]{2,1,0:T(8,128)(2,1)S(1)}, u32[]{:S(2)}, u32[]{:S(2)}) async-start(bf16[32,12,640]{2,1,0:T(8,128)(2,1)} %reshape.62), calls=%async_computation | async-start | bytes 1310720 | tf_op jit(solution)/shard_map/all_to_all | solution.py:438
  21.0 12.0 %copy-start.10 = (bf16[384,384]{1,0:T(8,128)(2,1)S(1)}, bf16[384,384]{1,0:T(8,128)(2,1)}, u32[]{:S(2)}) copy-start(bf16[384,384]{1,0:T(8,128)(2,1)} %constant.23.clone.matrix) | copy-start | bytes 884740
  21.0 89.0 %all-gather.5.cloned.1.call-start = ((), (), s32[]{:S(2)}) async-start(), calls=%async_computation.7 | async-start | bytes 4423680 | tf_op jit(solution)/shard_map/all_gather | solution.py:445
  56.3 126.3 %reduce-scatter.3.cloned.1.call-start = ((), (), s32[]{:S(2)}) async-start(), calls=%async_computation.8 | async-start | bytes 4423680 | tf_op jit(solution)/shard_map/reduce_scatter | solution.py:469
  61.4 33.5 %copy-start.2 = (bf16[384,384]{1,0:T(8,128)(2,1)S(1)}, bf16[384,384]{1,0:T(8,128)(2,1)}, u32[]{:S(2)}) copy-start(bf16[384,384]{1,0:T(8,128)(2,1)} %constant.22.clone.swap) | copy-start | bytes 884740
  94.9 2.0 copy-start.15
  96.9 5.3 %copy-start = (bf16[272,1024]{1,0:T(8,128)(2,1)S(1)}, bf16[272,1024]{1,0:T(8,128)(2,1)}, u32[]{:S(2)}) copy-start(bf16[272,1024]{1,0:T(8,128)(2,1)} %shard_map.159.own) | copy-start | bytes 1671172
  102.2 19.2 %collective-permute-start = (bf16[272,1024]{1,0:T(8,128)(2,1)S(1)}, bf16[272,1024]{1,0:T(8,128)(2,1)S(1)}, u32[]{:S(2)}, u32[]{:S(2)}) collective-permute-start(bf16[272,1024]{1,0:T(8,128)(2,1)S(1)} %copy-done), channel_id=1, source_target_pairs={{0,1},{1,2},{2,3},{4,5},{5,6},{6,7},{8,9},{9,10},{10,11},{12,13},{... | collective-permute-start | bytes 1671176 | tf_op jit(solution)/shard_map/ppermute | solution.py:433
  105.7 16.4 %collective-permute-start.1 = (bf16[272,1024]{1,0:T(8,128)(2,1)S(1)}, bf16[272,1024]{1,0:T(8,128)(2,1)S(1)}, u32[]{:S(2)}, u32[]{:S(2)}) collective-permute-start(bf16[272,1024]{1,0:T(8,128)(2,1)S(1)} %copy-done), channel_id=1, source_target_pairs={{3,2},{2,1},{1,0},{7,6},{6,5},{5,4},{11,10},{10,9},{9,8},{15,14},{... | collective-permute-start | bytes 1671176 | tf_op jit(solution)/shard_map/ppermute | solution.py:434
  122.1 8.2 %copy-start.13 = (bf16[272,1024]{1,0:T(8,128)(2,1)}, bf16[272,1024]{1,0:T(8,128)(2,1)S(1)}, u32[]{:S(2)}) copy-start(bf16[272,1024]{1,0:T(8,128)(2,1)S(1)} %collective-permute-done.1) | copy-start | bytes 1671172
  122.1 113.8 %reduce-scatter.5.cloned.1.call-start = ((), (), s32[]{:S(2)}) async-start(), calls=%async_computation.9 | async-start | bytes 2949120 | tf_op jit(solution)/shard_map/reduce_scatter | solution.py:488
  122.2 9.4 %collective-permute-start.2 = (bf16[272,1024]{1,0:T(8,128)(2,1)S(1)}, bf16[272,1024]{1,0:T(8,128)(2,1)S(1)}, u32[]{:S(2)}, u32[]{:S(2)}) collective-permute-start(bf16[272,1024]{1,0:T(8,128)(2,1)S(1)} %collective-permute-done), channel_id=1, source_target_pairs={{1,2},{2,3},{5,6},{6,7},{9,10},{10,11},{13,14},{14,15},{17,18},{18... | collective-permute-start | bytes 1671176 | tf_op jit(solution)/shard_map/ppermute | solution.py:433
  122.9 20.4 %collective-permute-start.3 = (bf16[272,1024]{1,0:T(8,128)(2,1)S(1)}, bf16[272,1024]{1,0:T(8,128)(2,1)S(1)}, u32[]{:S(2)}, u32[]{:S(2)}) collective-permute-start(bf16[272,1024]{1,0:T(8,128)(2,1)S(1)} %collective-permute-done.1), channel_id=1, source_target_pairs={{2,1},{1,0},{6,5},{5,4},{10,9},{9,8},{14,13},{13,12},{18,17},{17,1... | collective-permute-start | bytes 1671176 | tf_op jit(solution)/shard_map/ppermute | solution.py:434
  177.3 8.9 %copy-start.9 = (bf16[384,384]{1,0:T(8,128)(2,1)S(1)}, bf16[384,384]{1,0:T(8,128)(2,1)}, u32[]{:S(2)}) copy-start(bf16[384,384]{1,0:T(8,128)(2,1)} %constant.24.clone.matrix) | copy-start | bytes 884740
  182.6 3.6 %copy-start.8 = (bf16[384,640]{1,0:T(8,128)(2,1)S(1)}, bf16[384,640]{1,0:T(8,128)(2,1)}, u32[]{:S(2)}) copy-start(bf16[384,640]{1,0:T(8,128)(2,1)} %reduce-scatter.3.cloned.1.call-done.rows) | copy-start | bytes 1474564
  182.7 26.8 %collective-permute-start.4 = (bf16[272,1024]{1,0:T(8,128)(2,1)S(1)}, bf16[272,1024]{1,0:T(8,128)(2,1)}, u32[]{:S(2)}, u32[]{:S(2)}) collective-permute-start(bf16[272,1024]{1,0:T(8,128)(2,1)S(1)} %copy-done), channel_id=1, source_target_pairs={{0,3},{4,7},{8,11},{12,15},{16,19},{20,23},{24,27},{28,31},{32,35}... | collective-permute-start | bytes 1671176 | tf_op jit(solution)/shard_map/ppermute | solution.py:433
  184.9 24.5 %collective-permute-start.5 = (bf16[272,1024]{1,0:T(8,128)(2,1)S(1)}, bf16[272,1024]{1,0:T(8,128)(2,1)}, u32[]{:S(2)}, u32[]{:S(2)}) collective-permute-start(bf16[272,1024]{1,0:T(8,128)(2,1)S(1)} %copy-done), channel_id=1, source_target_pairs={{3,0},{7,4},{11,8},{15,12},{19,16},{23,20},{27,24},{31,28},{35,32}... | collective-permute-start | bytes 1671176 | tf_op jit(solution)/shard_map/ppermute | solution.py:434
  187.6 20.9 %all-to-all-start.3 = ((bf16[32,12,640]{2,1,0:T(8,128)(2,1)}), bf16[32,12,640]{2,1,0:T(8,128)(2,1)S(1)}, u32[]{:S(2)}, u32[]{:S(2)}) async-start(bf16[32,12,640]{2,1,0:T(8,128)(2,1)} %reshape.72), calls=%async_computation.4 | async-start | bytes 1310720 | tf_op jit(solution)/shard_map/all_to_all | solution.py:490
  197.5 14.8 %copy-start.14 = (bf16[272,1024]{1,0:T(8,128)(2,1)S(1)}, bf16[272,1024]{1,0:T(8,128)(2,1)}, u32[]{:S(2)}) copy-start(bf16[272,1024]{1,0:T(8,128)(2,1)} %copy-done.13) | copy-start | bytes 1671172
  218.9 25.2 %copy-start.1 = (bf16[272,1024]{1,0:T(8,128)(2,1)S(1)}, bf16[272,1024]{1,0:T(8,128)(2,1)}, u32[]{:S(2)}) copy-start(bf16[272,1024]{1,0:T(8,128)(2,1)} %shard_map.159.own) | copy-start | bytes 1671172
  218.9 25.2 %copy-start.3 = (bf16[272,1024]{1,0:T(8,128)(2,1)S(1)}, bf16[272,1024]{1,0:T(8,128)(2,1)}, u32[]{:S(2)}) copy-start(bf16[272,1024]{1,0:T(8,128)(2,1)} %broadcast_select_fusion.1.s2) | copy-start | bytes 1671172
  218.9 25.2 %copy-start.4 = (bf16[272,1024]{1,0:T(8,128)(2,1)S(1)}, bf16[272,1024]{1,0:T(8,128)(2,1)}, u32[]{:S(2)}) copy-start(bf16[272,1024]{1,0:T(8,128)(2,1)} %get-tuple-element.82.s3) | copy-start | bytes 1671172
  218.9 25.2 %copy-start.5 = (bf16[272,1024]{1,0:T(8,128)(2,1)S(1)}, bf16[272,1024]{1,0:T(8,128)(2,1)}, u32[]{:S(2)}) copy-start(bf16[272,1024]{1,0:T(8,128)(2,1)} %get-tuple-element.83.s1) | copy-start | bytes 1671172
  218.9 25.2 %copy-start.6 = (f32[128,1024]{1,0:T(8,128)S(1)}, f32[128,1024]{1,0:T(8,128)}, u32[]{:S(2)}) copy-start(f32[128,1024]{1,0:T(8,128)} %get-tuple-element.78.image_acc) | copy-start | bytes 1572868
  218.9 25.2 %copy-start.12 = (f32[1,128]{1,0:T(1,128)S(1)}, f32[1,128]{1,0:T(1,128)}, u32[]{:S(2)}) copy-start(f32[1,128]{1,0:T(1,128)} %get-tuple-element.77.loss) | copy-start | bytes 1540
  235.9 10.7 %copy-start.7 = (f32[128,1024]{1,0:T(8,128)S(1)}, f32[128,1024]{1,0:T(8,128)}, u32[]{:S(2)}) copy-start(f32[128,1024]{1,0:T(8,128)} %get-tuple-element.81.text_acc) | copy-start | bytes 1572868
  238.6 8.0 %collective-permute-start.6 = (bf16[1,1152]{1,0:T(2,128)(2,1)}, bf16[1,1152]{1,0:T(2,128)(2,1)S(1)}, u32[]{:S(2)}, u32[]{:S(2)}) collective-permute-start(bf16[1,1152]{1,0:T(2,128)(2,1)} %get-tuple-element.76.own_image.i0), channel_id=1, source_target_pairs={{0,1},{1,2},{2,3},{3,0},{4,5},{5,6},{6,7},{7,4},{8,9},{9,10},{10,1... | collective-permute-start | bytes 6920 | tf_op jit(solution)/shard_map/ppermute | solution.py:426
  239.9 6.8 %collective-permute-start.7 = (bf16[1,1152]{1,0:T(2,128)(2,1)}, bf16[1,1152]{1,0:T(2,128)(2,1)S(1)}, u32[]{:S(2)}, u32[]{:S(2)}) collective-permute-start(bf16[1,1152]{1,0:T(2,128)(2,1)} %get-tuple-element.76.own_image.i0), channel_id=1, source_target_pairs={{0,2},{1,3},{2,0},{3,1},{4,6},{5,7},{6,4},{7,5},{8,10},{9,11},{10,... | collective-permute-start | bytes 6920 | tf_op jit(solution)/shard_map/ppermute | solution.py:426
  242.5 4.1 %collective-permute-start.8 = (bf16[1,1152]{1,0:T(2,128)(2,1)}, bf16[1,1152]{1,0:T(2,128)(2,1)S(1)}, u32[]{:S(2)}, u32[]{:S(2)}) collective-permute-start(bf16[1,1152]{1,0:T(2,128)(2,1)} %get-tuple-element.76.own_image.i0), channel_id=1, source_target_pairs={{0,3},{1,0},{2,1},{3,2},{4,7},{5,4},{6,5},{7,6},{8,11},{9,8},{10,9... | collective-permute-start | bytes 6920 | tf_op jit(solution)/shard_map/ppermute | solution.py:426
  244.1 0.7 copy-start.11
Sparse Core Ops, SparseCore 0:
  10.4 45.9 all-gather.2
  58.7 51.2 all-gather.4
  122.2 56.0 reduce-scatter.2
  182.8 53.0 reduce-scatter.4

commit v9 on v8

--- a/solution.py
+++ b/solution.py
@@ -483,8 +483,8 @@
         scratch=[pltpu.VMEM((RING * BLOCK, half), BF16)],
         flops=1 << 30,
     )(back, swap, target)
-    by_token, result, own_pairs = lax.optimization_barrier((by_token, result, own_pairs))
-    r3, l3 = both(own_pairs, own_pairs, (0,), 3)
+    by_token, result, r2, l2 = lax.optimization_barrier((by_token, result, r2, l2))
+    r3, l3 = both(r2, l2, (2,), 1)
     given = lax.psum_scatter(by_token, Z, scatter_dimension=0, tiled=True)
     result = call(turn_kernel, struct((2 * BLOCK, half), BF16), flops=1 << 28, vmem=24)(result, together)
     returned = lax.all_to_all(

time: 255 us -> 254 us (level)
  starting transfers between devices: 32.8 us -> 28.3 us
  waiting for transfers between devices: 73.9 us -> 77.3 us
    all_to_all x1, starting transfers between devices: 9.02 us -> 5 us  [shards(): lax.all_to_all(result.reshape(PLANE, 2 * SLOTS, half), FLAT, split_axis=0...]
    reduce_scatter x1, waiting for transfers between devices: 17 us -> 19.7 us  [shards(): given = lax.psum_scatter(by_token, Z, scatter_dimension=0, tiled=True)]
  transfers between devices with their start and end apart: 15 -> 15, of which waited for: 7 -> 8; matrix products, arithmetic and copies ran while one was open for 7% -> 7% of each run, Pallas kernels for 16% -> 16%
where the time goes in v9:
time: 254 us; the launch traced here: 253 us
  waiting for transfers between devices  77.3 us (30%)
  blocking collectives  67.5 us (27%)
  Pallas kernels  46.6 us (18%)
  starting transfers between devices  28.3 us (11%)
  between operations  14 us (6%)
  matrix products  11.2 us (4%)
  local copies, waits for them, and re-layouts  5.29 us (2%)
  other arithmetic  3.07 us (1%)
    all_to_all x1, blocking collectives, shards(): lax.all_to_all(leaving.reshape(PLANE, PIECE, half), FLAT, split_axis=0, c...  34 us
    all_to_all x1, blocking collectives, shards(): lax.all_to_all(chosen.reshape(PLANE, PIECE, half), FLAT, split_axis=0, co...  33.5 us
    all_gather x1, waiting for transfers between devices, shards(): around = lax.all_gather(packed, Z, axis=0, tiled=True)  22.1 us
    reduce_scatter x1, waiting for transfers between devices, shards(): given = lax.psum_scatter(by_token, Z, scatter_dimension=0, tiled=True)  19.7 us
    ppermute x3, waiting for transfers between devices, both(): lax.ppermute(left_going, 'zl', [(LOOP - 1 - i, LOOP - 1 - i - hops) for i...  12.5 us
    pallas_call x1, Pallas kernels, expert_right(): pl.pallas_call(expert_kernel, out_shape=(struct((RING * BLOCK, inner), BF...  11.4 us
    all_to_all x1, waiting for transfers between devices, shards(): lax.all_to_all(result.reshape(PLANE, 2 * SLOTS, half), FLAT, split_axis=0...  11.1 us
    all_to_all x1, waiting for transfers between devices, shards(): lax.all_to_all(outgoing.reshape(PLANE, 2 * SLOTS, half), FLAT, split_axis...  8.47 us
  transfers between devices with their start and end apart: 15, of which 8 were waited for; matrix products, arithmetic and copies ran while one was open for 7% of the time, Pallas kernels for 16%

profile of v9, /device:TPU:2, one launch (start us, length us, event | category | flops | bytes accessed | tf_op | source)
XLA Modules:
  0.0 253.2 jit_solution(3266349992350137990)
XLA Ops:
  7.2 2.1 shard_map.156
  9.3 2.1 shard_map.157
  11.4 2.0 reshape.62
  13.4 7.6 %all-to-all-start = ((bf16[32,12,640]{2,1,0:T(8,128)(2,1)}), bf16[32,12,640]{2,1,0:T(8,128)(2,1)S(1)}, u32[]{:S(2)}, u32[]{:S(2)}) async-start(bf16[32,12,640]{2,1,0:T(8,128)(2,1)} %reshape.62), calls=%async_computation | async-start | bytes 1310720 | tf_op jit(solution)/shard_map/all_to_all | solution.py:438
  21.0 0.0 all-gather.5.cloned.1.call-start
  21.1 3.4 %shard_map.159.own = bf16[272,1024]{1,0:T(8,128)(2,1)} custom-call(bf16[127,1280]{1,0:T(8,128)(2,1)} %pooled.1, bf16[1280,1024]{1,0:T(8,128)(2,1)} %head.5, bf16[128,1024]{1,0:T(8,128)(2,1)} %text_embed.1, s32[1,128]{1,0:T(1,128)} %bitcast.30), custom_call_target="tpu_custom_call" | custom-call | flops 268435456 | bytes 4194304 | tf_op jit(solution)/shard_map/pallas_call | solution.py:338
  24.4 8.5 %all-to-all-done = bf16[32,12,640]{2,1,0:T(8,128)(2,1)S(1)} async-done(((bf16[32,12,640]{2,1,0:T(8,128)(2,1)}), bf16[32,12,640]{2,1,0:T(8,128)(2,1)S(1)}, u32[]{:S(2)}, u32[]{:S(2)}) %all-to-all-start) | async-done | bytes 491552 | tf_op jit(solution)/shard_map/all_to_all | solution.py:438
  32.9 0.1 reshape.63.rows
  33.0 1.2 shard_map.158
  34.2 22.1 %all-gather.3.cloned.1.call-done.gathered = bf16[2176,640]{1,0:T(8,128)(2,1)} async-done(((bf16[272,640]{1,0:T(8,128)(2,1)}), bf16[2176,640]{1,0:T(8,128)(2,1)}) %all-gather.3.cloned.1.call-update) | async-done | bytes 2785296 | tf_op jit(solution)/shard_map/all_gather | solution.py:437
  56.4 5.0 %shard_map.160 = (bf16[1536,640]{1,0:T(8,128)(2,1)}, f32[8,256]{1,0:T(8,128)}) custom-call(bf16[2176,640]{1,0:T(8,128)(2,1)} %all-gather.3.cloned.1.call-done.gathered, s32[1,1]{1,0:T(1,128)} %bitcast.4.side, bf16[384,384]{1,0:T(8,128)(2,1)} %constant.22.clone.swap), custom_call_target="tpu_custom_call" | custom-call | flops 1073741824 | bytes 4194304 | tf_op jit(solution)/shard_map/pallas_call | solution.py:447
  61.4 33.5 %all_to_all.20 = bf16[32,48,640]{2,1,0:T(8,128)(2,1)S(1)} all-to-all(bf16[32,48,640]{2,1,0:T(8,128)(2,1)} %bitcast.27), channel_id=1, replica_groups=mesh['zh'=2,'y'=4,'x'=4,'c'=2,'zl'=4] {'y','x','c'}, dimensions={0} | all-to-all | bytes 3932160 | tf_op jit(solution)/shard_map/all_to_all | solution.py:453
  94.9 1.3 shard_map.161
  96.2 0.7 copy-done.13
  96.9 5.3 %fusion.1.partial = f32[1536,1280]{1,0:T(8,128)} fusion(bf16[1536,640]{1,0:T(8,128)(2,1)S(1)} %shard_map.161, bf16[1,1280,1280]{2,1,0:T(8,128)(2,1)S(1)} %copy-done.13), kind=kOutput, calls=%fused_computation.2 | convolution fusion | flops 2516582400 | bytes 11468800 | tf_op jit(solution)/shard_map/dot_general | solution.py:58
  102.2 3.6 %collective-permute-start = (bf16[272,1024]{1,0:T(8,128)(2,1)S(1)}, bf16[272,1024]{1,0:T(8,128)(2,1)S(1)}, u32[]{:S(2)}, u32[]{:S(2)}) collective-permute-start(bf16[272,1024]{1,0:T(8,128)(2,1)S(1)} %copy-done), channel_id=1, source_target_pairs={{0,1},{1,2},{2,3},{4,5},{5,6},{6,7},{8,9},{9,10},{10,11},{12,13},{... | collective-permute-start | bytes 1671176 | tf_op jit(solution)/shard_map/ppermute | solution.py:433
  105.7 1.3 collective-permute-start.1
  107.0 2.9 %all-gather.5.cloned.1.call-done = bf16[3072,640]{1,0:T(8,128)(2,1)} async-done(((bf16[384,640]{1,0:T(8,128)(2,1)}), bf16[3072,640]{1,0:T(8,128)(2,1)}) %all-gather.5.cloned.1.call-update) | async-done | bytes 3932176 | tf_op jit(solution)/shard_map/all_gather | solution.py:445
  110.0 11.4 %shard_map.162 = (bf16[1536,1280]{1,0:T(8,128)(2,1)}, bf16[8,2,192,640]{3,2,1,0:T(8,128)(2,1)}) custom-call(s32[1]{0:T(128)} %bitcast.8.side, bf16[8,2,192,640]{3,2,1,0:T(8,128)(2,1)} %bitcast.34, f32[1536,1280]{1,0:T(8,128)} %fusion.1.partial, bf16[1280,1280]{1,0:T(8,128)(2,1)} %bitcast.35, bf16[1280,1280]{1,0:T(8,128)(2,1)} %bitcast.36), custom_call_target="tpu_custom_call" | custom-call | flops 5033164800 | bytes 20971520 | tf_op jit(solution)/shard_map/pallas_call | solution.py:212
  121.4 0.7 collective-permute-done.1
  122.1 0.0 reduce-scatter.5.cloned.1.call-start
  122.2 0.7 collective-permute-start.2
  122.9 1.5 collective-permute-start.3
  124.4 5.9 %convolution_convert_fusion.rows = bf16[1536,640]{1,0:T(8,128)(2,1)S(1)} fusion(bf16[1536,1280]{1,0:T(8,128)(2,1)} %get-tuple-element.54, bf16[1,1280,1280]{2,1,0:T(8,128)(2,1)} %param.18), kind=kOutput, calls=%fused_computation | convolution fusion | flops 2517565440 | bytes 7536640 | tf_op jit(solution)/shard_map/dot_general | solution.py:62
  130.3 1.3 shard_map.163
  131.6 11.8 %collective-permute-done.3 = bf16[272,1024]{1,0:T(8,128)(2,1)S(1)} collective-permute-done((bf16[272,1024]{1,0:T(8,128)(2,1)S(1)}, bf16[272,1024]{1,0:T(8,128)(2,1)S(1)}, u32[]{:S(2)}, u32[]{:S(2)}) %collective-permute-start.3) | collective-permute-done | bytes 557088 | tf_op jit(solution)/shard_map/ppermute | solution.py:434
  143.3 34.0 %all_to_all.21 = bf16[32,48,640]{2,1,0:T(8,128)(2,1)} all-to-all(bf16[32,48,640]{2,1,0:T(8,128)(2,1)S(1)} %bitcast.23), channel_id=1, replica_groups=mesh['zh'=2,'y'=4,'x'=4,'c'=2,'zl'=4] {'y','x','c'}, dimensions={0} | all-to-all | bytes 3932160 | tf_op jit(solution)/shard_map/all_to_all | solution.py:477
  177.3 5.3 %shard_map.164 = bf16[2048,640]{1,0:T(8,128)(2,1)} custom-call(bf16[1536,640]{1,0:T(8,128)(2,1)} %bitcast.25, bf16[384,384]{1,0:T(8,128)(2,1)} %constant.22.clone.swap, f32[8,256]{1,0:T(8,128)} %get-tuple-element.58.target), custom_call_target="tpu_custom_call" | custom-call | flops 1073741824 | bytes 4194304 | tf_op jit(solution)/shard_map/pallas_call | solution.py:480
  182.7 1.6 collective-permute-start.4
  184.3 1.3 collective-permute-start.5
  185.6 0.4 shard_map.165
  186.0 0.9 reshape.72
  187.0 5.0 %all-to-all-start.3 = ((bf16[32,12,640]{2,1,0:T(8,128)(2,1)}), bf16[32,12,640]{2,1,0:T(8,128)(2,1)S(1)}, u32[]{:S(2)}, u32[]{:S(2)}) async-start(bf16[32,12,640]{2,1,0:T(8,128)(2,1)} %reshape.72), calls=%async_computation.4 | async-start | bytes 1310720 | tf_op jit(solution)/shard_map/all_to_all | solution.py:490
  192.0 0.9 broadcast_select_fusion.1.s2
  192.9 11.1 %all-to-all-done.3 = bf16[32,12,640]{2,1,0:T(8,128)(2,1)S(1)} async-done(((bf16[32,12,640]{2,1,0:T(8,128)(2,1)}), bf16[32,12,640]{2,1,0:T(8,128)(2,1)S(1)}, u32[]{:S(2)}, u32[]{:S(2)}) %all-to-all-start.3) | async-done | bytes 491552 | tf_op jit(solution)/shard_map/all_to_all | solution.py:490
  204.0 0.9 reshape.73.returned
  204.9 2.9 %shard_map.167 = (bf16[256,1280]{1,0:T(8,128)(2,1)}, f32[16,1024]{1,0:T(8,128)}) custom-call(bf16[256,1280]{1,0:T(8,128)(2,1)} %tokens.7, f32[1,256]{1,0:T(1,128)} %get-tuple-element.44.position, f32[1,256]{1,0:T(1,128)} %bitcast.28, bf16[384,640]{1,0:T(8,128)(2,1)} %reshape.73.returned, bf16[1280,1024]{1,0:T(8,128)(2,1)} %head.5), custom_call_target="tpu_custom_call" | custom-call | flops 268435456 | bytes 4194304 | tf_op jit(solution)/shard_map/pallas_call | solution.py:286
  207.8 2.2 broadcast_select_fusion
  210.0 4.4 %shard_map.166 = (f32[1,128]{1,0:T(1,128)}, f32[128,1024]{1,0:T(8,128)}, f32[128,1024]{1,0:T(8,128)}) custom-call(bf16[272,1024]{1,0:T(8,128)(2,1)} %shard_map.159.own, bf16[272,1024]{1,0:T(8,128)(2,1)} %get-tuple-element.85.s1, bf16[272,1024]{1,0:T(8,128)(2,1)} %broadcast_select_fusion.1.s2, bf16[272,1024]{1,0:T(8,128)(2,1)} %get-tuple-element.84.s3), custom_call_target="tpu_custom_call" | custom-call | flops 1073741824 | bytes 4194304 | tf_op jit(solution)/shard_map/pallas_call | solution.py:505
  214.4 19.7 %reduce-scatter.5.cloned.1.call-done.given = bf16[256,640]{1,0:T(8,128)(2,1)} async-done(((bf16[2048,640]{1,0:T(8,128)(2,1)}), bf16[256,640]{1,0:T(8,128)(2,1)}) %reduce-scatter.5.cloned.1.call-update) | async-done | bytes 327696 | tf_op jit(solution)/shard_map/reduce_scatter | solution.py:488
  234.1 2.7 %shard_map.168 = (bf16[256,1280]{1,0:T(8,128)(2,1)}, bf16[1,1152]{1,0:T(2,128)(2,1)}) custom-call(bf16[256,1280]{1,0:T(8,128)(2,1)} %tokens.7, f32[1,256]{1,0:T(1,128)} %bitcast.29, bf16[256,640]{1,0:T(8,128)(2,1)} %reduce-scatter.5.cloned.1.call-done.given, bf16[1280,1024]{1,0:T(8,128)(2,1)} %head.5, ...), custom_call_target="tpu_custom_call", output_to_operand_aliasing={{0}: (6, {})} | custom-call | flops 268435456 | bytes 4194304 | tf_op jit(solution)/shard_map/pallas_call | solution.py:305
  236.8 2.0 collective-permute-start.6
  238.8 2.7 %collective-permute-start.7 = (bf16[1,1152]{1,0:T(2,128)(2,1)}, bf16[1,1152]{1,0:T(2,128)(2,1)S(1)}, u32[]{:S(2)}, u32[]{:S(2)}) collective-permute-start(bf16[1,1152]{1,0:T(2,128)(2,1)} %get-tuple-element.78.own_image.i0), channel_id=1, source_target_pairs={{0,2},{1,3},{2,0},{3,1},{4,6},{5,7},{6,4},{7,5},{8,10},{9,11},{10,... | collective-permute-start | bytes 6920 | tf_op jit(solution)/shard_map/ppermute | solution.py:426
  241.5 0.9 collective-permute-start.8
  242.4 0.7 copy-done.11
  243.1 1.8 shard_map.169
  244.9 0.4 collective-permute-done.8.i3
  245.3 1.3 shard_map.170
  (39 shorter events, 0.2 us)
Async XLA Ops:
  7.2 49.1 %all-gather.3.cloned.1.call-start = ((), (), s32[]{:S(2)}) async-start(), calls=%async_computation.6 | async-start | bytes 3133440 | tf_op jit(solution)/shard_map/all_gather | solution.py:437
  13.4 19.5 %all-to-all-start = ((bf16[32,12,640]{2,1,0:T(8,128)(2,1)}), bf16[32,12,640]{2,1,0:T(8,128)(2,1)S(1)}, u32[]{:S(2)}, u32[]{:S(2)}) async-start(bf16[32,12,640]{2,1,0:T(8,128)(2,1)} %reshape.62), calls=%async_computation | async-start | bytes 1310720 | tf_op jit(solution)/shard_map/all_to_all | solution.py:438
  21.0 12.0 %copy-start.10 = (bf16[384,384]{1,0:T(8,128)(2,1)S(1)}, bf16[384,384]{1,0:T(8,128)(2,1)}, u32[]{:S(2)}) copy-start(bf16[384,384]{1,0:T(8,128)(2,1)} %constant.23.clone.matrix) | copy-start | bytes 884740
  21.0 89.0 %all-gather.5.cloned.1.call-start = ((), (), s32[]{:S(2)}) async-start(), calls=%async_computation.7 | async-start | bytes 4423680 | tf_op jit(solution)/shard_map/all_gather | solution.py:445
  56.3 126.3 %reduce-scatter.3.cloned.1.call-start = ((), (), s32[]{:S(2)}) async-start(), calls=%async_computation.8 | async-start | bytes 4423680 | tf_op jit(solution)/shard_map/reduce_scatter | solution.py:469
  61.4 33.5 %copy-start.2 = (bf16[384,384]{1,0:T(8,128)(2,1)S(1)}, bf16[384,384]{1,0:T(8,128)(2,1)}, u32[]{:S(2)}) copy-start(bf16[384,384]{1,0:T(8,128)(2,1)} %constant.22.clone.swap) | copy-start | bytes 884740
  94.9 2.0 copy-start.13
  96.9 5.3 %copy-start = (bf16[272,1024]{1,0:T(8,128)(2,1)S(1)}, bf16[272,1024]{1,0:T(8,128)(2,1)}, u32[]{:S(2)}) copy-start(bf16[272,1024]{1,0:T(8,128)(2,1)} %shard_map.159.own) | copy-start | bytes 1671172
  102.2 19.2 %collective-permute-start = (bf16[272,1024]{1,0:T(8,128)(2,1)S(1)}, bf16[272,1024]{1,0:T(8,128)(2,1)S(1)}, u32[]{:S(2)}, u32[]{:S(2)}) collective-permute-start(bf16[272,1024]{1,0:T(8,128)(2,1)S(1)} %copy-done), channel_id=1, source_target_pairs={{0,1},{1,2},{2,3},{4,5},{5,6},{6,7},{8,9},{9,10},{10,11},{12,13},{... | collective-permute-start | bytes 1671176 | tf_op jit(solution)/shard_map/ppermute | solution.py:433
  105.7 16.4 %collective-permute-start.1 = (bf16[272,1024]{1,0:T(8,128)(2,1)S(1)}, bf16[272,1024]{1,0:T(8,128)(2,1)S(1)}, u32[]{:S(2)}, u32[]{:S(2)}) collective-permute-start(bf16[272,1024]{1,0:T(8,128)(2,1)S(1)} %copy-done), channel_id=1, source_target_pairs={{3,2},{2,1},{1,0},{7,6},{6,5},{5,4},{11,10},{10,9},{9,8},{15,14},{... | collective-permute-start | bytes 1671176 | tf_op jit(solution)/shard_map/ppermute | solution.py:434
  122.1 112.0 %reduce-scatter.5.cloned.1.call-start = ((), (), s32[]{:S(2)}) async-start(), calls=%async_computation.9 | async-start | bytes 2949120 | tf_op jit(solution)/shard_map/reduce_scatter | solution.py:488
  122.2 9.4 %collective-permute-start.2 = (bf16[272,1024]{1,0:T(8,128)(2,1)S(1)}, bf16[272,1024]{1,0:T(8,128)(2,1)S(1)}, u32[]{:S(2)}, u32[]{:S(2)}) collective-permute-start(bf16[272,1024]{1,0:T(8,128)(2,1)S(1)} %collective-permute-done), channel_id=1, source_target_pairs={{1,2},{2,3},{5,6},{6,7},{9,10},{10,11},{13,14},{14,15},{17,18},{18... | collective-permute-start | bytes 1671176 | tf_op jit(solution)/shard_map/ppermute | solution.py:433
  122.9 20.4 %collective-permute-start.3 = (bf16[272,1024]{1,0:T(8,128)(2,1)S(1)}, bf16[272,1024]{1,0:T(8,128)(2,1)S(1)}, u32[]{:S(2)}, u32[]{:S(2)}) collective-permute-start(bf16[272,1024]{1,0:T(8,128)(2,1)S(1)} %collective-permute-done.1), channel_id=1, source_target_pairs={{2,1},{1,0},{6,5},{5,4},{10,9},{9,8},{14,13},{13,12},{18,17},{17,1... | collective-permute-start | bytes 1671176 | tf_op jit(solution)/shard_map/ppermute | solution.py:434
  177.3 8.3 %copy-start.9 = (bf16[384,384]{1,0:T(8,128)(2,1)S(1)}, bf16[384,384]{1,0:T(8,128)(2,1)}, u32[]{:S(2)}) copy-start(bf16[384,384]{1,0:T(8,128)(2,1)} %constant.24.clone.matrix) | copy-start | bytes 884740
  182.6 2.9 %copy-start.8 = (bf16[384,640]{1,0:T(8,128)(2,1)S(1)}, bf16[384,640]{1,0:T(8,128)(2,1)}, u32[]{:S(2)}) copy-start(bf16[384,640]{1,0:T(8,128)(2,1)} %reduce-scatter.3.cloned.1.call-done.rows) | copy-start | bytes 1474564
  182.7 22.2 %collective-permute-start.4 = (bf16[272,1024]{1,0:T(8,128)(2,1)S(1)}, bf16[272,1024]{1,0:T(8,128)(2,1)}, u32[]{:S(2)}, u32[]{:S(2)}) collective-permute-start(bf16[272,1024]{1,0:T(8,128)(2,1)S(1)} %collective-permute-done.2), channel_id=1, source_target_pairs={{2,3},{6,7},{10,11},{14,15},{18,19},{22,23},{26,27},{30,31},{34,35... | collective-permute-start | bytes 1671176 | tf_op jit(solution)/shard_map/ppermute | solution.py:433
  184.3 20.6 %collective-permute-start.5 = (bf16[272,1024]{1,0:T(8,128)(2,1)S(1)}, bf16[272,1024]{1,0:T(8,128)(2,1)}, u32[]{:S(2)}, u32[]{:S(2)}) collective-permute-start(bf16[272,1024]{1,0:T(8,128)(2,1)S(1)} %collective-permute-done.3), channel_id=1, source_target_pairs={{1,0},{5,4},{9,8},{13,12},{17,16},{21,20},{25,24},{29,28},{33,32},... | collective-permute-start | bytes 1671176 | tf_op jit(solution)/shard_map/ppermute | solution.py:434
  187.0 17.0 %all-to-all-start.3 = ((bf16[32,12,640]{2,1,0:T(8,128)(2,1)}), bf16[32,12,640]{2,1,0:T(8,128)(2,1)S(1)}, u32[]{:S(2)}, u32[]{:S(2)}) async-start(bf16[32,12,640]{2,1,0:T(8,128)(2,1)} %reshape.72), calls=%async_computation.4 | async-start | bytes 1310720 | tf_op jit(solution)/shard_map/all_to_all | solution.py:490
  214.4 28.0 %copy-start.1 = (bf16[272,1024]{1,0:T(8,128)(2,1)S(1)}, bf16[272,1024]{1,0:T(8,128)(2,1)}, u32[]{:S(2)}) copy-start(bf16[272,1024]{1,0:T(8,128)(2,1)} %shard_map.159.own) | copy-start | bytes 1671172
  214.4 28.0 %copy-start.3 = (bf16[272,1024]{1,0:T(8,128)(2,1)S(1)}, bf16[272,1024]{1,0:T(8,128)(2,1)}, u32[]{:S(2)}) copy-start(bf16[272,1024]{1,0:T(8,128)(2,1)} %broadcast_select_fusion.1.s2) | copy-start | bytes 1671172
  214.4 28.0 %copy-start.4 = (bf16[272,1024]{1,0:T(8,128)(2,1)S(1)}, bf16[272,1024]{1,0:T(8,128)(2,1)}, u32[]{:S(2)}) copy-start(bf16[272,1024]{1,0:T(8,128)(2,1)} %get-tuple-element.84.s3) | copy-start | bytes 1671172
  214.4 28.0 %copy-start.5 = (bf16[272,1024]{1,0:T(8,128)(2,1)S(1)}, bf16[272,1024]{1,0:T(8,128)(2,1)}, u32[]{:S(2)}) copy-start(bf16[272,1024]{1,0:T(8,128)(2,1)} %get-tuple-element.85.s1) | copy-start | bytes 1671172
  214.4 28.0 %copy-start.6 = (f32[128,1024]{1,0:T(8,128)S(1)}, f32[128,1024]{1,0:T(8,128)}, u32[]{:S(2)}) copy-start(f32[128,1024]{1,0:T(8,128)} %get-tuple-element.80.image_acc) | copy-start | bytes 1572868
  214.4 28.0 %copy-start.12 = (f32[1,128]{1,0:T(1,128)S(1)}, f32[1,128]{1,0:T(1,128)}, u32[]{:S(2)}) copy-start(f32[1,128]{1,0:T(1,128)} %get-tuple-element.79.loss) | copy-start | bytes 1540
  234.1 11.2 %copy-start.7 = (f32[128,1024]{1,0:T(8,128)S(1)}, f32[128,1024]{1,0:T(8,128)}, u32[]{:S(2)}) copy-start(f32[128,1024]{1,0:T(8,128)} %get-tuple-element.83.text_acc) | copy-start | bytes 1572868
  236.8 8.1 %collective-permute-start.6 = (bf16[1,1152]{1,0:T(2,128)(2,1)}, bf16[1,1152]{1,0:T(2,128)(2,1)S(1)}, u32[]{:S(2)}, u32[]{:S(2)}) collective-permute-start(bf16[1,1152]{1,0:T(2,128)(2,1)} %get-tuple-element.78.own_image.i0), channel_id=1, source_target_pairs={{0,1},{1,2},{2,3},{3,0},{4,5},{5,6},{6,7},{7,4},{8,9},{9,10},{10,1... | collective-permute-start | bytes 6920 | tf_op jit(solution)/shard_map/ppermute | solution.py:426
  238.8 6.1 %collective-permute-start.7 = (bf16[1,1152]{1,0:T(2,128)(2,1)}, bf16[1,1152]{1,0:T(2,128)(2,1)S(1)}, u32[]{:S(2)}, u32[]{:S(2)}) collective-permute-start(bf16[1,1152]{1,0:T(2,128)(2,1)} %get-tuple-element.78.own_image.i0), channel_id=1, source_target_pairs={{0,2},{1,3},{2,0},{3,1},{4,6},{5,7},{6,4},{7,5},{8,10},{9,11},{10,... | collective-permute-start | bytes 6920 | tf_op jit(solution)/shard_map/ppermute | solution.py:426
  241.5 3.8 %collective-permute-start.8 = (bf16[1,1152]{1,0:T(2,128)(2,1)}, bf16[1,1152]{1,0:T(2,128)(2,1)S(1)}, u32[]{:S(2)}, u32[]{:S(2)}) collective-permute-start(bf16[1,1152]{1,0:T(2,128)(2,1)} %get-tuple-element.78.own_image.i0), channel_id=1, source_target_pairs={{0,3},{1,0},{2,1},{3,2},{4,7},{5,4},{6,5},{7,6},{8,11},{9,8},{10,9... | collective-permute-start | bytes 6920 | tf_op jit(solution)/shard_map/ppermute | solution.py:426
  242.4 0.7 copy-start.11
Sparse Core Ops, SparseCore 0:
  10.4 45.9 all-gather.2
  58.7 51.2 all-gather.4
  122.3 55.9 reduce-scatter.2
  182.8 51.2 reduce-scatter.4
